TPU v7x, 32 devices: a whole 2x2x4 slice. The times are simulated.
32 devices in a mesh: dp: 16 (over z, y, x), fsdp: 2 (over core).
Axes of the slice: x: 2, y: 2, z: 4, core: 2. Of those that a mesh axis runs over, the one named last changes fastest.
Arguments:
- cells: bfloat16 [4096, 13500], P(('dp', 'fsdp')), may hold values from -6 to 6
- coordinates: float32 [2, 4096], P(None, ('dp', 'fsdp')), may hold values from 0 to 100
- slide_ids: int32 [32, 128], P(('dp', 'fsdp')), may hold values from 0 to 7, never falling along the last dimension, each value on 1 to 32 neighbouring positions
- live_mask: int32 [32, 128], P(('dp', 'fsdp')), may hold values from 0 to 1, as said below
- components: int32 [4096], P(('dp', 'fsdp')), may hold values from 0 to 15
- noise: float32 [4096, 512], P(('dp', 'fsdp')), may hold values from -6 to 6
- ramp_weight: float32 [], replicated, may hold values from 0.3 to 1
- embed_weight: bfloat16 [1024, 13500], P(('dp', 'fsdp')), may hold values from -0.0546875 to 0.0546875
- query_key_value: bfloat16 [1024, 3072], P(('dp', 'fsdp')), may hold values from -0.1875 to 0.1875
- output_weight: bfloat16 [1024, 1024], P(('dp', 'fsdp')), may hold values from -0.5 to 0.5
- up_weight: bfloat16 [1024, 4096], P(('dp', 'fsdp')), may hold values from -0.1875 to 0.1875
- up_bias: bfloat16 [4096], P(('dp', 'fsdp')), may hold values from -3 to 3
- down_weight: bfloat16 [4096, 1024], P(('dp', 'fsdp')), may hold values from -0.09375 to 0.09375
- down_bias: bfloat16 [1024], P(('dp', 'fsdp')), may hold values from -3 to 3
- first_gain: bfloat16 [1024], P(('dp', 'fsdp')), may hold values from 0.25 to 1.75
- first_shift: bfloat16 [1024], P(('dp', 'fsdp')), may hold values from -3 to 3
- second_gain: bfloat16 [1024], P(('dp', 'fsdp')), may hold values from 0.25 to 1.75
- second_shift: bfloat16 [1024], P(('dp', 'fsdp')), may hold values from -3 to 3
- encoder_weight: bfloat16 [1024, 1024], P(('dp', 'fsdp')), may hold values from -0.09375 to 0.09375
- encoder_bias: bfloat16 [1024], P(('dp', 'fsdp')), may hold values from -3 to 3
- prior_mean: bfloat16 [16, 512], P(None, ('dp', 'fsdp')), may hold values from -3 to 3
- prior_logvar: bfloat16 [16, 512], P(None, ('dp', 'fsdp')), may hold values from -1.5 to 1.5
- decoder_weight: bfloat16 [512, 13500], P(('dp', 'fsdp')), may hold values from -0.25 to 0.25
Outputs:
- loss: float32 [], replicated
- cells_grad: bfloat16 [4096, 13500], P(('dp', 'fsdp'))
- embed_weight_grad: float32 [1024, 13500], P(('dp', 'fsdp'))
- query_key_value_grad: float32 [1024, 3072], P(('dp', 'fsdp'))
- output_weight_grad: float32 [1024, 1024], P(('dp', 'fsdp'))
- up_weight_grad: float32 [1024, 4096], P(('dp', 'fsdp'))
- up_bias_grad: float32 [4096], P(('dp', 'fsdp'))
- down_weight_grad: float32 [4096, 1024], P(('dp', 'fsdp'))
- down_bias_grad: float32 [1024], P(('dp', 'fsdp'))
- first_gain_grad: float32 [1024], P(('dp', 'fsdp'))
- first_shift_grad: float32 [1024], P(('dp', 'fsdp'))
- second_gain_grad: float32 [1024], P(('dp', 'fsdp'))
- second_shift_grad: float32 [1024], P(('dp', 'fsdp'))
- encoder_weight_grad: float32 [1024, 1024], P(('dp', 'fsdp'))
- encoder_bias_grad: float32 [1024], P(('dp', 'fsdp'))
- prior_mean_grad: float32 [16, 512], P(None, ('dp', 'fsdp'))
- prior_logvar_grad: float32 [16, 512], P(None, ('dp', 'fsdp'))
- decoder_weight_grad: float32 [512, 13500], P(('dp', 'fsdp'))
Inputs may be any that keep to these rules, and one draw needn't show every extreme that they name: `live_mask`: in each row the live cells come first; the last row is all live.
All inputs are finite; a program needn't handle non-finite values.
Results may differ from a plain program's by a relative error of at most 0.025.
Values may be sent and summed in bfloat16 or wider, within the bound.
A program may use at most 384 MiB of HBM per device.

v0:
```python
import math

import jax
import jax.numpy as jnp
from jax import lax
from jax.sharding import PartitionSpec as P

D = 1024
HEAD_DIM = 64
GENES = 13500
LATENT = 512


NEG_SCORE = -1000000000.0
NORM_EPS = 1e-05
FREE_FLOOR = 1.0
FREE_TEMP = 0.25


def layer_norm(hidden, gain, shift):
    center = hidden - jnp.mean(hidden, axis=-1, keepdims=True)
    spread = jnp.mean(center * center, axis=-1, keepdims=True)
    return center * lax.rsqrt(spread + NORM_EPS) * gain + shift


def positions(coordinates):
    quarter = D // 4
    frequency = jnp.exp(jnp.arange(quarter, dtype=jnp.float32) * (-math.log(10000.0) / quarter))
    angle_x = coordinates[0][:, None] * frequency[None, :]
    angle_y = coordinates[1][:, None] * frequency[None, :]
    return jnp.concatenate(
        [jnp.sin(angle_x), jnp.cos(angle_x), jnp.sin(angle_y), jnp.cos(angle_y)], axis=1
    )


def matmul(left, right):
    return jnp.dot(left, right, preferred_element_type=jnp.float32)


def across(left, right):
    return lax.dot_general(
        left, right, (((1,), (1,)), ((), ())), preferred_element_type=jnp.float32
    )


def contract_rows(left, right):
    return lax.dot_general(
        left, right, (((0,), (0,)), ((), ())), preferred_element_type=jnp.float32
    )


def split_heads(joint):
    row_count = joint.shape[0]
    queries = joint[:, :D].reshape(row_count, -1, HEAD_DIM)
    keys = joint[:, D : 2 * D].reshape(row_count, -1, HEAD_DIM)
    values = joint[:, 2 * D :].reshape(row_count, -1, HEAD_DIM)
    return (queries, keys, values)


def masked_scores(queries, keys, allowed):
    scores = jnp.einsum(
        "qhd,khd->hqk", queries, keys, preferred_element_type=jnp.float32
    ) * HEAD_DIM ** (-0.5)
    return jnp.where(allowed[None], scores, NEG_SCORE)


def attention_forward(joint, allowed):
    queries, keys, values = split_heads(joint)
    masked = masked_scores(queries, keys, allowed)
    peak = jnp.max(masked, axis=-1, keepdims=True)
    raised = jnp.exp(masked - peak)
    denom = jnp.sum(raised, axis=-1, keepdims=True)
    probs = raised / denom
    logsum = peak + jnp.log(denom)
    context = jnp.einsum(
        "hqk,khd->qhd", probs.astype(jnp.bfloat16), values, preferred_element_type=jnp.float32
    )
    return (context.reshape(joint.shape[0], D).astype(jnp.bfloat16), logsum)


def attention_backward(joint, allowed, logsum, context_grad):
    row_count = joint.shape[0]
    queries, keys, values = split_heads(joint)
    probs = jnp.exp(masked_scores(queries, keys, allowed) - logsum)
    probs_low = probs.astype(jnp.bfloat16)
    incoming = context_grad.reshape(row_count, -1, HEAD_DIM)
    value_grad = jnp.einsum("hqk,qhd->khd", probs_low, incoming, preferred_element_type=jnp.float32)
    prob_grad = jnp.einsum("qhd,khd->hqk", incoming, values, preferred_element_type=jnp.float32)
    score_grad = (probs * (prob_grad - jnp.sum(probs * prob_grad, axis=-1, keepdims=True))).astype(
        jnp.bfloat16
    )
    query_grad = jnp.einsum(
        "hqk,khd->qhd", score_grad, keys, preferred_element_type=jnp.float32
    ) * HEAD_DIM ** (-0.5)
    key_grad = jnp.einsum(
        "hqk,qhd->khd", score_grad, queries, preferred_element_type=jnp.float32
    ) * HEAD_DIM ** (-0.5)
    return jnp.concatenate(
        [
            query_grad.reshape(row_count, D),
            key_grad.reshape(row_count, D),
            value_grad.reshape(row_count, D),
        ],
        axis=1,
    ).astype(jnp.bfloat16)


def shards(
    cells,
    coordinates,
    slide_ids,
    live_mask,
    components,
    noise,
    ramp_weight,
    embed_weight,
    query_key_value,
    output_weight,
    up_weight,
    up_bias,
    down_weight,
    down_bias,
    first_gain,
    first_shift,
    second_gain,
    second_shift,
    encoder_weight,
    encoder_bias,
    prior_mean,
    prior_logvar,
    decoder_weight,
):
    row_count = cells.shape[0]
    cell_total = row_count * lax.axis_size("dp") * lax.axis_size("fsdp")
    live = live_mask[0].astype(jnp.float32)
    slides = slide_ids[0]
    places = jnp.arange(row_count)
    allowed = (slides[:, None] == slides[None, :]) & (
        (live[None, :] > 0.5) | (places[:, None] == places[None, :])
    )
    onehot = (
        components[:, None] == jnp.arange(prior_mean.shape[0], dtype=jnp.int32)[None, :]
    ).astype(jnp.float32)
    middle = (
        lax.all_gather(query_key_value, ("dp", "fsdp"), axis=0, tiled=True),
        lax.all_gather(output_weight, ("dp", "fsdp"), axis=0, tiled=True),
        lax.all_gather(up_weight, ("dp", "fsdp"), axis=0, tiled=True),
        lax.all_gather(up_bias, ("dp", "fsdp"), axis=0, tiled=True),
        lax.all_gather(down_weight, ("dp", "fsdp"), axis=0, tiled=True),
        lax.all_gather(down_bias, ("dp", "fsdp"), axis=0, tiled=True),
        lax.all_gather(first_gain, ("dp", "fsdp"), axis=0, tiled=True),
        lax.all_gather(first_shift, ("dp", "fsdp"), axis=0, tiled=True),
        lax.all_gather(second_gain, ("dp", "fsdp"), axis=0, tiled=True),
        lax.all_gather(second_shift, ("dp", "fsdp"), axis=0, tiled=True),
        lax.all_gather(encoder_weight, ("dp", "fsdp"), axis=0, tiled=True),
        lax.all_gather(encoder_bias, ("dp", "fsdp"), axis=0, tiled=True),
        lax.all_gather(prior_mean, ("dp", "fsdp"), axis=1, tiled=True),
        lax.all_gather(prior_logvar, ("dp", "fsdp"), axis=1, tiled=True),
    )
    (
        joint_full,
        output_full,
        up_full,
        up_bias_full,
        down_full,
        down_bias_full,
        gain_first,
        shift_first,
        gain_second,
        shift_second,
        encoder_full,
        encoder_bias_full,
        prior_mean_full,
        prior_logvar_full,
    ) = middle
    gain_first = gain_first.astype(jnp.float32)
    shift_first = shift_first.astype(jnp.float32)
    gain_second = gain_second.astype(jnp.float32)
    shift_second = shift_second.astype(jnp.float32)
    cells_pair, embed_half, decoder_half = (
        lax.all_to_all(cells, "fsdp", split_axis=1, concat_axis=0, tiled=True),
        lax.all_to_all(embed_weight, "fsdp", split_axis=1, concat_axis=0, tiled=True),
        lax.all_to_all(decoder_weight, "fsdp", split_axis=1, concat_axis=0, tiled=True),
    )
    embed_cols, decoder_cols = (
        lax.all_gather(embed_half, "dp", axis=0, tiled=True),
        lax.all_gather(decoder_half, "dp", axis=0, tiled=True),
    )
    embedded = lax.psum_scatter(
        across(cells_pair, embed_cols), "fsdp", scatter_dimension=0, tiled=True
    )
    start_state = embedded + positions(coordinates)
    normed_first = layer_norm(start_state, gain_first, shift_first).astype(jnp.bfloat16)
    joint = matmul(normed_first, joint_full).astype(jnp.bfloat16)
    context, logsum = attention_forward(joint, allowed)
    middle_state = start_state + matmul(context, output_full)
    normed_second = layer_norm(middle_state, gain_second, shift_second).astype(jnp.bfloat16)
    pre = matmul(normed_second, up_full) + up_bias_full.astype(jnp.float32)
    active = jax.nn.gelu(pre, approximate=True).astype(jnp.bfloat16)
    end_state = middle_state + (matmul(active, down_full) + down_bias_full.astype(jnp.float32))
    end_low = end_state.astype(jnp.bfloat16)
    encoded = matmul(end_low, encoder_full) + encoder_bias_full.astype(jnp.float32)
    latent_mean = encoded[:, :LATENT]
    latent_logvar = encoded[:, LATENT:]
    latent = (latent_mean + jnp.exp(0.5 * latent_logvar) * noise).astype(jnp.bfloat16)
    latent_pair, live_rows = (
        lax.all_gather(latent, "fsdp", axis=0, tiled=True),
        lax.all_gather(live_mask, "fsdp", axis=0, tiled=True),
    )
    live_used = live_rows.reshape(-1).astype(jnp.float32)
    recon = matmul(latent_pair, decoder_cols)
    miss = recon - cells_pair.astype(jnp.float32)
    recon_local = jnp.sum(live_used * (0.5 * jnp.sum(miss * miss, axis=1)))
    center = jnp.dot(onehot, prior_mean_full.astype(jnp.float32), precision=lax.Precision.HIGHEST)
    scale = jnp.dot(onehot, prior_logvar_full.astype(jnp.float32), precision=lax.Precision.HIGHEST)
    gap = latent_mean - center
    inverse = jnp.exp(-scale)
    grown = jnp.exp(latent_logvar)
    diverge = 0.5 * (scale - latent_logvar + (grown + gap * gap) * inverse - 1.0)
    diverge_sum, recon_total, count = lax.psum(
        (jnp.sum(live[:, None] * diverge, axis=0), recon_local, jnp.sum(live)), ("dp", "fsdp")
    )
    kl_mean = diverge_sum / count
    shifted = (kl_mean - FREE_FLOOR) / FREE_TEMP
    free = FREE_FLOOR + FREE_TEMP * jax.nn.softplus(shifted)
    loss = (recon_total / count + ramp_weight * jnp.sum(free)) / GENES
    ratio = cell_total / count
    target_grad = ratio * live_used[:, None] * miss
    recon_grad = target_grad.astype(jnp.bfloat16)
    latent_grad = lax.psum_scatter(
        across(recon_grad, decoder_cols).astype(jnp.bfloat16),
        "fsdp",
        scatter_dimension=0,
        tiled=True,
    ).astype(jnp.float32)
    kl_scale = ratio * ramp_weight * jax.nn.sigmoid(shifted)[None, :] * live[:, None]
    pulled = kl_scale * gap * inverse
    mean_grad = latent_grad + pulled
    logvar_grad = latent_grad * 0.5 * jnp.exp(0.5 * latent_logvar) * noise + kl_scale * 0.5 * (
        grown * inverse - 1.0
    )
    encoded_grad = jnp.concatenate([mean_grad, logvar_grad], axis=1).astype(jnp.bfloat16)
    prior_mean_grad = jnp.dot(onehot.T, -pulled, precision=lax.Precision.HIGHEST)
    prior_logvar_grad = jnp.dot(
        onehot.T,
        kl_scale * 0.5 * (1.0 - (grown + gap * gap) * inverse),
        precision=lax.Precision.HIGHEST,
    )
    encoder_weight_grad = contract_rows(end_low, encoded_grad)
    encoder_bias_grad = jnp.sum(encoded_grad.astype(jnp.float32), axis=0)
    end_grad = across(encoded_grad, encoder_full)
    branch_grad = end_grad.astype(jnp.bfloat16)
    down_weight_grad = contract_rows(active, branch_grad)
    down_bias_grad = jnp.sum(branch_grad.astype(jnp.float32), axis=0)
    active_grad = across(branch_grad, down_full)
    gelu_value, gelu_back = jax.vjp(lambda value: jax.nn.gelu(value, approximate=True), pre)
    pre_grad = gelu_back(active_grad)[0].astype(jnp.bfloat16)
    up_weight_grad = contract_rows(normed_second, pre_grad)
    up_bias_grad = jnp.sum(pre_grad.astype(jnp.float32), axis=0)
    second_out_grad = across(pre_grad, up_full)
    norm_value, second_back = jax.vjp(layer_norm, middle_state, gain_second, shift_second)
    state_part, second_gain_grad, second_shift_grad = second_back(second_out_grad)
    middle_grad = end_grad + state_part
    attend_grad = middle_grad.astype(jnp.bfloat16)
    output_weight_grad = contract_rows(context, attend_grad)
    context_grad = across(attend_grad, output_full).astype(jnp.bfloat16)
    joint_grad = attention_backward(joint, allowed, logsum, context_grad)
    joint_weight_grad = contract_rows(normed_first, joint_grad)
    first_out_grad = across(joint_grad, joint_full)
    first_value, first_back = jax.vjp(layer_norm, start_state, gain_first, shift_first)
    start_part, first_gain_grad, first_shift_grad = first_back(first_out_grad)
    start_grad = middle_grad + start_part
    start_low = start_grad.astype(jnp.bfloat16)
    shared = (
        lax.psum_scatter(joint_weight_grad, ("dp", "fsdp"), scatter_dimension=0, tiled=True),
        lax.psum_scatter(output_weight_grad, ("dp", "fsdp"), scatter_dimension=0, tiled=True),
        lax.psum_scatter(up_weight_grad, ("dp", "fsdp"), scatter_dimension=0, tiled=True),
        lax.psum_scatter(up_bias_grad, ("dp", "fsdp"), scatter_dimension=0, tiled=True),
        lax.psum_scatter(down_weight_grad, ("dp", "fsdp"), scatter_dimension=0, tiled=True),
        lax.psum_scatter(down_bias_grad, ("dp", "fsdp"), scatter_dimension=0, tiled=True),
        lax.psum_scatter(first_gain_grad, ("dp", "fsdp"), scatter_dimension=0, tiled=True),
        lax.psum_scatter(first_shift_grad, ("dp", "fsdp"), scatter_dimension=0, tiled=True),
        lax.psum_scatter(second_gain_grad, ("dp", "fsdp"), scatter_dimension=0, tiled=True),
        lax.psum_scatter(second_shift_grad, ("dp", "fsdp"), scatter_dimension=0, tiled=True),
        lax.psum_scatter(encoder_weight_grad, ("dp", "fsdp"), scatter_dimension=0, tiled=True),
        lax.psum_scatter(encoder_bias_grad, ("dp", "fsdp"), scatter_dimension=0, tiled=True),
        lax.psum_scatter(prior_mean_grad, ("dp", "fsdp"), scatter_dimension=1, tiled=True),
        lax.psum_scatter(prior_logvar_grad, ("dp", "fsdp"), scatter_dimension=1, tiled=True),
    )
    start_pair = lax.all_gather(start_low, "fsdp", axis=0, tiled=True)
    embed_term = contract_rows(start_pair, cells_pair)
    decoder_term_half = contract_rows(latent_pair, recon_grad)
    embed_block, decoder_block = (
        lax.psum_scatter(embed_term, "dp", scatter_dimension=0, tiled=True),
        lax.psum_scatter(decoder_term_half, "dp", scatter_dimension=0, tiled=True),
    )
    cells_half = matmul(start_pair, embed_cols) - target_grad
    embed_grad, decoder_grad, cells_back = (
        lax.all_to_all(
            embed_block.astype(jnp.bfloat16), "fsdp", split_axis=0, concat_axis=1, tiled=True
        ).astype(embed_block.dtype),
        lax.all_to_all(
            decoder_block.astype(jnp.bfloat16), "fsdp", split_axis=0, concat_axis=1, tiled=True
        ).astype(decoder_block.dtype),
        lax.all_to_all(
            cells_half.astype(jnp.bfloat16), "fsdp", split_axis=0, concat_axis=1, tiled=True
        ).astype(cells_half.dtype),
    )
    cells_grad = cells_back.astype(jnp.bfloat16)
    return (
        loss,
        cells_grad,
        embed_grad,
        shared[0],
        shared[1],
        shared[2],
        shared[3],
        shared[4],
        shared[5],
        shared[6],
        shared[7],
        shared[8],
        shared[9],
        shared[10],
        shared[11],
        shared[12],
        shared[13],
        decoder_grad,
    )


def solution(mesh):
    in_specs = (
        P(("dp", "fsdp"), None),
        P(None, ("dp", "fsdp")),
        P(("dp", "fsdp"), None),
        P(("dp", "fsdp"), None),
        P(("dp", "fsdp")),
        P(("dp", "fsdp"), None),
        P(),
        P(("dp", "fsdp"), None),
        P(("dp", "fsdp"), None),
        P(("dp", "fsdp"), None),
        P(("dp", "fsdp"), None),
        P(("dp", "fsdp")),
        P(("dp", "fsdp"), None),
        P(("dp", "fsdp")),
        P(("dp", "fsdp")),
        P(("dp", "fsdp")),
        P(("dp", "fsdp")),
        P(("dp", "fsdp")),
        P(("dp", "fsdp"), None),
        P(("dp", "fsdp")),
        P(None, ("dp", "fsdp")),
        P(None, ("dp", "fsdp")),
        P(("dp", "fsdp"), None),
    )
    out_specs = (
        P(),
        P(("dp", "fsdp"), None),
        P(("dp", "fsdp"), None),
        P(("dp", "fsdp"), None),
        P(("dp", "fsdp"), None),
        P(("dp", "fsdp"), None),
        P(("dp", "fsdp")),
        P(("dp", "fsdp"), None),
        P(("dp", "fsdp")),
        P(("dp", "fsdp")),
        P(("dp", "fsdp")),
        P(("dp", "fsdp")),
        P(("dp", "fsdp")),
        P(("dp", "fsdp"), None),
        P(("dp", "fsdp")),
        P(None, ("dp", "fsdp")),
        P(None, ("dp", "fsdp")),
        P(("dp", "fsdp"), None),
    )
    return jax.shard_map(shards, mesh=mesh, in_specs=in_specs, out_specs=out_specs, check_vma=False)
```

profile of v0, /device:TPU:0, one launch (start us, length us, event | category | flops | bytes accessed | tf_op | source)
XLA Modules:
  0.0 2622.9 jit_solution(14391396643759751765)
XLA Ops:
  18.8 6.5 all_to_all.103
  25.3 26.2 copy.109
  54.7 128.6 %all-gather.10.cloned.1.call-done = bf16[1024,6750]{1,0:T(8,128)(2,1)} async-done(((bf16[64,6750]{1,0:T(8,128)(2,1)}), bf16[1024,6750]{1,0:T(8,128)(2,1)}) %all-gather.10.cloned.1.call-update) | async-done | bytes 13824016 | tf_op jit(solution)/shard_map/all_gather | solution.py:186
  183.3 8.2 fusion.75
  204.2 39.1 %all-reduce.15 = (bf16[1024]{0:T(1024)(128)(2,1)S(1)}, bf16[1024]{0:T(1024)(128)(2,1)S(1)}, bf16[1024]{0:T(1024)(128)(2,1)S(1)}, bf16[1024]{0:T(1024)(128)(2,1)S...) all-reduce(bf16[1024]{0:T(1024)(128)(2,1)S(1)} %dynamic-update-slic, ...), channel_id=1, replica_groups=mesh['dp'=16,'fsdp'=2] {'dp','fsdp'}, use_global_device_ids=true, to_apply=%add.1 | all-reduce | flops 6144 | bytes 24576
  243.3 41.1 %all-gather.1 = bf16[32,1,128]{2,1,0:T(2,128)(2,1)S(1)} all-gather(bf16[1,1,128]{2,1,0:T(2,128)(2,1)S(1)} %bitcast.142), channel_id=1, replica_groups=mesh['dp'=16,'fsdp'=2] {'dp','fsdp'}, dimensions={0}, use_global_device_ids=true | all-gather | bytes 8448 | tf_op jit(solution)/shard_map/all_gather | solution.py:148
  284.7 37.3 %all_gather.74 = bf16[16,512]{0,1:T(8,128)(2,1)S(1)} all-gather(bf16[16,16]{0,1:T(8,128)(2,1)S(1)} %copy.91), channel_id=1, replica_groups=mesh['dp'=16,'fsdp'=2] {'dp','fsdp'}, dimensions={1}, use_global_device_ids=true | all-gather | bytes 16896 | tf_op jit(solution)/shard_map/all_gather | solution.py:157
  321.9 41.4 %all_gather.73 = bf16[16,512]{0,1:T(8,128)(2,1)} all-gather(bf16[16,16]{0,1:T(8,128)(2,1)S(1)} %copy.90), channel_id=1, replica_groups=mesh['dp'=16,'fsdp'=2] {'dp','fsdp'}, dimensions={1}, use_global_device_ids=true | all-gather | bytes 16896 | tf_op jit(solution)/shard_map/all_gather | solution.py:158
  375.2 26.4 %all-gather.16.cloned.1.call-done = bf16[1024,4096]{1,0:T(8,128)(2,1)} async-done(((bf16[32,4096]{1,0:T(8,128)(2,1)}), bf16[1024,4096]{1,0:T(8,128)(2,1)}) %all-gather.16.cloned.1.call-update) | async-done | bytes 8388624 | tf_op jit(solution)/shard_map/all_gather | solution.py:147
  407.7 73.0 %all-gather.18.cloned.1.call-done = bf16[4096,1024]{1,0:T(8,128)(2,1)} async-done(((bf16[128,1024]{1,0:T(8,128)(2,1)}), bf16[4096,1024]{1,0:T(8,128)(2,1)}) %all-gather.18.cloned.1.call-update) | async-done | bytes 8388624 | tf_op jit(solution)/shard_map/all_gather | solution.py:149
  486.3 52.8 %all-gather.20.cloned.1.call-done = bf16[1024,1024]{1,0:T(8,128)(2,1)} async-done(((bf16[32,1024]{1,0:T(8,128)(2,1)}), bf16[1024,1024]{1,0:T(8,128)(2,1)}) %all-gather.20.cloned.1.call-update) | async-done | bytes 2097168 | tf_op jit(solution)/shard_map/all_gather | solution.py:155
  542.4 39.2 %all-reduce.14 = (f32[]{:T(128)}, f32[512]{0:T(512)}) all-reduce(f32[]{:T(128)} %convert_reduce_fusion.3, f32[512]{0:T(512)} %get-tuple-element.51), channel_id=1, replica_groups=mesh['dp'=16,'fsdp'=2] {'dp','fsdp'}, use_global_device_ids=true, to_apply=%region_11.12 | all-reduce | flops 513 | bytes 4104 | tf_op jit(solution)/shard_map/psum | solution.py:220
  584.9 56.7 %all-gather.22.cloned.1.call-done = bf16[512,6750]{1,0:T(8,128)(2,1)} async-done(((bf16[32,6750]{1,0:T(8,128)(2,1)}), bf16[512,6750]{1,0:T(8,128)(2,1)}) %all-gather.22.cloned.1.call-update) | async-done | bytes 6912016 | tf_op jit(solution)/shard_map/all_gather | solution.py:187
  641.6 7.5 multiply_reduce_fusion
  659.3 10.1 fusion.9
  675.4 7.8 convert_reduce_fusion
  703.7 11.3 fusion.76
  723.4 6.5 fusion.22
  731.2 8.2 fusion.68
  741.0 8.2 fusion.59
  749.9 47.7 %reduce-scatter.34.cloned.1.call-done = f32[16,16]{1,0:T(8,128)} async-done(((f32[512,16]{1,0:T(8,128)}), f32[16,16]{1,0:T(8,128)}) %reduce-scatter.34.cloned.1.call-update) | async-done | bytes 1040
  798.9 130.2 %reduce-scatter.36.cloned.1.call-done = f32[16,16]{1,0:T(8,128)} async-done(((f32[512,16]{1,0:T(8,128)}), f32[16,16]{1,0:T(8,128)}) %reduce-scatter.36.cloned.1.call-update) | async-done | bytes 1040
  930.6 56.5 %all-reduce.13 = (f32[]{:T(128)}, f32[4096]{0:T(1024)S(1)}, f32[1024]{0:T(1024)S(1)}, f32[1024]{0:T(1024)S(1)}, f32[1024]{0:T(1024)S(1)}, /*index=5*/f32[1024]{0:T(1024)S(1)}, f32[1024]{0:T(1024)S(1)}, f32[1024]{0:T(1024)S(1)}) all-reduce(f32[]{:T(128)} %get-tuple-element.62, ...), channel_id=1, replica_groups=mesh['dp'=16,'fsdp'=2] {'dp','fsdp'}, use_global_device_ids=true, to_apply=%region_9.10 | all-reduce | flops 10241 | bytes 81928 | tf_op jit(solution)/shard_map/psum | solution.py:220
  988.5 14.4 fusion
  1009.8 6.5 all_to_all.105
  1022.8 194.1 %reduce-scatter.32.cloned.1.call-done = f32[32,6750]{1,0:T(8,128)} async-done(((f32[512,6750]{1,0:T(8,128)}), f32[32,6750]{1,0:T(8,128)}) %reduce-scatter.32.cloned.1.call-update) | async-done | bytes 864016 | tf_op jit(solution)/shard_map/reduce_scatter | solution.py:295
  1224.2 569.5 %reduce-scatter.20.cloned.1.call-done = f32[64,6750]{1,0:T(8,128)} async-done(((f32[1024,6750]{1,0:T(8,128)}), f32[64,6750]{1,0:T(8,128)}) %reduce-scatter.20.cloned.1.call-update) | async-done | bytes 1728016 | tf_op jit(solution)/shard_map/reduce_scatter | solution.py:294
  1804.0 139.4 %reduce-scatter.24.cloned.1.call-done = f32[32,1024]{1,0:T(8,128)} async-done(((f32[1024,1024]{1,0:T(8,128)}), f32[32,1024]{1,0:T(8,128)}) %reduce-scatter.24.cloned.1.call-update) | async-done | bytes 131088 | tf_op jit(solution)/shard_map/reduce_scatter | solution.py:276
  1943.4 139.7 %reduce-scatter.30.cloned.1.call-done = f32[32,1024]{1,0:T(8,128)} async-done(((f32[1024,1024]{1,0:T(8,128)}), f32[32,1024]{1,0:T(8,128)}) %reduce-scatter.30.cloned.1.call-update) | async-done | bytes 131088 | tf_op jit(solution)/shard_map/reduce_scatter | solution.py:285
  2083.1 158.8 %reduce-scatter.22.cloned.1.call-done = f32[32,3072]{1,0:T(8,128)} async-done(((f32[1024,3072]{1,0:T(8,128)}), f32[32,3072]{1,0:T(8,128)}) %reduce-scatter.22.cloned.1.call-update) | async-done | bytes 393232 | tf_op jit(solution)/shard_map/reduce_scatter | solution.py:275
  2241.9 184.7 %reduce-scatter.26.cloned.1.call-done = f32[32,4096]{1,0:T(8,128)} async-done(((f32[1024,4096]{1,0:T(8,128)}), f32[32,4096]{1,0:T(8,128)}) %reduce-scatter.26.cloned.1.call-update) | async-done | bytes 524304 | tf_op jit(solution)/shard_map/reduce_scatter | solution.py:277
  2426.6 187.2 %reduce-scatter.28.cloned.1.call-done = f32[128,1024]{1,0:T(8,128)} async-done(((f32[4096,1024]{1,0:T(8,128)}), f32[128,1024]{1,0:T(8,128)}) %reduce-scatter.28.cloned.1.call-update) | async-done | bytes 524304 | tf_op jit(solution)/shard_map/reduce_scatter | solution.py:279
  (318 shorter events, 136.2 us)
Async XLA Ops:
  8.0 175.3 %all-gather.10.cloned.1.call-start = ((), (), s32[]{:S(2)}) async-start(), calls=%async_computation.17 | async-start | bytes 14761984 | tf_op jit(solution)/shard_map/all_gather | solution.py:186
  16.1 349.5 %reduce-scatter.16.cloned.1.call-start = ((), (), s32[]{:S(2)}) async-start(), calls=%async_computation.18 | async-start | bytes 1572864 | tf_op jit(solution)/shard_map/reduce_scatter | solution.py:189
  54.7 136.8 %copy-start.1 = (bf16[844,8,2,128]{3,1,2,0:T(8,128)(2,1)}, bf16[844,8,2,128]{3,1,2,0:T(8,128)(2,1)S(1)}, u32[]{:S(2)}) copy-start(bf16[844,8,2,128]{3,1,2,0:T(8,128)(2,1)S(1)} %copy.107) | copy-start | bytes 10371076
  191.7 92.8 %copy-start.58 = (bf16[16,16]{1,0:T(8,128)(2,1)S(1)}, bf16[16,16]{1,0:T(8,128)(2,1)}, u32[]{:S(2)}) copy-start(bf16[16,16]{1,0:T(8,128)(2,1)} %param.43) | copy-start | bytes 1540
  191.7 92.9 %copy-start.59 = (bf16[16,16]{1,0:T(8,128)(2,1)S(1)}, bf16[16,16]{1,0:T(8,128)(2,1)}, u32[]{:S(2)}) copy-start(bf16[16,16]{1,0:T(8,128)(2,1)} %param.44) | copy-start | bytes 1540
  191.7 175.3 %all-gather.12.cloned.1.call-start = ((), (), s32[]{:S(2)}) async-start(), calls=%async_computation.19 | async-start | bytes 6488064 | tf_op jit(solution)/shard_map/all_gather | solution.py:145
  192.3 172.1 %copy-start.65 = (f32[2,128]{1,0:T(2,128)S(1)}, f32[2,128]{1,0:T(2,128)}, u32[]{:S(2)}) copy-start(f32[2,128]{1,0:T(2,128)} %param.24) | copy-start | bytes 3076
  192.3 172.1 %copy-start.63 = (s32[1,128]{1,0:T(1,128)S(1)}, s32[1,128]{1,0:T(1,128)}, u32[]{:S(2)}) copy-start(s32[1,128]{1,0:T(1,128)} %param.25) | copy-start | bytes 1540
  192.3 180.4 %all-gather.14.cloned.1.call-start = ((), (), s32[]{:S(2)}) async-start(), calls=%async_computation.20 | async-start | bytes 2162688 | tf_op jit(solution)/shard_map/all_gather | solution.py:146
  192.9 208.7 %all-gather.16.cloned.1.call-start = ((), (), s32[]{:S(2)}) async-start(), calls=%async_computation.21 | async-start | bytes 8650752 | tf_op jit(solution)/shard_map/all_gather | solution.py:147
  193.5 287.2 %all-gather.18.cloned.1.call-start = ((), (), s32[]{:S(2)}) async-start(), calls=%async_computation.22 | async-start | bytes 8650752 | tf_op jit(solution)/shard_map/all_gather | solution.py:149
  194.2 344.9 %all-gather.20.cloned.1.call-start = ((), (), s32[]{:S(2)}) async-start(), calls=%async_computation.23 | async-start | bytes 2162688 | tf_op jit(solution)/shard_map/all_gather | solution.py:155
  195.0 446.6 %all-gather.22.cloned.1.call-start = ((), (), s32[]{:S(2)}) async-start(), calls=%async_computation.24 | async-start | bytes 7380992 | tf_op jit(solution)/shard_map/all_gather | solution.py:187
  200.4 470.3 %reduce-scatter.18.cloned.1.call-start = ((), (), s32[]{:S(2)}) async-start(), calls=%async_computation.25 | async-start | bytes 393216 | tf_op jit(solution)/shard_map/reduce_scatter | solution.py:230
  584.9 64.2 %copy-start.60 = (f32[2,1,128]{2,1,0:T(1,128)S(1)}, f32[2,1,128]{2,1,0:T(1,128)}, u32[]{:S(2)}) copy-start(f32[2,1,128]{2,1,0:T(1,128)} %convert_element_type.194) | copy-start | bytes 3076
  654.7 142.8 %reduce-scatter.34.cloned.1.call-start = ((), (), s32[]{:S(2)}) async-start(), calls=%async_computation.33 | async-start | bytes 270336
  658.0 271.1 %reduce-scatter.36.cloned.1.call-start = ((), (), s32[]{:S(2)}) async-start(), calls=%async_computation.34 | async-start | bytes 270336
  659.2 557.7 %reduce-scatter.32.cloned.1.call-start = ((), (), s32[]{:S(2)}) async-start(), calls=%async_computation.32 | async-start | bytes 14761984 | tf_op jit(solution)/shard_map/reduce_scatter | solution.py:295
  669.4 1124.3 %reduce-scatter.20.cloned.1.call-start = ((), (), s32[]{:S(2)}) async-start(), calls=%async_computation.26 | async-start | bytes 29523968 | tf_op jit(solution)/shard_map/reduce_scatter | solution.py:294
  715.0 1228.4 %reduce-scatter.24.cloned.1.call-start = ((), (), s32[]{:S(2)}) async-start(), calls=%async_computation.28 | async-start | bytes 4325376 | tf_op jit(solution)/shard_map/reduce_scatter | solution.py:276
  718.6 1364.5 %reduce-scatter.30.cloned.1.call-start = ((), (), s32[]{:S(2)}) async-start(), calls=%async_computation.31 | async-start | bytes 4325376 | tf_op jit(solution)/shard_map/reduce_scatter | solution.py:285
  722.3 1519.5 %reduce-scatter.22.cloned.1.call-start = ((), (), s32[]{:S(2)}) async-start(), calls=%async_computation.27 | async-start | bytes 12976128 | tf_op jit(solution)/shard_map/reduce_scatter | solution.py:275
  730.0 1696.6 %reduce-scatter.26.cloned.1.call-start = ((), (), s32[]{:S(2)}) async-start(), calls=%async_computation.29 | async-start | bytes 17301504 | tf_op jit(solution)/shard_map/reduce_scatter | solution.py:277
  739.4 1874.4 %reduce-scatter.28.cloned.1.call-start = ((), (), s32[]{:S(2)}) async-start(), calls=%async_computation.30 | async-start | bytes 17301504 | tf_op jit(solution)/shard_map/reduce_scatter | solution.py:279
  749.1 181.4 %copy-start.42 = (f32[1024]{0:T(1024)S(1)}, f32[1024]{0:T(1024)}, u32[]{:S(2)}) copy-start(f32[1024]{0:T(1024)} %get-tuple-element.18) | copy-start | bytes 12292
  749.1 181.4 %copy-start.43 = (f32[1024]{0:T(1024)S(1)}, f32[1024]{0:T(1024)}, u32[]{:S(2)}) copy-start(f32[1024]{0:T(1024)} %get-tuple-element.22) | copy-start | bytes 12292
  749.1 181.4 %copy-start.44 = (f32[1024]{0:T(1024)S(1)}, f32[1024]{0:T(1024)}, u32[]{:S(2)}) copy-start(f32[1024]{0:T(1024)} %get-tuple-element.50) | copy-start | bytes 12292
  749.1 181.4 %copy-start.45 = (f32[4096]{0:T(1024)S(1)}, f32[4096]{0:T(1024)}, u32[]{:S(2)}) copy-start(f32[4096]{0:T(1024)} %get-tuple-element.74) | copy-start | bytes 49156
  749.1 181.4 %copy-start.61 = (f32[1024]{0:T(1024)S(1)}, f32[1024]{0:T(1024)}, u32[]{:S(2)}) copy-start(f32[1024]{0:T(1024)} %get-tuple-element.20) | copy-start | bytes 12292
  749.1 181.4 %copy-start.62 = (f32[1024]{0:T(1024)S(1)}, f32[1024]{0:T(1024)}, u32[]{:S(2)}) copy-start(f32[1024]{0:T(1024)} %get-tuple-element.23) | copy-start | bytes 12292
  749.2 239.3 %copy-start.10 = (bf16[256,1024]{1,0:T(8,128)(2,1)S(1)}, bf16[256,1024]{1,0:T(8,128)(2,1)}, u32[]{:S(2)}) copy-start(bf16[256,1024]{1,0:T(8,128)(2,1)} %copy-done.9) | copy-start | bytes 1572868
  749.2 239.3 %copy-start.50 = (f32[256]{0:T(256)S(1)}, f32[256]{0:T(256)}, u32[]{:S(2)}) copy-start(f32[256]{0:T(256)} %copy-done.49) | copy-start | bytes 3076
  (68 other events, 569.1 us)
Sparse Core Ops, SparseCore 0:
  16.2 167.1 all-gather.9
  191.7 6.7 reduce-scatter.15
  654.9 5.9 reduce-scatter.17
  662.9 134.5 reduce-scatter.33
  799.7 129.3 reduce-scatter.35
  931.3 285.5 reduce-scatter.31
  1219.3 574.4 reduce-scatter.19
  1796.7 146.6 reduce-scatter.23
  1946.3 136.6 reduce-scatter.29
  2090.5 151.2 reduce-scatter.21
  2244.8 181.7 reduce-scatter.25
  2429.3 184.4 reduce-scatter.27
Sparse Core Ops, SparseCore 1:
  195.5 68.0 all-gather.11
  266.6 55.2 all-gather.13
  325.0 76.5 all-gather.15
  404.9 75.8 all-gather.17
  484.0 55.1 all-gather.19
  542.2 99.3 all-gather.21
where the time goes:
time: 2630 us; the launch traced here: 2620 us
  waiting for transfers between devices  2090 us (79%)
  blocking collectives  293 us (11%)
  matrix products  130 us (5%)
  local copies, waits for them, and re-layouts  71.3 us (3%)
    reduce_scatter x1, waiting for transfers between devices, shards(): lax.psum_scatter(embed_term, 'dp', scatter_dimension=0, tiled=True)  570 us
    reduce_scatter x1, waiting for transfers between devices, shards(): lax.psum_scatter(decoder_term_half, 'dp', scatter_dimension=0, tiled=True)  194 us
    reduce_scatter x1, waiting for transfers between devices, shards(): lax.psum_scatter(down_weight_grad, ('dp', 'fsdp'), scatter_dimension=0, t...  187 us
    reduce_scatter x1, waiting for transfers between devices, shards(): lax.psum_scatter(up_weight_grad, ('dp', 'fsdp'), scatter_dimension=0, til...  185 us
    unnamed x20, waiting for transfers between devices  181 us
    reduce_scatter x1, waiting for transfers between devices, shards(): lax.psum_scatter(joint_weight_grad, ('dp', 'fsdp'), scatter_dimension=0,...  159 us
    reduce_scatter x1, waiting for transfers between devices, shards(): lax.psum_scatter(encoder_weight_grad, ('dp', 'fsdp'), scatter_dimension=0...  140 us
    reduce_scatter x1, waiting for transfers between devices, shards(): lax.psum_scatter(output_weight_grad, ('dp', 'fsdp'), scatter_dimension=0,...  139 us
  transfers between devices with their start and end apart: 18, of which 14 were waited for; matrix products, arithmetic and copies ran while one was open for 7% of the time, Pallas kernels for 0%

commit v1 on v0

v1 whole, which is shorter than its diff:
```python
import math

import jax
import jax.numpy as jnp
from jax import lax
from jax.sharding import PartitionSpec as P

D = 1024
HEAD_DIM = 64
GENES = 13500
LATENT = 512


NEG_SCORE = -1000000000.0
NORM_EPS = 1e-05
FREE_FLOOR = 1.0
FREE_TEMP = 0.25


def layer_norm(hidden, gain, shift):
    center = hidden - jnp.mean(hidden, axis=-1, keepdims=True)
    spread = jnp.mean(center * center, axis=-1, keepdims=True)
    return center * lax.rsqrt(spread + NORM_EPS) * gain + shift


def positions(coordinates):
    quarter = D // 4
    frequency = jnp.exp(jnp.arange(quarter, dtype=jnp.float32) * (-math.log(10000.0) / quarter))
    angle_x = coordinates[0][:, None] * frequency[None, :]
    angle_y = coordinates[1][:, None] * frequency[None, :]
    return jnp.concatenate(
        [jnp.sin(angle_x), jnp.cos(angle_x), jnp.sin(angle_y), jnp.cos(angle_y)], axis=1
    )


def matmul(left, right):
    return jnp.dot(left, right, preferred_element_type=jnp.float32)


def across(left, right):
    return lax.dot_general(
        left, right, (((1,), (1,)), ((), ())), preferred_element_type=jnp.float32
    )


def contract_rows(left, right):
    return lax.dot_general(
        left, right, (((0,), (0,)), ((), ())), preferred_element_type=jnp.float32
    )


def split_heads(joint):
    row_count = joint.shape[0]
    queries = joint[:, :D].reshape(row_count, -1, HEAD_DIM)
    keys = joint[:, D : 2 * D].reshape(row_count, -1, HEAD_DIM)
    values = joint[:, 2 * D :].reshape(row_count, -1, HEAD_DIM)
    return (queries, keys, values)


def masked_scores(queries, keys, allowed):
    scores = jnp.einsum(
        "qhd,khd->hqk", queries, keys, preferred_element_type=jnp.float32
    ) * HEAD_DIM ** (-0.5)
    return jnp.where(allowed[None], scores, NEG_SCORE)


def attention_forward(joint, allowed):
    queries, keys, values = split_heads(joint)
    masked = masked_scores(queries, keys, allowed)
    peak = jnp.max(masked, axis=-1, keepdims=True)
    raised = jnp.exp(masked - peak)
    denom = jnp.sum(raised, axis=-1, keepdims=True)
    probs = raised / denom
    logsum = peak + jnp.log(denom)
    context = jnp.einsum(
        "hqk,khd->qhd", probs.astype(jnp.bfloat16), values, preferred_element_type=jnp.float32
    )
    return (context.reshape(joint.shape[0], D).astype(jnp.bfloat16), logsum)


def attention_backward(joint, allowed, logsum, context_grad):
    row_count = joint.shape[0]
    queries, keys, values = split_heads(joint)
    probs = jnp.exp(masked_scores(queries, keys, allowed) - logsum)
    probs_low = probs.astype(jnp.bfloat16)
    incoming = context_grad.reshape(row_count, -1, HEAD_DIM)
    value_grad = jnp.einsum("hqk,qhd->khd", probs_low, incoming, preferred_element_type=jnp.float32)
    prob_grad = jnp.einsum("qhd,khd->hqk", incoming, values, preferred_element_type=jnp.float32)
    score_grad = (probs * (prob_grad - jnp.sum(probs * prob_grad, axis=-1, keepdims=True))).astype(
        jnp.bfloat16
    )
    query_grad = jnp.einsum(
        "hqk,khd->qhd", score_grad, keys, preferred_element_type=jnp.float32
    ) * HEAD_DIM ** (-0.5)
    key_grad = jnp.einsum(
        "hqk,qhd->khd", score_grad, queries, preferred_element_type=jnp.float32
    ) * HEAD_DIM ** (-0.5)
    return jnp.concatenate(
        [
            query_grad.reshape(row_count, D),
            key_grad.reshape(row_count, D),
            value_grad.reshape(row_count, D),
        ],
        axis=1,
    ).astype(jnp.bfloat16)

AXES = ("dp", "fsdp")
GROUP = 4
CHUNK = 3456
NARROW = 8


def low(values):
    return values.astype(jnp.bfloat16)


def wide(values):
    return values.astype(jnp.float32)


def device_total():
    return lax.axis_size("dp") * lax.axis_size("fsdp")


def device_index():
    return lax.axis_index("dp") * lax.axis_size("fsdp") + lax.axis_index("fsdp")


def swap(values, mask):
    return lax.ppermute(values, AXES, [(i, i ^ mask) for i in range(device_total())])


def ring_order():
    total = device_total() // GROUP
    return list(range(0, total, 2)) + list(range(total - 1, 0, -2))


def shift(values, step):
    order = ring_order()
    total = len(order)
    pairs = []
    for place in range(total):
        for quarter in range(GROUP):
            pairs.append(
                (order[place] * GROUP + quarter, order[(place + step) % total] * GROUP + quarter)
            )
    return lax.ppermute(values, AXES, pairs)


def ring_place():
    order = ring_order()
    inverse = [order.index(t) for t in range(len(order))]
    return jnp.array(inverse, jnp.int32)[device_index() // GROUP]


def ring_owner(step):
    order = ring_order()
    return jnp.array(order, jnp.int32)[(ring_place() - step) % len(order)]


def same_quarter():
    return [[d for d in range(lax.axis_size("dp")) if d % 2 == odd] for odd in range(2)]


def pick(blocks, index):
    return lax.dynamic_index_in_dim(blocks, index, 0, keepdims=False)


def ring_gather(block):
    total = device_total() // GROUP
    if total > NARROW:
        full = lax.all_gather(block, "dp", axis_index_groups=same_quarter(), axis=0, tiled=False)
        return jnp.stack([pick(full, ring_owner(s)) for s in range(total)])
    half = block.shape[0] // 2
    tops, bottoms = [block[:half]], [block[half:]]
    for _ in range(total - 1):
        tops.append(shift(tops[-1], 1))
        bottoms.append(shift(bottoms[-1], -1))
    return jnp.stack(
        [jnp.concatenate([tops[s], bottoms[(total - s) % total]]) for s in range(total)]
    )


def ring_scatter(blocks):
    total = device_total() // GROUP
    if total > NARROW:
        full = jnp.zeros_like(blocks)
        for s in range(total):
            full = lax.dynamic_update_index_in_dim(full, blocks[s], ring_owner(s), 0)
        return lax.psum_scatter(
            full, "dp", axis_index_groups=same_quarter(), scatter_dimension=0, tiled=False
        )
    half = blocks.shape[1] // 2
    top, bottom = blocks[1, :half], blocks[total - 1, half:]
    for s in range(2, total + 1):
        top = shift(top, 1)
        bottom = shift(bottom, -1)
        top = wide(top) + wide(blocks[s % total, :half])
        bottom = wide(bottom) + wide(blocks[(total - s) % total, half:])
        if s < total:
            top, bottom = low(top), low(bottom)
    return jnp.concatenate([top, bottom])


def group_exchange(blocks, quarter):
    return [pick(blocks, quarter)] + [swap(pick(blocks, quarter ^ m), m) for m in range(1, GROUP)]


def group_gather(values):
    pair = jnp.stack([values, swap(values, 2)])
    other = swap(pair, 1)
    return jnp.stack([pair[0], other[0], pair[1], other[1]])


def group_scatter(parts):
    mine = jnp.stack([parts[0], parts[2]])
    theirs = low(jnp.stack([parts[1], parts[3]]))
    summed = wide(mine) + wide(swap(theirs, 1))
    return summed[0] + wide(swap(low(summed[1]), 2))


def by_quarter(pieces, quarter):
    stacked = jnp.stack(pieces)
    return [pick(stacked, quarter ^ j) for j in range(GROUP)]


def gene_chunks(values):
    padded = jnp.pad(values, ((0, 0), (0, GROUP * CHUNK - GENES)))
    return jnp.stack([padded[:, j * CHUNK : (j + 1) * CHUNK] for j in range(GROUP)])


def sum_all(values):
    mask = 1
    while mask < device_total():
        values = values + swap(values, mask)
        mask *= 2
    return values


def scatter_all(values):
    me = device_index()
    mask = 1
    values = values[None]
    while mask < device_total():
        bit = (me // mask) % 2
        rows = values.shape[1]
        split = values.reshape(values.shape[0], rows // 2, 2, values.shape[2])
        keep = lax.dynamic_index_in_dim(split, bit, 2, keepdims=False)
        give = lax.dynamic_index_in_dim(split, 1 - bit, 2, keepdims=False)
        values = keep + swap(give, mask)
        mask *= 2
    return values[0, 0]


def place_rows(pieces, columns, quarter):
    total, rows, _ = pieces[0].shape
    low_col, high_col = columns
    full = jnp.zeros((total, GROUP, rows, high_col - low_col), jnp.bfloat16)
    for m in range(GROUP):
        for s in range(total):
            full = lax.dynamic_update_slice(
                full,
                pieces[m][s, :, low_col:high_col][None, None],
                (ring_owner(s), quarter ^ m, 0, 0),
            )
    return full.reshape(total * GROUP * rows, high_col - low_col)


def block_order(count):
    total = device_total() // GROUP
    owners = jnp.stack([ring_owner(s) for s in range(total)])
    source = jnp.repeat(owners, count) * count + jnp.tile(jnp.arange(count), total)
    return low(jnp.arange(total * count)[:, None] == source[None, :])


def halves_scatter(values, rows, ring_first):
    total = device_total() // GROUP
    me = device_index()
    core, side = me % 2, (me // 2) % 2
    split = values.reshape(total, 2, 2, rows, values.shape[1])
    keep = lax.dynamic_index_in_dim(split, core, 2, keepdims=False)
    give = lax.dynamic_index_in_dim(split, 1 - core, 2, keepdims=False)
    chip = low(wide(keep) + wide(swap(low(give), 1)))
    if ring_first:
        ringed = jnp.stack([pick(chip, ring_owner(s)) for s in range(total)])
        pair = low(ring_scatter(ringed.reshape(total, 2 * rows, -1)).reshape(2, rows, -1))
        return wide(pick(pair, side)) + wide(swap(pick(pair, 1 - side), 2))
    keep = lax.dynamic_index_in_dim(chip, side, 1, keepdims=False)
    give = lax.dynamic_index_in_dim(chip, 1 - side, 1, keepdims=False)
    both = low(wide(keep) + wide(swap(give, 2)))
    return wide(ring_scatter(jnp.stack([pick(both, ring_owner(s)) for s in range(total)])))


def shards(
    cells,
    coordinates,
    slide_ids,
    live_mask,
    components,
    noise,
    ramp_weight,
    embed_weight,
    query_key_value,
    output_weight,
    up_weight,
    up_bias,
    down_weight,
    down_bias,
    first_gain,
    first_shift,
    second_gain,
    second_shift,
    encoder_weight,
    encoder_bias,
    prior_mean,
    prior_logvar,
    decoder_weight,
):
    row_count = cells.shape[0]
    devices = device_total()
    total = devices // GROUP
    me = device_index()
    quarter = me % GROUP
    rows = embed_weight.shape[0]
    thin = decoder_weight.shape[0]
    cell_total = row_count * devices
    live = live_mask[0].astype(jnp.float32)
    slides = slide_ids[0]
    places = jnp.arange(row_count)
    allowed = (slides[:, None] == slides[None, :]) & (
        (live[None, :] > 0.5) | (places[:, None] == places[None, :])
    )
    onehot = (
        components[:, None] == jnp.arange(prior_mean.shape[0], dtype=jnp.int32)[None, :]
    ).astype(jnp.float32)

    cells_group = jnp.stack(group_exchange(gene_chunks(cells), quarter)).reshape(
        GROUP * row_count, CHUNK
    )
    live_group = group_gather(live_mask).reshape(-1).astype(jnp.float32)
    both = gene_chunks(jnp.concatenate([embed_weight, decoder_weight]))
    both = jnp.stack(by_quarter(group_exchange(both, quarter), quarter))
    embed_cols = ring_gather(both[:, :rows].reshape(GROUP * rows, CHUNK)).reshape(-1, CHUNK)
    small = jnp.concatenate(
        [
            up_bias.reshape(rows, 4),
            down_bias.reshape(rows, 1),
            first_gain.reshape(rows, 1),
            first_shift.reshape(rows, 1),
            second_gain.reshape(rows, 1),
            second_shift.reshape(rows, 1),
            encoder_bias.reshape(rows, 1),
            prior_mean.reshape(rows, 8),
            prior_logvar.reshape(rows, 8),
            jnp.full((rows, 1), jnp.sum(live), jnp.bfloat16),
        ],
        axis=1,
    )
    small_columns = small.shape[1]
    small = jnp.pad(small, ((0, 0), (0, 128 - small_columns)))
    first_unit = jnp.concatenate([query_key_value, output_weight, encoder_weight, small], axis=1)
    second_unit = jnp.concatenate(
        [
            up_weight,
            down_weight.reshape(4, rows, D).transpose(1, 0, 2).reshape(rows, 4 * D),
        ],
        axis=1,
    )
    width = first_unit.shape[1]
    pair = jnp.concatenate([first_unit, swap(first_unit, 2)])
    ringed = ring_gather(pair).reshape(total, 2, rows, width)
    other = swap(ringed, 1)
    first_pieces = [ringed[:, 0], other[:, 0], ringed[:, 1], other[:, 1]]
    ringed = ring_gather(second_unit)
    pair = jnp.stack([ringed, swap(ringed, 2)])
    other = swap(pair, 1)
    second_pieces = [pair[0], other[0], pair[1], other[1]]
    decoder_cols = ring_gather(both[:, rows:].reshape(GROUP * thin, CHUNK)).reshape(-1, CHUNK)

    joint_full = place_rows(first_pieces, (0, 3 * D), quarter)
    output_full = place_rows(first_pieces, (3 * D, 4 * D), quarter)
    encoder_full = place_rows(first_pieces, (4 * D, 5 * D), quarter)
    small_full = place_rows(first_pieces, (5 * D, 5 * D + 128), quarter)
    up_full = place_rows(second_pieces, (0, 4 * D), quarter)
    down_full = place_rows(second_pieces, (4 * D, 8 * D), quarter)
    down_full = (
        down_full.reshape(devices, rows, 4, D).transpose(0, 2, 1, 3).reshape(4 * devices * rows, D)
    )
    small_full = wide(small_full)
    up_bias_full = small_full[:, 0:4].reshape(-1)
    down_bias_full = small_full[:, 4]
    gain_first = small_full[:, 5]
    shift_first = small_full[:, 6]
    gain_second = small_full[:, 7]
    shift_second = small_full[:, 8]
    encoder_bias_full = small_full[:, 9]
    kinds = prior_mean.shape[0]

    def prior_full(columns):
        return columns.reshape(devices, kinds, -1).transpose(1, 0, 2).reshape(kinds, LATENT)

    prior_mean_full = prior_full(small_full[:, 10:18])
    prior_logvar_full = prior_full(small_full[:, 18:26])
    count = jnp.sum(small_full.reshape(devices, rows, 128)[:, 0, 26])

    feature_order = block_order(GROUP * rows)
    latent_order = block_order(GROUP * thin)
    embedded = low(across(cells_group, embed_cols))
    embedded = low(across(embedded, feature_order)).reshape(GROUP, row_count, D)
    embedded = group_scatter(embedded)
    start_state = embedded + positions(coordinates)
    normed_first = layer_norm(start_state, gain_first, shift_first).astype(jnp.bfloat16)
    joint = matmul(normed_first, joint_full).astype(jnp.bfloat16)
    context, logsum = attention_forward(joint, allowed)
    middle_state = start_state + matmul(context, output_full)
    normed_second = layer_norm(middle_state, gain_second, shift_second).astype(jnp.bfloat16)
    pre = matmul(normed_second, up_full) + up_bias_full
    active = jax.nn.gelu(pre, approximate=True).astype(jnp.bfloat16)
    end_state = middle_state + (matmul(active, down_full) + down_bias_full)
    end_low = end_state.astype(jnp.bfloat16)
    encoded = matmul(end_low, encoder_full) + encoder_bias_full
    latent_mean = encoded[:, :LATENT]
    latent_logvar = encoded[:, LATENT:]
    latent = (latent_mean + jnp.exp(0.5 * latent_logvar) * noise).astype(jnp.bfloat16)
    latent_group = group_gather(latent).reshape(GROUP * row_count, LATENT)
    latent_group = low(matmul(latent_group, latent_order))

    center = jnp.dot(onehot, prior_mean_full, precision=lax.Precision.HIGHEST)
    scale = jnp.dot(onehot, prior_logvar_full, precision=lax.Precision.HIGHEST)
    gap = latent_mean - center
    inverse = jnp.exp(-scale)
    grown = jnp.exp(latent_logvar)
    diverge = 0.5 * (scale - latent_logvar + (grown + gap * gap) * inverse - 1.0)
    kl_mean = sum_all(jnp.sum(live[:, None] * diverge, axis=0, keepdims=True))[0] / count

    recon = matmul(latent_group, decoder_cols)
    miss = recon - wide(cells_group)
    recon_local = jnp.sum(live_group * (0.5 * jnp.sum(miss * miss, axis=1)))
    shifted = (kl_mean - FREE_FLOOR) / FREE_TEMP
    free = FREE_FLOOR + FREE_TEMP * jax.nn.softplus(shifted)
    ratio = cell_total / count
    recon_grad = low(ratio * live_group[:, None] * miss)
    decoder_term = low(contract_rows(latent_group, recon_grad))
    decoder_block = low(ring_scatter(decoder_term.reshape(total, GROUP * thin, CHUNK)))
    latent_grad = low(across(recon_grad, decoder_cols))
    latent_grad = low(across(latent_grad, latent_order)).reshape(GROUP, row_count, LATENT)
    latent_grad = wide(low(group_scatter(latent_grad)))

    kl_scale = ratio * ramp_weight * jax.nn.sigmoid(shifted)[None, :] * live[:, None]
    pulled = kl_scale * gap * inverse
    mean_grad = latent_grad + pulled
    logvar_grad = latent_grad * 0.5 * jnp.exp(0.5 * latent_logvar) * noise + kl_scale * 0.5 * (
        grown * inverse - 1.0
    )
    encoded_grad = jnp.concatenate([mean_grad, logvar_grad], axis=1).astype(jnp.bfloat16)
    prior_mean_grad = jnp.dot(onehot.T, -pulled, precision=lax.Precision.HIGHEST)
    prior_logvar_grad = jnp.dot(
        onehot.T,
        kl_scale * 0.5 * (1.0 - (grown + gap * gap) * inverse),
        precision=lax.Precision.HIGHEST,
    )
    end_grad = across(encoded_grad, encoder_full)
    branch_grad = end_grad.astype(jnp.bfloat16)
    encoder_term = low(contract_rows(end_low, encoded_grad))
    encoder_bias_grad = jnp.sum(encoded_grad.astype(jnp.float32), axis=0)
    down_term = low(contract_rows(active, branch_grad))
    down_bias_grad = jnp.sum(branch_grad.astype(jnp.float32), axis=0)
    down_pack = jnp.concatenate(
        [
            encoder_term.reshape(devices, rows, D),
            down_term.reshape(devices, 4 * rows, D),
        ],
        axis=1,
    ).reshape(-1, D)
    down_pack = halves_scatter(down_pack, 5 * rows, False)
    encoder_weight_grad = down_pack[:rows]
    down_weight_grad = down_pack[rows:]
    active_grad = across(branch_grad, down_full)
    gelu_value, gelu_back = jax.vjp(lambda value: jax.nn.gelu(value, approximate=True), pre)
    pre_grad = gelu_back(active_grad)[0].astype(jnp.bfloat16)
    up_weight_grad = halves_scatter(low(contract_rows(normed_second, pre_grad)), rows, False)
    up_bias_grad = jnp.sum(pre_grad.astype(jnp.float32), axis=0)
    second_out_grad = across(pre_grad, up_full)
    norm_value, second_back = jax.vjp(layer_norm, middle_state, gain_second, shift_second)
    state_part, second_gain_grad, second_shift_grad = second_back(second_out_grad)
    middle_grad = end_grad + state_part
    attend_grad = middle_grad.astype(jnp.bfloat16)
    output_term = low(contract_rows(context, attend_grad))
    context_grad = across(attend_grad, output_full).astype(jnp.bfloat16)
    joint_grad = attention_backward(joint, allowed, logsum, context_grad)
    joint_term = low(contract_rows(normed_first, joint_grad))
    joint_pack = halves_scatter(jnp.concatenate([joint_term, output_term], axis=1), rows, True)
    joint_weight_grad = joint_pack[:, : 3 * D]
    output_weight_grad = joint_pack[:, 3 * D :]
    first_out_grad = across(joint_grad, joint_full)
    first_value, first_back = jax.vjp(layer_norm, start_state, gain_first, shift_first)
    start_part, first_gain_grad, first_shift_grad = first_back(first_out_grad)
    start_grad = middle_grad + start_part
    start_low = start_grad.astype(jnp.bfloat16)
    start_group = group_gather(start_low).reshape(GROUP * row_count, D)
    start_group = low(matmul(start_group, feature_order))
    embed_term = low(contract_rows(start_group, cells_group))
    embed_block = low(ring_scatter(embed_term.reshape(total, GROUP * rows, CHUNK)))
    cells_half = low(matmul(start_group, embed_cols) - wide(recon_grad))

    def to_owners(blocks):
        pieces = [blocks[0]] + [swap(blocks[m], m) for m in range(1, GROUP)]
        return jnp.concatenate(by_quarter(pieces, quarter), axis=1)[:, :GENES]

    cells_grad = to_owners(cells_half.reshape(GROUP, row_count, CHUNK))
    embed_block = embed_block.reshape(GROUP, rows, CHUNK)
    decoder_block = decoder_block.reshape(GROUP, thin, CHUNK)
    blocks = jnp.concatenate([embed_block, decoder_block], axis=1)
    blocks = [pick(blocks, quarter ^ m) for m in range(GROUP)]
    weight_grads = wide(to_owners(jnp.stack(blocks)))
    embed_grad, decoder_grad = weight_grads[:rows], weight_grads[rows:]

    def prior_rows(values):
        return values.reshape(kinds, devices, -1).transpose(1, 0, 2).reshape(devices, -1)

    vectors = [
        up_bias_grad,
        down_bias_grad,
        first_gain_grad,
        first_shift_grad,
        second_gain_grad,
        second_shift_grad,
        encoder_bias_grad,
    ]
    packed = jnp.concatenate(
        [vector.reshape(devices, -1) for vector in vectors]
        + [prior_rows(prior_mean_grad), prior_rows(prior_logvar_grad)],
        axis=1,
    )
    packed = scatter_all(packed)
    ends = [0]
    for vector in vectors:
        ends.append(ends[-1] + vector.shape[0] // devices)
    vector_grads = [packed[ends[i] : ends[i + 1]] for i in range(len(vectors))]
    prior_size = kinds * LATENT // devices
    prior_mean_out = packed[ends[-1] : ends[-1] + prior_size].reshape(kinds, -1)
    prior_logvar_out = packed[ends[-1] + prior_size :].reshape(kinds, -1)
    recon_total = sum_all(jnp.full((1, 128), recon_local, jnp.float32))[0, 0]
    loss = (recon_total / count + ramp_weight * jnp.sum(free)) / GENES
    return (
        loss,
        cells_grad,
        embed_grad,
        joint_weight_grad,
        output_weight_grad,
        up_weight_grad,
        vector_grads[0],
        down_weight_grad,
        vector_grads[1],
        vector_grads[2],
        vector_grads[3],
        vector_grads[4],
        vector_grads[5],
        encoder_weight_grad,
        vector_grads[6],
        prior_mean_out,
        prior_logvar_out,
        decoder_grad,
    )


def solution(mesh):
    in_specs = (
        P(("dp", "fsdp"), None),
        P(None, ("dp", "fsdp")),
        P(("dp", "fsdp"), None),
        P(("dp", "fsdp"), None),
        P(("dp", "fsdp")),
        P(("dp", "fsdp"), None),
        P(),
        P(("dp", "fsdp"), None),
        P(("dp", "fsdp"), None),
        P(("dp", "fsdp"), None),
        P(("dp", "fsdp"), None),
        P(("dp", "fsdp")),
        P(("dp", "fsdp"), None),
        P(("dp", "fsdp")),
        P(("dp", "fsdp")),
        P(("dp", "fsdp")),
        P(("dp", "fsdp")),
        P(("dp", "fsdp")),
        P(("dp", "fsdp"), None),
        P(("dp", "fsdp")),
        P(None, ("dp", "fsdp")),
        P(None, ("dp", "fsdp")),
        P(("dp", "fsdp"), None),
    )
    out_specs = (
        P(),
        P(("dp", "fsdp"), None),
        P(("dp", "fsdp"), None),
        P(("dp", "fsdp"), None),
        P(("dp", "fsdp"), None),
        P(("dp", "fsdp"), None),
        P(("dp", "fsdp")),
        P(("dp", "fsdp"), None),
        P(("dp", "fsdp")),
        P(("dp", "fsdp")),
        P(("dp", "fsdp")),
        P(("dp", "fsdp")),
        P(("dp", "fsdp")),
        P(("dp", "fsdp"), None),
        P(("dp", "fsdp")),
        P(None, ("dp", "fsdp")),
        P(None, ("dp", "fsdp")),
        P(("dp", "fsdp"), None),
    )
    return jax.shard_map(shards, mesh=mesh, in_specs=in_specs, out_specs=out_specs, check_vma=False)
```

time: 2630 us -> 1070 us (0.41)
  waiting for transfers between devices: 2090 us -> 402 us
  blocking collectives: 293 us -> 0 us
  starting transfers between devices: 0.92 us -> 187 us
  local copies, waits for them, and re-layouts: 71.3 us -> 230 us
  other arithmetic: 13.2 us -> 119 us
  matrix products: 130 us -> 89 us
    reduce_scatter x9 -> x0, waiting for transfers between devices: 1570 us -> none  [the longest x1 570 us: shards(): lax.psum_scatter(embed_term, 'dp', scatter_dimension=0, tiled=True)]
    ppermute x0 -> x173, waiting for transfers between devices: none -> 402 us  [the longest x126 252 us: shift(): return lax.ppermute(values, AXES, pairs)]
    all_gather x7 -> x0, waiting for transfers between devices: 338 us -> none  [the longest x1 129 us: shards(): lax.all_gather(embed_half, 'dp', axis=0, tiled=True)]
    ppermute x0 -> x173, starting transfers between devices: none -> 187 us  [the longest x126 152 us: shift(): return lax.ppermute(values, AXES, pairs)]
    unnamed x20 -> x0, waiting for transfers between devices: 181 us -> none
    all_gather x6 -> x0, blocking collectives: 127 us -> none  [the longest x1 41.4 us: shards(): lax.all_gather(prior_logvar, ('dp', 'fsdp'), axis=1, tiled=True)]
    psum x2 -> x0, blocking collectives: 95.7 us -> none  [shards(): lax.psum((jnp.sum(live[:, None] * diverge, axis=0), recon_local, jnp.sum(...]
    dynamic_update_slice x0 -> x134, local copies, waits for them, and re-layouts: none -> 92.7 us  [place_rows(): lax.dynamic_update_slice(full, pieces[m][s, :, low_col:high_col][None, No...]
  transfers between devices with their start and end apart: 18 -> 173, of which waited for: 14 -> 101; matrix products, arithmetic and copies ran while one was open for 7% -> 39% of each run, Pallas kernels for 0% -> 0%
where the time goes in v1:
time: 1070 us; the launch traced here: 1060 us
  waiting for transfers between devices  402 us (38%)
  local copies, waits for them, and re-layouts  230 us (21%)
  starting transfers between devices  187 us (17%)
  other arithmetic  119 us (11%)
  matrix products  89 us (8%)
  between operations  30.1 us (3%)
    ppermute x126, waiting for transfers between devices, shift(): return lax.ppermute(values, AXES, pairs)  252 us
    ppermute x126, starting transfers between devices, shift(): return lax.ppermute(values, AXES, pairs)  152 us
    ppermute x47, waiting for transfers between devices, swap(): lax.ppermute(values, AXES, [(i, i ^ mask) for i in range(device_total())])  150 us
    dynamic_update_slice x134, local copies, waits for them, and re-layouts, place_rows(): lax.dynamic_update_slice(full, pieces[m][s, :, low_col:high_col][None, No...  92.7 us
    dot_general x7, matrix products, across(): lax.dot_general(left, right, (((1,), (1,)), ((), ())), preferred_element_...  36.1 us
    ppermute x47, starting transfers between devices, swap(): lax.ppermute(values, AXES, [(i, i ^ mask) for i in range(device_total())])  35.9 us
    convert_element_type x45, other arithmetic, low(): return values.astype(jnp.bfloat16)  25.4 us
    unnamed x282, local copies, waits for them, and re-layouts  24.7 us
  transfers between devices with their start and end apart: 173, of which 101 were waited for; matrix products, arithmetic and copies ran while one was open for 39% of the time, Pallas kernels for 0%

profile of v1, /device:TPU:0, one launch (start us, length us, event | category | flops | bytes accessed | tf_op | source)
XLA Modules:
  0.0 1057.1 jit_solution(816010003531889425)
XLA Ops:
  107.9 16.0 %collective-permute-done.4 = bf16[128,3456]{0,1:T(8,128)(2,1)S(1)} collective-permute-done((bf16[128,3456]{0,1:T(8,128)(2,1)S(1)}, bf16[128,3456]{0,1:T(8,128)(2,1)S(1)}, u32[]{:S(2)}, u32[]{:S(2)}) %collective-permute-start.4) | collective-permute-done | bytes 884768 | tf_op jit(solution)/shard_map/ppermute | solution.py:130
  149.6 10.6 %collective-permute-done.60 = bf16[32,3456]{1,0:T(8,128)(2,1)S(1)} collective-permute-done((bf16[32,3456]{1,0:T(8,128)(2,1)}, bf16[32,3456]{1,0:T(8,128)(2,1)S(1)}, u32[]{:S(2)}, u32[]{:S(2)}) %collective-permute-start.60) | collective-permute-done | bytes 221216 | tf_op jit(solution)/shard_map/ppermute | solution.py:147
  166.9 9.0 collective-permute-done.61
  184.0 11.6 %collective-permute-done.62 = bf16[32,3456]{1,0:T(8,128)(2,1)S(1)} collective-permute-done((bf16[32,3456]{1,0:T(8,128)(2,1)S(1)}, bf16[32,3456]{1,0:T(8,128)(2,1)S(1)}, u32[]{:S(2)}, u32[]{:S(2)}) %collective-permute-start.62) | collective-permute-done | bytes 221216 | tf_op jit(solution)/shard_map/ppermute | solution.py:147
  210.3 5.7 collective-permute-done.35
  222.8 14.6 %collective-permute-done.36 = bf16[32,5248]{1,0:T(8,128)(2,1)S(1)} collective-permute-done((bf16[32,5248]{1,0:T(8,128)(2,1)S(1)}, bf16[32,5248]{1,0:T(8,128)(2,1)S(1)}, u32[]{:S(2)}, u32[]{:S(2)}) %collective-permute-start.36) | collective-permute-done | bytes 335904 | tf_op jit(solution)/shard_map/ppermute | solution.py:147
  311.7 10.4 collective-permute-done.15
  326.5 10.1 fusion.18
  342.3 15.1 %collective-permute-done.23 = bf16[128,1024]{1,0:T(8,128)(2,1)S(1)} collective-permute-done((bf16[128,1024]{1,0:T(8,128)(2,1)S(1)}, bf16[128,1024]{1,0:T(8,128)(2,1)S(1)}, u32[]{:S(2)}, u32[]{:S(2)}) %collective-permute-start.23) | collective-permute-done | bytes 262176 | tf_op jit(solution)/shard_map/ppermute | solution.py:130
  358.4 7.7 pad_maximum_fusion
  395.8 12.1 %constant_dynamic-update-slice_fusion.36 = (bf16[8,4,32,1024]{3,2,1,0:T(8,128)(2,1)}, bf16[8,4,32,1024]{3,2,1,0:T(8,128)(2,1)}) fusion(bf16[8,4,32,1024]{3,2,1,0:T(8,128)(2,1)} %get-tuple-element.360, s32[]{:T(128)S(6)} %select_n.3112, s32[]{:T(128)S(6)} %select_n.3087, bf16[8,32,5248]{2,1,0:T(8,128)(2,1)} %get-tuple-element.102, ...), kind=kLoop, calls=%fused_computation.742 | loop fusion | bytes 262156 | tf_op jit(solution)/shard_map/dynamic_update_slice | solution.py:261
  469.4 14.5 %reshape_reshape.4 = bf16[32,32,4,1024]{3,2,1,0:T(4,128)(2,1)} reshape(bf16[8,4,32,4096]{3,2,1,0:T(8,128)(2,1)} %fusion.129) | data formatting | bytes 16777216 | tf_op jit(solution)/shard_map/reshape;reshape | solution.py:387
  483.9 10.4 copy.570
  534.3 7.5 multiply_convert_fusion
  543.6 6.2 convolution_convert_fusion.9
  580.4 7.6 convert_reduce_fusion
  588.0 7.4 multiply_reduce_fusion.2
  607.5 6.0 convolution_convert_fusion.2
  618.6 5.9 fusion.4
  629.1 7.9 constant_dynamic-slice_fusion
  646.3 7.0 pad_maximum_fusion.1
  705.9 6.7 collective-permute-done.89
  719.9 8.2 collective-permute-done.90
  737.3 8.8 collective-permute-done.91
  749.6 7.1 collective-permute-done.92
  759.2 20.1 %collective-permute-done.87 = bf16[128,3456]{1,0:T(8,128)(2,1)S(1)} collective-permute-done((bf16[128,3456]{1,0:T(8,128)(2,1)S(1)}, bf16[128,3456]{1,0:T(8,128)(2,1)S(1)}, u32[]{:S(2)}, u32[]{:S(2)}) %collective-permute-start.87) | collective-permute-done | bytes 884768 | tf_op jit(solution)/shard_map/ppermute | solution.py:130
  780.4 11.8 %collective-permute-done.88 = bf16[128,3456]{1,0:T(8,128)(2,1)S(1)} collective-permute-done((bf16[128,3456]{1,0:T(8,128)(2,1)S(1)}, bf16[128,3456]{1,0:T(8,128)(2,1)S(1)}, u32[]{:S(2)}, u32[]{:S(2)}) %collective-permute-start.88) | collective-permute-done | bytes 884768 | tf_op jit(solution)/shard_map/ppermute | solution.py:130
  793.4 10.9 %collective-permute-done.93 = bf16[64,3456]{1,0:T(8,128)(2,1)S(1)} collective-permute-done((bf16[64,3456]{1,0:T(8,128)(2,1)S(1)}, bf16[64,3456]{1,0:T(8,128)(2,1)S(1)}, u32[]{:S(2)}, u32[]{:S(2)}) %collective-permute-start.93) | collective-permute-done | bytes 442400 | tf_op jit(solution)/shard_map/ppermute | solution.py:147
  806.9 10.5 collective-permute-done.101
  825.0 6.2 collective-permute-done.102
  902.9 8.7 collective-permute-done.137
  914.6 58.7 %collective-permute-done.135 = bf16[32,4096]{1,0:T(8,128)(2,1)S(1)} collective-permute-done((bf16[32,4096]{1,0:T(8,128)(2,1)S(1)}, bf16[32,4096]{1,0:T(8,128)(2,1)S(1)}, u32[]{:S(2)}, u32[]{:S(2)}) %collective-permute-start.135) | collective-permute-done | bytes 262176 | tf_op jit(solution)/shard_map/ppermute | solution.py:130
  (1044 shorter events, 666.0 us)
Async XLA Ops:
  4.4 72.0 %collective-permute-start.5 = (bf16[48,3456]{1,0:T(8,128)(2,1)}, bf16[48,3456]{1,0:T(8,128)(2,1)}, u32[]{:S(2)}, u32[]{:S(2)}) collective-permute-start(bf16[48,3456]{1,0:T(8,128)(2,1)} %get-tuple-element.277), channel_id=1, source_target_pairs={{0,1},{1,0},{2,3},{3,2},{4,5},{5,4},{6,7},{7,6},{8,9},{9,8},{10,11... | collective-permute-start | bytes 995336 | tf_op jit(solution)/shard_map/ppermute | solution.py:130
  4.9 71.9 %collective-permute-start.6 = (bf16[48,3456]{1,0:T(8,128)(2,1)}, bf16[48,3456]{1,0:T(8,128)(2,1)}, u32[]{:S(2)}, u32[]{:S(2)}) collective-permute-start(bf16[48,3456]{1,0:T(8,128)(2,1)} %get-tuple-element.276), channel_id=1, source_target_pairs={{0,2},{1,3},{2,0},{3,1},{4,6},{5,7},{6,4},{7,5},{8,10},{9,11},{10,... | collective-permute-start | bytes 995336 | tf_op jit(solution)/shard_map/ppermute | solution.py:130
  7.4 71.1 %collective-permute-start.7 = (bf16[48,3456]{1,0:T(8,128)(2,1)}, bf16[48,3456]{1,0:T(8,128)(2,1)}, u32[]{:S(2)}, u32[]{:S(2)}) collective-permute-start(bf16[48,3456]{1,0:T(8,128)(2,1)} %get-tuple-element.275), channel_id=1, source_target_pairs={{0,3},{1,2},{2,1},{3,0},{4,7},{5,6},{6,5},{7,4},{8,11},{9,10},{10,... | collective-permute-start | bytes 995336 | tf_op jit(solution)/shard_map/ppermute | solution.py:130
  8.5 76.0 %collective-permute-start.41 = (bf16[16,8192]{1,0:T(8,128)(2,1)}, bf16[16,8192]{1,0:T(8,128)(2,1)}, u32[]{:S(2)}, u32[]{:S(2)}) collective-permute-start(bf16[16,8192]{1,0:T(8,128)(2,1)} %get-tuple-element.316), channel_id=1, source_target_pairs={{0,4},{1,5},{2,6},{3,7},{8,0},{9,1},{10,2},{11,3},{16,8},{17,9},{1... | collective-permute-start | bytes 786440 | tf_op jit(solution)/shard_map/ppermute | solution.py:147
  10.3 59.1 %collective-permute-start = (s32[1,128]{1,0:T(1,128)}, s32[1,128]{1,0:T(1,128)}, u32[]{:S(2)}, u32[]{:S(2)}) collective-permute-start(s32[1,128]{1,0:T(1,128)} %param.490), channel_id=1, source_target_pairs={{0,2},{1,3},{2,0},{3,1},{4,6},{5,7},{6,4},{7,5},{8,10},{9,11},{10,... | collective-permute-start | bytes 1544 | tf_op jit(solution)/shard_map/ppermute | solution.py:130
  76.8 29.6 %collective-permute-start.3 = (bf16[128,3456]{0,1:T(8,128)(2,1)S(1)}, bf16[128,3456]{0,1:T(8,128)(2,1)S(1)}, u32[]{:S(2)}, u32[]{:S(2)}) collective-permute-start(bf16[128,3456]{0,1:T(8,128)(2,1)S(1)} %get-tuple-element.188), channel_id=1, source_target_pairs={{0,2},{1,3},{2,0},{3,1},{4,6},{5,7},{6,4},{7,5},{8,10},{9,11},{10,... | collective-permute-start | bytes 2654216 | tf_op jit(solution)/shard_map/ppermute | solution.py:130
  78.5 45.4 %collective-permute-start.4 = (bf16[128,3456]{0,1:T(8,128)(2,1)S(1)}, bf16[128,3456]{0,1:T(8,128)(2,1)S(1)}, u32[]{:S(2)}, u32[]{:S(2)}) collective-permute-start(bf16[128,3456]{0,1:T(8,128)(2,1)S(1)} %get-tuple-element.187), channel_id=1, source_target_pairs={{0,3},{1,2},{2,1},{3,0},{4,7},{5,6},{6,5},{7,4},{8,11},{9,10},{10,... | collective-permute-start | bytes 2654216 | tf_op jit(solution)/shard_map/ppermute | solution.py:130
  84.5 40.9 %collective-permute-start.2 = (bf16[128,3456]{0,1:T(8,128)(2,1)S(1)}, bf16[128,3456]{0,1:T(8,128)(2,1)S(1)}, u32[]{:S(2)}, u32[]{:S(2)}) collective-permute-start(bf16[128,3456]{0,1:T(8,128)(2,1)S(1)} %get-tuple-element.189), channel_id=1, source_target_pairs={{0,1},{1,0},{2,3},{3,2},{4,5},{5,4},{6,7},{7,6},{8,9},{9,8},{10,11... | collective-permute-start | bytes 2654216 | tf_op jit(solution)/shard_map/ppermute | solution.py:130
  101.1 29.4 %collective-permute-start.25 = (bf16[32,5248]{1,0:T(8,128)(2,1)}, bf16[32,5248]{1,0:T(8,128)(2,1)}, u32[]{:S(2)}, u32[]{:S(2)}) collective-permute-start(bf16[32,5248]{1,0:T(8,128)(2,1)} %pad_maximum_fusion.32), channel_id=1, source_target_pairs={{0,8},{1,9},{2,10},{3,11},{8,16},{9,17},{10,18},{11,19},{16,24},{1... | collective-permute-start | bytes 1007624 | tf_op jit(solution)/shard_map/ppermute | solution.py:147
  102.7 34.1 %collective-permute-start.59 = (bf16[32,3456]{1,0:T(8,128)(2,1)}, bf16[32,3456]{1,0:T(8,128)(2,1)}, u32[]{:S(2)}, u32[]{:S(2)}) collective-permute-start(bf16[32,3456]{1,0:T(8,128)(2,1)} %bitcast.302), channel_id=1, source_target_pairs={{0,4},{1,5},{2,6},{3,7},{8,0},{9,1},{10,2},{11,3},{16,8},{17,9},{1... | collective-permute-start | bytes 663560 | tf_op jit(solution)/shard_map/ppermute | solution.py:147
  106.3 32.2 %collective-permute-start.58 = (bf16[32,3456]{1,0:T(8,128)(2,1)}, bf16[32,3456]{1,0:T(8,128)(2,1)}, u32[]{:S(2)}, u32[]{:S(2)}) collective-permute-start(bf16[32,3456]{1,0:T(8,128)(2,1)} %bitcast.301), channel_id=1, source_target_pairs={{0,8},{1,9},{2,10},{3,11},{8,16},{9,17},{10,18},{11,19},{16,24},{1... | collective-permute-start | bytes 663560 | tf_op jit(solution)/shard_map/ppermute | solution.py:147
  208.8 35.0 %collective-permute-start.11 = (bf16[64,3456]{1,0:T(8,128)(2,1)S(1)}, bf16[64,3456]{1,0:T(8,128)(2,1)S(1)}, u32[]{:S(2)}, u32[]{:S(2)}) collective-permute-start(bf16[64,3456]{1,0:T(8,128)(2,1)S(1)} %collective-permute-done.10), channel_id=1, source_target_pairs={{0,4},{1,5},{2,6},{3,7},{8,0},{9,1},{10,2},{11,3},{16,8},{17,9},{1... | collective-permute-start | bytes 1327112 | tf_op jit(solution)/shard_map/ppermute | solution.py:147
  243.8 262.8 %collective-permute-start.71 = (bf16[32,3456]{1,0:T(8,128)(2,1)}, bf16[32,3456]{1,0:T(8,128)(2,1)}, u32[]{:S(2)}, u32[]{:S(2)}) collective-permute-start(bf16[32,3456]{1,0:T(8,128)(2,1)} %collective-permute-done.70), channel_id=1, source_target_pairs={{0,8},{1,9},{2,10},{3,11},{8,16},{9,17},{10,18},{11,19},{16,24},{1... | collective-permute-start | bytes 663560 | tf_op jit(solution)/shard_map/ppermute | solution.py:147
  244.3 33.6 %collective-permute-start.12 = (bf16[64,3456]{1,0:T(8,128)(2,1)S(1)}, bf16[64,3456]{1,0:T(8,128)(2,1)S(1)}, u32[]{:S(2)}, u32[]{:S(2)}) collective-permute-start(bf16[64,3456]{1,0:T(8,128)(2,1)S(1)} %collective-permute-done.11), channel_id=1, source_target_pairs={{0,4},{1,5},{2,6},{3,7},{8,0},{9,1},{10,2},{11,3},{16,8},{17,9},{1... | collective-permute-start | bytes 1327112 | tf_op jit(solution)/shard_map/ppermute | solution.py:147
  246.6 31.6 %collective-permute-start.18 = (bf16[64,3456]{1,0:T(8,128)(2,1)S(1)}, bf16[64,3456]{1,0:T(8,128)(2,1)S(1)}, u32[]{:S(2)}, u32[]{:S(2)}) collective-permute-start(bf16[64,3456]{1,0:T(8,128)(2,1)S(1)} %collective-permute-done.17), channel_id=1, source_target_pairs={{0,8},{1,9},{2,10},{3,11},{8,16},{9,17},{10,18},{11,19},{16,24},{1... | collective-permute-start | bytes 1327112 | tf_op jit(solution)/shard_map/ppermute | solution.py:147
  272.2 85.7 %collective-permute-start.54 = (bf16[8,32,8192]{2,1,0:T(8,128)(2,1)}, bf16[8,32,8192]{2,1,0:T(8,128)(2,1)}, u32[]{:S(2)}, u32[]{:S(2)}) collective-permute-start(bf16[8,32,8192]{2,1,0:T(8,128)(2,1)} %constant_dynamic-update-slice_fusion.12), channel_id=1, source_target_pairs={{0,2},{1,3},{2,0},{3,1},{4,6},{5,7},{6,4},{7,5},{8,10},{9,11},{10,... | collective-permute-start | bytes 12582920 | tf_op jit(solution)/shard_map/ppermute | solution.py:130
  307.7 58.4 %collective-permute-start.39 = (bf16[8,2,32,5248]{3,2,1,0:T(8,128)(2,1)}, bf16[8,2,32,5248]{3,2,1,0:T(8,128)(2,1)}, u32[]{:S(2)}, u32[]{:S(2)}) collective-permute-start(bf16[8,2,32,5248]{3,2,1,0:T(8,128)(2,1)} %constant_dynamic-update-slice_fusion.2), channel_id=1, source_target_pairs={{0,1},{1,0},{2,3},{3,2},{4,5},{5,4},{6,7},{7,6},{8,9},{9,8},{10,11... | collective-permute-start | bytes 16121864 | tf_op jit(solution)/shard_map/ppermute | solution.py:130
  366.1 68.7 %collective-permute-start.55 = (bf16[2,8,32,8192]{3,2,1,0:T(8,128)(2,1)}, bf16[2,8,32,8192]{3,2,1,0:T(8,128)(2,1)}, u32[]{:S(2)}, u32[]{:S(2)}) collective-permute-start(bf16[2,8,32,8192]{3,2,1,0:T(8,128)(2,1)} %pad_maximum_fusion), channel_id=1, source_target_pairs={{0,1},{1,0},{2,3},{3,2},{4,5},{5,4},{6,7},{7,6},{8,9},{9,8},{10,11... | collective-permute-start | bytes 25165832 | tf_op jit(solution)/shard_map/ppermute | solution.py:130
  576.3 85.9 %collective-permute-start.104 = (bf16[32,3456]{1,0:T(8,128)(2,1)}, bf16[32,3456]{1,0:T(8,128)(2,1)}, u32[]{:S(2)}, u32[]{:S(2)}) collective-permute-start(bf16[32,3456]{1,0:T(8,128)(2,1)} %get-tuple-element.174), channel_id=1, source_target_pairs={{0,8},{1,9},{2,10},{3,11},{8,16},{9,17},{10,18},{11,19},{16,24},{1... | collective-permute-start | bytes 663560 | tf_op jit(solution)/shard_map/ppermute | solution.py:147
  576.3 86.9 %collective-permute-start.111 = (bf16[32,3456]{1,0:T(8,128)(2,1)}, bf16[32,3456]{1,0:T(8,128)(2,1)}, u32[]{:S(2)}, u32[]{:S(2)}) collective-permute-start(bf16[32,3456]{1,0:T(8,128)(2,1)} %get-tuple-element.175), channel_id=1, source_target_pairs={{0,4},{1,5},{2,6},{3,7},{8,0},{9,1},{10,2},{11,3},{16,8},{17,9},{1... | collective-permute-start | bytes 663560 | tf_op jit(solution)/shard_map/ppermute | solution.py:147
  617.0 67.9 %collective-permute-start.84 = (bf16[128,1024]{1,0:T(8,128)(2,1)}, bf16[128,1024]{1,0:T(8,128)(2,1)}, u32[]{:S(2)}, u32[]{:S(2)}) collective-permute-start(bf16[128,1024]{1,0:T(8,128)(2,1)} %add_convert_fusion), channel_id=1, source_target_pairs={{0,2},{1,3},{2,0},{3,1},{4,6},{5,7},{6,4},{7,5},{8,10},{9,11},{10,... | collective-permute-start | bytes 786440 | tf_op jit(solution)/shard_map/ppermute | solution.py:130
  627.6 266.5 %collective-permute-start.157 = (bf16[8,2,160,1024]{3,2,0,1:T(8,128)(2,1)}, bf16[8,2,160,1024]{3,2,0,1:T(8,128)(2,1)}, u32[]{:S(2)}, u32[]{:S(2)}) collective-permute-start(bf16[8,2,160,1024]{3,2,0,1:T(8,128)(2,1)} %bitcast.1571), channel_id=1, source_target_pairs={{0,1},{1,0},{2,3},{3,2},{4,5},{5,4},{6,7},{7,6},{8,9},{9,8},{10,11... | collective-permute-start | bytes 15728648 | tf_op jit(solution)/shard_map/ppermute | solution.py:130
  662.1 178.7 %collective-permute-start.136 = (bf16[8,2,32,4096]{3,2,0,1:T(8,128)(2,1)}, bf16[8,2,32,4096]{3,2,0,1:T(8,128)(2,1)}, u32[]{:S(2)}, u32[]{:S(2)}) collective-permute-start(bf16[8,2,32,4096]{3,2,0,1:T(8,128)(2,1)} %bitcast.1572), channel_id=1, source_target_pairs={{0,1},{1,0},{2,3},{3,2},{4,5},{5,4},{6,7},{7,6},{8,9},{9,8},{10,11... | collective-permute-start | bytes 12582920 | tf_op jit(solution)/shard_map/ppermute | solution.py:130
  715.2 42.2 %collective-permute-start.86 = (bf16[128,3456]{1,0:T(8,128)(2,1)S(1)}, bf16[128,3456]{1,0:T(8,128)(2,1)S(1)}, u32[]{:S(2)}, u32[]{:S(2)}) collective-permute-start(bf16[128,3456]{1,0:T(8,128)(2,1)S(1)} %get-tuple-element.185), channel_id=1, source_target_pairs={{0,1},{1,0},{2,3},{3,2},{4,5},{5,4},{6,7},{7,6},{8,9},{9,8},{10,11... | collective-permute-start | bytes 2654216 | tf_op jit(solution)/shard_map/ppermute | solution.py:130
  757.2 35.0 %collective-permute-start.88 = (bf16[128,3456]{1,0:T(8,128)(2,1)S(1)}, bf16[128,3456]{1,0:T(8,128)(2,1)S(1)}, u32[]{:S(2)}, u32[]{:S(2)}) collective-permute-start(bf16[128,3456]{1,0:T(8,128)(2,1)S(1)} %get-tuple-element.183), channel_id=1, source_target_pairs={{0,3},{1,2},{2,1},{3,0},{4,7},{5,6},{6,5},{7,4},{8,11},{9,10},{10,... | collective-permute-start | bytes 2654216 | tf_op jit(solution)/shard_map/ppermute | solution.py:130
  757.4 77.3 %collective-permute-start.120 = (bf16[8,2,32,4096]{3,2,1,0:T(8,128)(2,1)}, bf16[8,2,32,4096]{3,2,1,0:T(8,128)(2,1)}, u32[]{:S(2)}, u32[]{:S(2)}) collective-permute-start(bf16[8,2,32,4096]{3,2,1,0:T(8,128)(2,1)} %dynamic-slice_bitcast_fusion), channel_id=1, source_target_pairs={{0,1},{1,0},{2,3},{3,2},{4,5},{5,4},{6,7},{7,6},{8,9},{9,8},{10,11... | collective-permute-start | bytes 12582920 | tf_op jit(solution)/shard_map/ppermute | solution.py:130
  857.4 54.3 %collective-permute-start.137 = (bf16[8,32,4096]{2,1,0:T(8,128)(2,1)}, bf16[8,32,4096]{2,1,0:T(8,128)(2,1)S(1)}, u32[]{:S(2)}, u32[]{:S(2)}) collective-permute-start(bf16[8,32,4096]{2,1,0:T(8,128)(2,1)} %dynamic-slice_bitcast_fusion.2), channel_id=1, source_target_pairs={{0,2},{1,3},{2,0},{3,1},{4,6},{5,7},{6,4},{7,5},{8,10},{9,11},{10,... | collective-permute-start | bytes 6291464 | tf_op jit(solution)/shard_map/ppermute | solution.py:130
  899.5 76.6 %collective-permute-start.158 = (bf16[8,160,1024]{2,1,0:T(8,128)(2,1)S(1)}, bf16[8,160,1024]{2,1,0:T(8,128)(2,1)S(1)}, u32[]{:S(2)}, u32[]{:S(2)}) collective-permute-start(bf16[8,160,1024]{2,1,0:T(8,128)(2,1)S(1)} %dynamic-slice_bitcast_fusion.1), channel_id=1, source_target_pairs={{0,2},{1,3},{2,0},{3,1},{4,6},{5,7},{6,4},{7,5},{8,10},{9,11},{10,... | collective-permute-start | bytes 7864328 | tf_op jit(solution)/shard_map/ppermute | solution.py:130
  902.0 71.4 %collective-permute-start.135 = (bf16[32,4096]{1,0:T(8,128)(2,1)S(1)}, bf16[32,4096]{1,0:T(8,128)(2,1)S(1)}, u32[]{:S(2)}, u32[]{:S(2)}) collective-permute-start(bf16[32,4096]{1,0:T(8,128)(2,1)S(1)} %dynamic-slice_bitcast_fusion.17), channel_id=1, source_target_pairs={{0,2},{1,3},{2,0},{3,1},{4,6},{5,7},{6,4},{7,5},{8,10},{9,11},{10,... | collective-permute-start | bytes 786440 | tf_op jit(solution)/shard_map/ppermute | solution.py:130
  912.5 62.3 %collective-permute-start.138 = (bf16[16,4096]{1,0:T(8,128)(2,1)S(1)}, bf16[16,4096]{1,0:T(8,128)(2,1)S(1)}, u32[]{:S(2)}, u32[]{:S(2)}) collective-permute-start(bf16[16,4096]{1,0:T(8,128)(2,1)S(1)} %get-tuple-element.260), channel_id=1, source_target_pairs={{0,8},{1,9},{2,10},{3,11},{8,16},{9,17},{10,18},{11,19},{16,24},{1... | collective-permute-start | bytes 393224 | tf_op jit(solution)/shard_map/ppermute | solution.py:147
  913.7 92.2 %collective-permute-start.145 = (bf16[16,4096]{1,0:T(8,128)(2,1)S(1)}, bf16[16,4096]{1,0:T(8,128)(2,1)S(1)}, u32[]{:S(2)}, u32[]{:S(2)}) collective-permute-start(bf16[16,4096]{1,0:T(8,128)(2,1)S(1)} %get-tuple-element.261), channel_id=1, source_target_pairs={{0,4},{1,5},{2,6},{3,7},{8,0},{9,1},{10,2},{11,3},{16,8},{17,9},{1... | collective-permute-start | bytes 393224 | tf_op jit(solution)/shard_map/ppermute | solution.py:147
  1009.5 35.3 %collective-permute-start.144 = (bf16[16,4096]{1,0:T(8,128)(2,1)S(1)}, bf16[16,4096]{1,0:T(8,128)(2,1)S(1)}, u32[]{:S(2)}, u32[]{:S(2)}) collective-permute-start(bf16[16,4096]{1,0:T(8,128)(2,1)S(1)} %get-tuple-element.258), channel_id=1, source_target_pairs={{0,8},{1,9},{2,10},{3,11},{8,16},{9,17},{10,18},{11,19},{16,24},{1... | collective-permute-start | bytes 393224 | tf_op jit(solution)/shard_map/ppermute | solution.py:147
  (272 other events, 3225.8 us)

commit v2 on v1

--- a/solution.py
+++ b/solution.py
@@ -1,8 +1,11 @@
+import functools
 import math
 
 import jax
 import jax.numpy as jnp
 from jax import lax
+from jax.experimental import pallas as pl
+from jax.experimental.pallas import tpu as pltpu
 from jax.sharding import PartitionSpec as P
 
 D = 1024
@@ -164,21 +167,6 @@
 
 def pick(blocks, index):
     return lax.dynamic_index_in_dim(blocks, index, 0, keepdims=False)
-
-
-def ring_gather(block):
-    total = device_total() // GROUP
-    if total > NARROW:
-        full = lax.all_gather(block, "dp", axis_index_groups=same_quarter(), axis=0, tiled=False)
-        return jnp.stack([pick(full, ring_owner(s)) for s in range(total)])
-    half = block.shape[0] // 2
-    tops, bottoms = [block[:half]], [block[half:]]
-    for _ in range(total - 1):
-        tops.append(shift(tops[-1], 1))
-        bottoms.append(shift(bottoms[-1], -1))
-    return jnp.stack(
-        [jnp.concatenate([tops[s], bottoms[(total - s) % total]]) for s in range(total)]
-    )
 
 
 def ring_scatter(blocks):
@@ -252,25 +240,8 @@
     return values[0, 0]
 
 
-def place_rows(pieces, columns, quarter):
-    total, rows, _ = pieces[0].shape
-    low_col, high_col = columns
-    full = jnp.zeros((total, GROUP, rows, high_col - low_col), jnp.bfloat16)
-    for m in range(GROUP):
-        for s in range(total):
-            full = lax.dynamic_update_slice(
-                full,
-                pieces[m][s, :, low_col:high_col][None, None],
-                (ring_owner(s), quarter ^ m, 0, 0),
-            )
-    return full.reshape(total * GROUP * rows, high_col - low_col)
-
-
-def block_order(count):
-    total = device_total() // GROUP
-    owners = jnp.stack([ring_owner(s) for s in range(total)])
-    source = jnp.repeat(owners, count) * count + jnp.tile(jnp.arange(count), total)
-    return low(jnp.arange(total * count)[:, None] == source[None, :])
+def by_ring(blocks):
+    return jnp.stack([pick(blocks, ring_owner(s)) for s in range(blocks.shape[0])])
 
 
 def halves_scatter(values, rows, ring_first):
@@ -289,6 +260,218 @@
     give = lax.dynamic_index_in_dim(chip, 1 - side, 1, keepdims=False)
     both = low(wide(keep) + wide(swap(give, 2)))
     return wide(ring_scatter(jnp.stack([pick(both, ring_owner(s)) for s in range(total)])))
+
+
+MESH = pl.DeviceIdType.MESH
+
+
+class Where:
+    def __init__(self, total):
+        dp = lax.axis_index("dp")
+        self.total = total
+        self.core = lax.axis_index("fsdp")
+        self.x = dp % 2
+        self.t = dp // 2
+        self.quarter = 2 * self.x + self.core
+        y, z = self.t % 2, self.t // 2
+        self.k = z + y * (total - 1 - 2 * z)
+        self.right = (2 * self.owner(-1) + self.x, self.core)
+        self.left = (2 * self.owner(1) + self.x, self.core)
+        self.peers = [
+            None,
+            (dp, 1 - self.core),
+            (2 * self.t + 1 - self.x, self.core),
+            (2 * self.t + 1 - self.x, 1 - self.core),
+        ]
+        self.quarters = [
+            self.quarter,
+            2 * self.x + 1 - self.core,
+            2 * (1 - self.x) + self.core,
+            2 * (1 - self.x) + 1 - self.core,
+        ]
+
+    def owner(self, step):
+        place = (self.k - step + self.total) % self.total
+        y = place // (self.total // 2)
+        return 2 * (place + y * (self.total - 1 - 2 * place)) + y
+
+    def meet(self):
+        barrier = pltpu.get_barrier_semaphore()
+        others = self.peers[1:] + [self.right, self.left]
+        for other in others:
+            pl.semaphore_signal(barrier, inc=1, device_id=other, device_id_type=MESH)
+        pl.semaphore_wait(barrier, len(others))
+
+
+class Copies:
+    def __init__(self, send_sems, recv_sems, local_sems):
+        self.send_sems, self.recv_sems, self.local_sems = send_sems, recv_sems, local_sems
+        self.remote_count = self.local_count = 0
+        self.sent = []
+
+    def send(self, source, target, device):
+        at = self.remote_count
+        self.remote_count += 1
+        copy = pltpu.make_async_remote_copy(
+            source,
+            target,
+            self.send_sems.at[at],
+            self.recv_sems.at[at],
+            device_id=device,
+            device_id_type=MESH,
+        )
+        copy.start()
+        self.sent.append(copy)
+        return copy
+
+    def local(self, source, target):
+        at = self.local_count
+        self.local_count += 1
+        copy = pltpu.make_async_copy(source, target, self.local_sems.at[at])
+        copy.start()
+        return copy
+
+    def finish(self):
+        for copy in self.sent:
+            copy.wait_send()
+
+
+def gather_kernel(total, *refs):
+    (cells, embed, decoder, joint, small, output, encoder, up, down) = refs[:9]
+    (cells_all, embed_all, decoder_all, joint_all, small_all) = refs[9:14]
+    (output_all, encoder_all, up_all, down_all) = refs[14:18]
+    here = Where(total)
+    copies = Copies(*refs[18:])
+    here.meet()
+    t, x, core = here.t, here.x, here.core
+    last = total - 1
+
+    late = [(up, up_all, 1), (output, output_all, 1), (down, down_all, -1), (encoder, encoder_all, -1)]
+    towards = {1: here.right, -1: here.left}
+    flying = {}
+    for n, (own, full, way) in enumerate(late):
+        flying["late", n] = copies.send(own, full.at[t, x, core], towards[way])
+    shares = []
+    for m in (2, 3, 1):
+        to, chunk = here.peers[m], here.quarters[m]
+        shares.append(copies.send(embed.at[chunk], embed_all.at[t, here.quarter], to))
+        shares.append(copies.send(decoder.at[chunk], decoder_all.at[t, here.quarter], to))
+    pairs = [
+        copies.send(own, full.at[t, x, core], here.peers[2])
+        for own, full in ((joint, joint_all), (small, small_all))
+    ]
+    cell_moves = [
+        copies.send(cells.at[here.quarters[m]], cells_all.at[m], here.peers[m]) for m in (2, 3, 1)
+    ]
+    own_table = [
+        copies.local(embed.at[here.quarter], embed_all.at[t, here.quarter]),
+        copies.local(decoder.at[here.quarter], decoder_all.at[t, here.quarter]),
+    ]
+    own_early = [
+        copies.local(own, full.at[t, x, core])
+        for own, full in ((joint, joint_all), (small, small_all))
+    ]
+    own_late = [copies.local(own, full.at[t, x, core]) for own, full, _ in late]
+    own_cells = copies.local(cells.at[here.quarter], cells_all.at[0])
+
+    def late_step(s):
+        for n, (_, full, way) in enumerate(late):
+            flying["late", n].wait_recv()
+            if s < last:
+                block = full.at[here.owner(way * s), x, core]
+                flying["late", n] = copies.send(block, block, towards[way])
+
+    def early_block(full, way, s):
+        return full.at[here.owner(way * s), 0 if way == 1 else 1, core]
+
+    def table_block(full, way, s):
+        return full.at[here.owner(way * s), pl.ds(0 if way == 1 else 2, 2)]
+
+    early = [(full, way, early_block) for full in (joint_all, small_all) for way in (1, -1)]
+    tables = [(full, way, table_block) for full in (embed_all, decoder_all) for way in (1, -1)]
+
+    def step(name, items, s):
+        if s == 0:
+            for copy in {"early": own_early, "table": own_table}[name]:
+                copy.wait()
+            for copy in {"early": pairs, "table": shares}[name]:
+                copy.wait_recv()
+        for n, (full, way, block_of) in enumerate(items):
+            if s > 0:
+                flying[name, n].wait_recv()
+            if s < last:
+                block = block_of(full, way, s)
+                flying[name, n] = copies.send(block, block, towards[way])
+
+    across_x, across_core = [], []
+    for slot in range(1, last + 7):
+        if slot <= last:
+            late_step(slot)
+        if slot == last:
+            for copy in own_late:
+                copy.wait()
+            for _, full, _ in late:
+                block = full.at[:, x, core]
+                across_x.append(copies.send(block, block, here.peers[2]))
+        if 0 <= slot - 2 <= last:
+            step("early", early, slot - 2)
+        if slot - 2 == last:
+            for full in (joint_all, small_all):
+                block = full.at[:, :, core]
+                across_core.append(copies.send(block, block, here.peers[1]))
+        if 0 <= slot - 3 <= last:
+            step("table", tables, slot - 3)
+    for copy, (_, full, _) in zip(across_x, late):
+        copy.wait_recv()
+        block = full.at[:, :, core]
+        across_core.append(copies.send(block, block, here.peers[1]))
+    for copy in cell_moves + across_core:
+        copy.wait_recv()
+    own_cells.wait()
+    copies.finish()
+
+
+def gather_weights(cells, embed, decoder, joint, small, output, encoder, up, down):
+    total = device_total() // GROUP
+    own = [joint, small, output, encoder, up, down]
+    tables = [embed, decoder]
+    operands = [cells] + tables + own
+    shapes = (
+        [cells.shape]
+        + [(total,) + v.shape for v in tables]
+        + [(total, 2, 2) + v.shape for v in own]
+    )
+    remote = 15 + 12 * (total - 1) + 10
+    return pl.pallas_call(
+        functools.partial(gather_kernel, total),
+        out_shape=[jax.ShapeDtypeStruct(s, jnp.bfloat16) for s in shapes],
+        in_specs=[pl.BlockSpec(memory_space=pl.ANY)] * len(operands),
+        out_specs=[pl.BlockSpec(memory_space=pl.ANY)] * len(operands),
+        scratch_shapes=[
+            pltpu.SemaphoreType.DMA((remote,)),
+            pltpu.SemaphoreType.DMA((remote,)),
+            pltpu.SemaphoreType.DMA((9,)),
+        ],
+        compiler_params=pltpu.CompilerParams(
+            collective_id=1, has_side_effects=True, vmem_limit_bytes=8 * 2**20
+        ),
+        name="gather_weights",
+    )(*operands)
+
+
+def gather_plain(cells, embed, decoder, *own):
+    quarter = device_index() % GROUP
+    total = device_total() // GROUP
+    groups = same_quarter()
+
+    def table(values):
+        block = jnp.stack(by_quarter(group_exchange(values, quarter), quarter))
+        return lax.all_gather(block, "dp", axis_index_groups=groups, axis=0, tiled=False)
+
+    cells_all = jnp.stack(group_exchange(cells, quarter))
+    return [cells_all, table(embed), table(decoder)] + [
+        lax.all_gather(v, AXES, axis=0, tiled=False) for v in own
+    ]
 
 
 def shards(
@@ -334,13 +517,7 @@
         components[:, None] == jnp.arange(prior_mean.shape[0], dtype=jnp.int32)[None, :]
     ).astype(jnp.float32)
 
-    cells_group = jnp.stack(group_exchange(gene_chunks(cells), quarter)).reshape(
-        GROUP * row_count, CHUNK
-    )
     live_group = group_gather(live_mask).reshape(-1).astype(jnp.float32)
-    both = gene_chunks(jnp.concatenate([embed_weight, decoder_weight]))
-    both = jnp.stack(by_quarter(group_exchange(both, quarter), quarter))
-    embed_cols = ring_gather(both[:, :rows].reshape(GROUP * rows, CHUNK)).reshape(-1, CHUNK)
     small = jnp.concatenate(
         [
             up_bias.reshape(rows, 4),
@@ -358,34 +535,23 @@
     )
     small_columns = small.shape[1]
     small = jnp.pad(small, ((0, 0), (0, 128 - small_columns)))
-    first_unit = jnp.concatenate([query_key_value, output_weight, encoder_weight, small], axis=1)
-    second_unit = jnp.concatenate(
-        [
-            up_weight,
-            down_weight.reshape(4, rows, D).transpose(1, 0, 2).reshape(rows, 4 * D),
-        ],
-        axis=1,
-    )
-    width = first_unit.shape[1]
-    pair = jnp.concatenate([first_unit, swap(first_unit, 2)])
-    ringed = ring_gather(pair).reshape(total, 2, rows, width)
-    other = swap(ringed, 1)
-    first_pieces = [ringed[:, 0], other[:, 0], ringed[:, 1], other[:, 1]]
-    ringed = ring_gather(second_unit)
-    pair = jnp.stack([ringed, swap(ringed, 2)])
-    other = swap(pair, 1)
-    second_pieces = [pair[0], other[0], pair[1], other[1]]
-    decoder_cols = ring_gather(both[:, rows:].reshape(GROUP * thin, CHUNK)).reshape(-1, CHUNK)
-
-    joint_full = place_rows(first_pieces, (0, 3 * D), quarter)
-    output_full = place_rows(first_pieces, (3 * D, 4 * D), quarter)
-    encoder_full = place_rows(first_pieces, (4 * D, 5 * D), quarter)
-    small_full = place_rows(first_pieces, (5 * D, 5 * D + 128), quarter)
-    up_full = place_rows(second_pieces, (0, 4 * D), quarter)
-    down_full = place_rows(second_pieces, (4 * D, 8 * D), quarter)
-    down_full = (
-        down_full.reshape(devices, rows, 4, D).transpose(0, 2, 1, 3).reshape(4 * devices * rows, D)
-    )
+    gather = gather_weights if total <= NARROW else gather_plain
+    cells_group, embed_cols, decoder_cols, *middle = gather(
+        gene_chunks(cells),
+        gene_chunks(embed_weight),
+        gene_chunks(decoder_weight),
+        query_key_value,
+        small,
+        output_weight,
+        encoder_weight,
+        up_weight,
+        down_weight,
+    )
+    cells_group = cells_group.reshape(GROUP * row_count, CHUNK)
+    embed_cols = embed_cols.reshape(-1, CHUNK)
+    decoder_cols = decoder_cols.reshape(-1, CHUNK)
+    middle = [full.reshape(-1, full.shape[-1]) for full in middle]
+    joint_full, small_full, output_full, encoder_full, up_full, down_full = middle
     small_full = wide(small_full)
     up_bias_full = small_full[:, 0:4].reshape(-1)
     down_bias_full = small_full[:, 4]
@@ -403,10 +569,8 @@
     prior_logvar_full = prior_full(small_full[:, 18:26])
     count = jnp.sum(small_full.reshape(devices, rows, 128)[:, 0, 26])
 
-    feature_order = block_order(GROUP * rows)
-    latent_order = block_order(GROUP * thin)
     embedded = low(across(cells_group, embed_cols))
-    embedded = low(across(embedded, feature_order)).reshape(GROUP, row_count, D)
+    embedded = embedded.reshape(GROUP, row_count, D)
     embedded = group_scatter(embedded)
     start_state = embedded + positions(coordinates)
     normed_first = layer_norm(start_state, gain_first, shift_first).astype(jnp.bfloat16)
@@ -423,7 +587,6 @@
     latent_logvar = encoded[:, LATENT:]
     latent = (latent_mean + jnp.exp(0.5 * latent_logvar) * noise).astype(jnp.bfloat16)
     latent_group = group_gather(latent).reshape(GROUP * row_count, LATENT)
-    latent_group = low(matmul(latent_group, latent_order))
 
     center = jnp.dot(onehot, prior_mean_full, precision=lax.Precision.HIGHEST)
     scale = jnp.dot(onehot, prior_logvar_full, precision=lax.Precision.HIGHEST)
@@ -441,9 +604,9 @@
     ratio = cell_total / count
     recon_grad = low(ratio * live_group[:, None] * miss)
     decoder_term = low(contract_rows(latent_group, recon_grad))
-    decoder_block = low(ring_scatter(decoder_term.reshape(total, GROUP * thin, CHUNK)))
+    decoder_block = low(ring_scatter(by_ring(decoder_term.reshape(total, GROUP * thin, CHUNK))))
     latent_grad = low(across(recon_grad, decoder_cols))
-    latent_grad = low(across(latent_grad, latent_order)).reshape(GROUP, row_count, LATENT)
+    latent_grad = latent_grad.reshape(GROUP, row_count, LATENT)
     latent_grad = wide(low(group_scatter(latent_grad)))
 
     kl_scale = ratio * ramp_weight * jax.nn.sigmoid(shifted)[None, :] * live[:, None]
@@ -498,9 +661,8 @@
     start_grad = middle_grad + start_part
     start_low = start_grad.astype(jnp.bfloat16)
     start_group = group_gather(start_low).reshape(GROUP * row_count, D)
-    start_group = low(matmul(start_group, feature_order))
     embed_term = low(contract_rows(start_group, cells_group))
-    embed_block = low(ring_scatter(embed_term.reshape(total, GROUP * rows, CHUNK)))
+    embed_block = low(ring_scatter(by_ring(embed_term.reshape(total, GROUP * rows, CHUNK))))
     cells_half = low(matmul(start_group, embed_cols) - wide(recon_grad))
 
     def to_owners(blocks):

time: 1070 us -> 898 us (0.84)
  Pallas kernels: 0 us -> 230 us
  waiting for transfers between devices: 402 us -> 249 us
  local copies, waits for them, and re-layouts: 230 us -> 97.5 us
  starting transfers between devices: 187 us -> 95.6 us
  other arithmetic: 119 us -> 93.5 us
    pallas_call x0 -> x1, Pallas kernels: none -> 230 us  [gather_weights(): pl.pallas_call(functools.partial(gather_kernel, total), out_shape=[jax.Sh...]
    ppermute x47 -> x37, waiting for transfers between devices: 150 us -> 37.7 us  [swap(): lax.ppermute(values, AXES, [(i, i ^ mask) for i in range(device_total())])]
    dynamic_update_slice x134 -> x0, local copies, waits for them, and re-layouts: 92.7 us -> none  [place_rows(): lax.dynamic_update_slice(full, pieces[m][s, :, low_col:high_col][None, No...]
    ppermute x126 -> x70, starting transfers between devices: 152 us -> 66.3 us  [shift(): return lax.ppermute(values, AXES, pairs)]
    ppermute x126 -> x70, waiting for transfers between devices: 252 us -> 211 us  [shift(): return lax.ppermute(values, AXES, pairs)]
    another operation x8 -> x0, local copies, waits for them, and re-layouts: 33.9 us -> none  [the longest x1 14.5 us: shards(): down_full.reshape(devices, rows, 4, D).transpose(0, 2, 1, 3)]
    unnamed x25 -> x5, other arithmetic: 18.2 us -> 0.01 us
    another operation x20 -> x4, other arithmetic: 22.6 us -> 4.88 us  [the longest x10 8.82 us: ring_gather(): jnp.stack([jnp.concatenate([tops[s], bottoms[(total - s) % total]]) for s...]
  transfers between devices with their start and end apart: 173 -> 107, of which waited for: 101 -> 63; matrix products, arithmetic and copies ran while one was open for 39% -> 29% of each run, Pallas kernels for 0% -> 26%
where the time goes in v2:
time: 898 us; the launch traced here: 886 us
  waiting for transfers between devices  249 us (28%)
  Pallas kernels  230 us (26%)
  local copies, waits for them, and re-layouts  97.5 us (11%)
  starting transfers between devices  95.6 us (11%)
  other arithmetic  93.5 us (10%)
  matrix products  90.2 us (10%)
  between operations  29.6 us (3%)
    pallas_call x1, Pallas kernels, gather_weights(): pl.pallas_call(functools.partial(gather_kernel, total), out_shape=[jax.Sh...  230 us
    ppermute x70, waiting for transfers between devices, shift(): return lax.ppermute(values, AXES, pairs)  211 us
    ppermute x70, starting transfers between devices, shift(): return lax.ppermute(values, AXES, pairs)  66.3 us
    convert_element_type x55, other arithmetic, low(): return values.astype(jnp.bfloat16)  39.2 us
    ppermute x37, waiting for transfers between devices, swap(): lax.ppermute(values, AXES, [(i, i ^ mask) for i in range(device_total())])  37.7 us
    ppermute x37, starting transfers between devices, swap(): lax.ppermute(values, AXES, [(i, i ^ mask) for i in range(device_total())])  29.3 us
    unnamed x251, local copies, waits for them, and re-layouts  28.2 us
    dot_general x7, matrix products, across(): lax.dot_general(left, right, (((1,), (1,)), ((), ())), preferred_element_...  27.3 us
  transfers between devices with their start and end apart: 107, of which 63 were waited for; matrix products, arithmetic and copies ran while one was open for 29% of the time, Pallas kernels for 26%

profile of v2, /device:TPU:0, one launch (start us, length us, event | category | flops | bytes accessed | tf_op | source)
XLA Modules:
  0.0 885.5 jit_solution(14101019360918194235)
XLA Ops:
  26.9 230.3 %gather_weights.1 = (bf16[4,128,3456]{2,1,0:T(8,128)(2,1)S(1)}, bf16[8,4,32,3456]{3,2,1,0:T(8,128)(2,1)S(1)}, bf16[8,4,16,3456]{3,2,1,0:T(8,128)(2,1)S(1)}, bf16...) custom-call(bf16[4,128,3456]{2,1,0:T(8,128)(2,1)S(1)} %pad_maximum_f, ...), custom_call_target="tpu_custom_call" | custom-call | tf_op jit(solution)/shard_map/gather_weights/pallas_call | solution.py:445
  265.7 8.7 convolution_convert_fusion.7
  323.8 5.3 convolution_add_fusion
  378.0 5.7 multiply_convert_fusion
  415.4 8.2 convert_reduce_fusion
  444.9 5.8 convolution_convert_fusion.1
  450.8 5.8 convolution_convert_fusion
  458.7 10.3 %fusion.4 = (bf16[8,2,1,160,1024]{4,3,2,1,0:T(8,128)(2,1)}, bf16[8,2,1,160,1024]{4,3,2,1,0:T(8,128)(2,1)}) fusion(s32[]{:T(128)S(6)} %select_n.684, bf16[8,2,2,128,1024]{4,3,2,1,0:T(8,128)(2,1)} %bitcast.688, bf16[8,2,2,32,1024]{4,3,2,1,0:T(8,128)(2,1)S(1)} %bitcast.709, s32[]{:T(128)S(6)} %select_n.685), kind=kLoop, calls=%fused_computation.21 | loop fusion | flops 20971520 | bytes 20971528 | tf_op jit(solution)/shard_map/concatenate | solution.py:631
  472.1 7.7 pad_maximum_fusion
  487.2 6.4 constant_dynamic-slice_fusion.4
  505.5 5.3 collective-permute-done.39
  526.7 7.2 subtract_convert_fusion
  537.6 5.3 bitcast_convert_fusion
  546.0 6.3 collective-permute-done.46
  552.9 11.1 %collective-permute-done.23 = bf16[64,3456]{1,0:T(8,128)(2,1)S(1)} collective-permute-done((bf16[64,3456]{1,0:T(8,128)(2,1)S(1)}, bf16[64,3456]{1,0:T(8,128)(2,1)S(1)}, u32[]{:S(2)}, u32[]{:S(2)}) %collective-permute-start.23) | collective-permute-done | bytes 442400 | tf_op jit(solution)/shard_map/ppermute | solution.py:150
  571.4 9.8 %collective-permute-done.24 = bf16[64,3456]{1,0:T(8,128)(2,1)S(1)} collective-permute-done((bf16[64,3456]{1,0:T(8,128)(2,1)S(1)}, bf16[64,3456]{1,0:T(8,128)(2,1)S(1)}, u32[]{:S(2)}, u32[]{:S(2)}) %collective-permute-start.24) | collective-permute-done | bytes 442400 | tf_op jit(solution)/shard_map/ppermute | solution.py:150
  588.3 5.9 copy.179
  594.2 6.8 collective-permute-done.25
  602.7 5.0 collective-permute-done.48
  608.4 9.8 %collective-permute-done.26 = bf16[64,3456]{1,0:T(8,128)(2,1)S(1)} collective-permute-done((bf16[64,3456]{1,0:T(8,128)(2,1)S(1)}, bf16[64,3456]{1,0:T(8,128)(2,1)S(1)}, u32[]{:S(2)}, u32[]{:S(2)}) %collective-permute-start.26) | collective-permute-done | bytes 442400 | tf_op jit(solution)/shard_map/ppermute | solution.py:150
  624.7 7.7 collective-permute-done.27
  634.5 5.1 collective-permute-done.50
  644.4 6.3 collective-permute-done.28
  654.9 10.2 %collective-permute-done.31 = bf16[64,3456]{1,0:T(8,128)(2,1)S(1)} collective-permute-done((bf16[64,3456]{1,0:T(8,128)(2,1)S(1)}, bf16[64,3456]{1,0:T(8,128)(2,1)S(1)}, u32[]{:S(2)}, u32[]{:S(2)}) %collective-permute-start.31) | collective-permute-done | bytes 442400 | tf_op jit(solution)/shard_map/ppermute | solution.py:150
  666.6 5.0 fusion.2
  703.6 5.4 collective-permute-done.33
  712.4 5.9 collective-permute-done.65
  720.2 7.3 collective-permute-done.34
  728.8 6.2 collective-permute-done.66
  739.1 5.2 fusion
  759.8 5.2 collective-permute-done.36
  769.3 22.6 %collective-permute-done.69 = bf16[32,4096]{1,0:T(8,128)(2,1)S(1)} collective-permute-done((bf16[32,4096]{1,0:T(8,128)(2,1)S(1)}, bf16[32,4096]{1,0:T(8,128)(2,1)S(1)}, u32[]{:S(2)}, u32[]{:S(2)}) %collective-permute-start.69) | collective-permute-done | bytes 262176 | tf_op jit(solution)/shard_map/ppermute | solution.py:133
  (687 shorter events, 397.2 us)
Async XLA Ops:
  0.7 333.6 %collective-permute-start = (s32[1,128]{1,0:T(1,128)}, s32[1,128]{1,0:T(1,128)}, u32[]{:S(2)}, u32[]{:S(2)}) collective-permute-start(s32[1,128]{1,0:T(1,128)} %param.106), channel_id=1, source_target_pairs={{0,2},{1,3},{2,0},{3,1},{4,6},{5,7},{6,4},{7,5},{8,10},{9,11},{10,... | collective-permute-start | bytes 1544 | tf_op jit(solution)/shard_map/ppermute | solution.py:133
  281.8 30.5 %collective-permute-start.3 = (bf16[128,1024]{1,0:T(8,128)(2,1)}, bf16[128,1024]{1,0:T(8,128)(2,1)}, u32[]{:S(2)}, u32[]{:S(2)}) collective-permute-start(bf16[128,1024]{1,0:T(8,128)(2,1)} %fusion.99), channel_id=1, source_target_pairs={{0,2},{1,3},{2,0},{3,1},{4,6},{5,7},{6,4},{7,5},{8,10},{9,11},{10,... | collective-permute-start | bytes 786440 | tf_op jit(solution)/shard_map/ppermute | solution.py:133
  362.5 13.5 %collective-permute-start.5 = (bf16[2,128,512]{2,1,0:T(8,128)(2,1)}, bf16[2,128,512]{2,1,0:T(8,128)(2,1)}, u32[]{:S(2)}, u32[]{:S(2)}) collective-permute-start(bf16[2,128,512]{2,1,0:T(8,128)(2,1)} %pad_maximum_fusion.24), channel_id=1, source_target_pairs={{0,1},{1,0},{2,3},{3,2},{4,5},{5,4},{6,7},{7,6},{8,9},{9,8},{10,11... | collective-permute-start | bytes 786440 | tf_op jit(solution)/shard_map/ppermute | solution.py:133
  403.0 131.1 %collective-permute-start.44 = (bf16[32,3456]{1,0:T(8,128)(2,1)}, bf16[32,3456]{1,0:T(8,128)(2,1)}, u32[]{:S(2)}, u32[]{:S(2)}) collective-permute-start(bf16[32,3456]{1,0:T(8,128)(2,1)} %get-tuple-element.109), channel_id=1, source_target_pairs={{0,4},{1,5},{2,6},{3,7},{8,0},{9,1},{10,2},{11,3},{16,8},{17,9},{1... | collective-permute-start | bytes 663560 | tf_op jit(solution)/shard_map/ppermute | solution.py:150
  410.0 89.4 %collective-permute-start.38 = (bf16[32,3456]{1,0:T(8,128)(2,1)}, bf16[32,3456]{1,0:T(8,128)(2,1)}, u32[]{:S(2)}, u32[]{:S(2)}) collective-permute-start(bf16[32,3456]{1,0:T(8,128)(2,1)} %fusion.68), channel_id=1, source_target_pairs={{0,8},{1,9},{2,10},{3,11},{8,16},{9,17},{10,18},{11,19},{16,24},{1... | collective-permute-start | bytes 663560 | tf_op jit(solution)/shard_map/ppermute | solution.py:150
  458.6 11.9 %collective-permute-start.86 = (f32[1,16,832]{2,0,1:T(1,128)S(1)}, f32[1,16,832]{2,0,1:T(1,128)S(1)}, u32[]{:S(2)}, u32[]{:S(2)}) collective-permute-start(f32[1,16,832]{2,0,1:T(1,128)S(1)} %dynamic-slice_bitcast_fusion.76), channel_id=1, source_target_pairs={{0,1},{1,0},{2,3},{3,2},{4,5},{5,4},{6,7},{7,6},{8,9},{9,8},{10,11... | collective-permute-start | bytes 159752 | tf_op jit(solution)/shard_map/ppermute | solution.py:133
  469.9 49.7 %collective-permute-start.18 = (bf16[128,1024]{1,0:T(8,128)(2,1)}, bf16[128,1024]{1,0:T(8,128)(2,1)}, u32[]{:S(2)}, u32[]{:S(2)}) collective-permute-start(bf16[128,1024]{1,0:T(8,128)(2,1)} %add_convert_fusion), channel_id=1, source_target_pairs={{0,2},{1,3},{2,0},{3,1},{4,6},{5,7},{6,4},{7,5},{8,10},{9,11},{10,... | collective-permute-start | bytes 786440 | tf_op jit(solution)/shard_map/ppermute | solution.py:133
  485.6 181.0 %collective-permute-start.54 = (bf16[8,2,32,4096]{3,2,1,0:T(8,128)(2,1)}, bf16[8,2,32,4096]{3,2,1,0:T(8,128)(2,1)}, u32[]{:S(2)}, u32[]{:S(2)}) collective-permute-start(bf16[8,2,32,4096]{3,2,1,0:T(8,128)(2,1)} %dynamic-slice_bitcast_fusion), channel_id=1, source_target_pairs={{0,1},{1,0},{2,3},{3,2},{4,5},{5,4},{6,7},{7,6},{8,9},{9,8},{10,11... | collective-permute-start | bytes 12582920 | tf_op jit(solution)/shard_map/ppermute | solution.py:133
  485.7 13.5 %collective-permute-start.89 = (f32[1,2,832]{2,1,0:T(2,128)S(1)}, f32[1,2,832]{2,1,0:T(2,128)S(1)}, u32[]{:S(2)}, u32[]{:S(2)}) collective-permute-start(f32[1,2,832]{2,1,0:T(2,128)S(1)} %bitcast.780), channel_id=1, source_target_pairs={{0,8},{1,9},{2,10},{3,11},{4,12},{5,13},{6,14},{7,15},{8,0},{9,1},... | collective-permute-start | bytes 19976 | tf_op jit(solution)/shard_map/ppermute | solution.py:133
  499.1 174.7 %collective-permute-start.70 = (bf16[8,2,32,4096]{3,2,0,1:T(8,128)(2,1)}, bf16[8,2,32,4096]{3,2,0,1:T(8,128)(2,1)}, u32[]{:S(2)}, u32[]{:S(2)}) collective-permute-start(bf16[8,2,32,4096]{3,2,0,1:T(8,128)(2,1)} %bitcast.659), channel_id=1, source_target_pairs={{0,1},{1,0},{2,3},{3,2},{4,5},{5,4},{6,7},{7,6},{8,9},{9,8},{10,11... | collective-permute-start | bytes 12582920 | tf_op jit(solution)/shard_map/ppermute | solution.py:133
  542.9 39.1 %collective-permute-start.22 = (bf16[128,3456]{1,0:T(8,128)(2,1)S(1)}, bf16[128,3456]{1,0:T(8,128)(2,1)S(1)}, u32[]{:S(2)}, u32[]{:S(2)}) collective-permute-start(bf16[128,3456]{1,0:T(8,128)(2,1)S(1)} %get-tuple-element.115), channel_id=1, source_target_pairs={{0,3},{1,2},{2,1},{3,0},{4,7},{5,6},{6,5},{7,4},{8,11},{9,10},{10,... | collective-permute-start | bytes 2654216 | tf_op jit(solution)/shard_map/ppermute | solution.py:133
  543.0 40.7 %collective-permute-start.21 = (bf16[128,3456]{1,0:T(8,128)(2,1)S(1)}, bf16[128,3456]{1,0:T(8,128)(2,1)S(1)}, u32[]{:S(2)}, u32[]{:S(2)}) collective-permute-start(bf16[128,3456]{1,0:T(8,128)(2,1)S(1)} %get-tuple-element.116), channel_id=1, source_target_pairs={{0,2},{1,3},{2,0},{3,1},{4,6},{5,7},{6,4},{7,5},{8,10},{9,11},{10,... | collective-permute-start | bytes 2654216 | tf_op jit(solution)/shard_map/ppermute | solution.py:133
  552.3 11.7 %collective-permute-start.23 = (bf16[64,3456]{1,0:T(8,128)(2,1)S(1)}, bf16[64,3456]{1,0:T(8,128)(2,1)S(1)}, u32[]{:S(2)}, u32[]{:S(2)}) collective-permute-start(bf16[64,3456]{1,0:T(8,128)(2,1)S(1)} %get-tuple-element.84), channel_id=1, source_target_pairs={{0,8},{1,9},{2,10},{3,11},{8,16},{9,17},{10,18},{11,19},{16,24},{1... | collective-permute-start | bytes 1327112 | tf_op jit(solution)/shard_map/ppermute | solution.py:150
  570.1 11.0 %collective-permute-start.24 = (bf16[64,3456]{1,0:T(8,128)(2,1)S(1)}, bf16[64,3456]{1,0:T(8,128)(2,1)S(1)}, u32[]{:S(2)}, u32[]{:S(2)}) collective-permute-start(bf16[64,3456]{1,0:T(8,128)(2,1)S(1)} %fusion.35), channel_id=1, source_target_pairs={{0,8},{1,9},{2,10},{3,11},{8,16},{9,17},{10,18},{11,19},{16,24},{1... | collective-permute-start | bytes 1327112 | tf_op jit(solution)/shard_map/ppermute | solution.py:150
  582.0 157.1 %collective-permute-start.91 = (bf16[8,2,160,1024]{3,2,0,1:T(8,128)(2,1)}, bf16[8,2,160,1024]{3,2,0,1:T(8,128)(2,1)}, u32[]{:S(2)}, u32[]{:S(2)}) collective-permute-start(bf16[8,2,160,1024]{3,2,0,1:T(8,128)(2,1)} %bitcast.658), channel_id=1, source_target_pairs={{0,1},{1,0},{2,3},{3,2},{4,5},{5,4},{6,7},{7,6},{8,9},{9,8},{10,11... | collective-permute-start | bytes 15728648 | tf_op jit(solution)/shard_map/ppermute | solution.py:133
  583.7 50.2 %collective-permute-start.43 = (bf16[32,3456]{1,0:T(8,128)(2,1)}, bf16[32,3456]{1,0:T(8,128)(2,1)}, u32[]{:S(2)}, u32[]{:S(2)}) collective-permute-start(bf16[32,3456]{1,0:T(8,128)(2,1)} %get-tuple-element.106), channel_id=1, source_target_pairs={{0,8},{1,9},{2,10},{3,11},{8,16},{9,17},{10,18},{11,19},{16,24},{1... | collective-permute-start | bytes 663560 | tf_op jit(solution)/shard_map/ppermute | solution.py:150
  584.2 16.7 %collective-permute-start.25 = (bf16[64,3456]{1,0:T(8,128)(2,1)}, bf16[64,3456]{1,0:T(8,128)(2,1)}, u32[]{:S(2)}, u32[]{:S(2)}) collective-permute-start(bf16[64,3456]{1,0:T(8,128)(2,1)} %fusion.34), channel_id=1, source_target_pairs={{0,8},{1,9},{2,10},{3,11},{8,16},{9,17},{10,18},{11,19},{16,24},{1... | collective-permute-start | bytes 1327112 | tf_op jit(solution)/shard_map/ppermute | solution.py:150
  639.6 11.0 %collective-permute-start.28 = (bf16[64,3456]{1,0:T(8,128)(2,1)S(1)}, bf16[64,3456]{1,0:T(8,128)(2,1)S(1)}, u32[]{:S(2)}, u32[]{:S(2)}) collective-permute-start(bf16[64,3456]{1,0:T(8,128)(2,1)S(1)} %fusion.31), channel_id=1, source_target_pairs={{0,8},{1,9},{2,10},{3,11},{8,16},{9,17},{10,18},{11,19},{16,24},{1... | collective-permute-start | bytes 1327112 | tf_op jit(solution)/shard_map/ppermute | solution.py:150
  652.8 12.3 %collective-permute-start.31 = (bf16[64,3456]{1,0:T(8,128)(2,1)S(1)}, bf16[64,3456]{1,0:T(8,128)(2,1)S(1)}, u32[]{:S(2)}, u32[]{:S(2)}) collective-permute-start(bf16[64,3456]{1,0:T(8,128)(2,1)S(1)} %get-tuple-element.83), channel_id=1, source_target_pairs={{0,4},{1,5},{2,6},{3,7},{8,0},{9,1},{10,2},{11,3},{16,8},{17,9},{1... | collective-permute-start | bytes 1327112 | tf_op jit(solution)/shard_map/ppermute | solution.py:150
  653.0 106.8 %collective-permute-start.29 = (bf16[64,3456]{1,0:T(8,128)(2,1)}, bf16[64,3456]{1,0:T(8,128)(2,1)S(1)}, u32[]{:S(2)}, u32[]{:S(2)}) collective-permute-start(bf16[64,3456]{1,0:T(8,128)(2,1)} %get-tuple-element.82), channel_id=1, source_target_pairs={{0,8},{1,9},{2,10},{3,11},{8,16},{9,17},{10,18},{11,19},{16,24},{1... | collective-permute-start | bytes 1327112 | tf_op jit(solution)/shard_map/ppermute | solution.py:150
  666.2 27.3 %collective-permute-start.32 = (bf16[64,3456]{1,0:T(8,128)(2,1)S(1)}, bf16[64,3456]{1,0:T(8,128)(2,1)S(1)}, u32[]{:S(2)}, u32[]{:S(2)}) collective-permute-start(bf16[64,3456]{1,0:T(8,128)(2,1)S(1)} %fusion.27), channel_id=1, source_target_pairs={{0,4},{1,5},{2,6},{3,7},{8,0},{9,1},{10,2},{11,3},{16,8},{17,9},{1... | collective-permute-start | bytes 1327112 | tf_op jit(solution)/shard_map/ppermute | solution.py:150
  691.4 75.4 %collective-permute-start.71 = (bf16[8,32,4096]{2,1,0:T(8,128)(2,1)}, bf16[8,32,4096]{2,1,0:T(8,128)(2,1)S(1)}, u32[]{:S(2)}, u32[]{:S(2)}) collective-permute-start(bf16[8,32,4096]{2,1,0:T(8,128)(2,1)} %dynamic-slice_bitcast_fusion.2), channel_id=1, source_target_pairs={{0,2},{1,3},{2,0},{3,1},{4,6},{5,7},{6,4},{7,5},{8,10},{9,11},{10,... | collective-permute-start | bytes 6291464 | tf_op jit(solution)/shard_map/ppermute | solution.py:133
  698.3 10.7 %collective-permute-start.33 = (bf16[64,3456]{1,0:T(8,128)(2,1)S(1)}, bf16[64,3456]{1,0:T(8,128)(2,1)S(1)}, u32[]{:S(2)}, u32[]{:S(2)}) collective-permute-start(bf16[64,3456]{1,0:T(8,128)(2,1)S(1)} %fusion.26), channel_id=1, source_target_pairs={{0,4},{1,5},{2,6},{3,7},{8,0},{9,1},{10,2},{11,3},{16,8},{17,9},{1... | collective-permute-start | bytes 1327112 | tf_op jit(solution)/shard_map/ppermute | solution.py:150
  710.2 17.3 %collective-permute-start.34 = (bf16[64,3456]{1,0:T(8,128)(2,1)S(1)}, bf16[64,3456]{1,0:T(8,128)(2,1)S(1)}, u32[]{:S(2)}, u32[]{:S(2)}) collective-permute-start(bf16[64,3456]{1,0:T(8,128)(2,1)S(1)} %fusion.25), channel_id=1, source_target_pairs={{0,4},{1,5},{2,6},{3,7},{8,0},{9,1},{10,2},{11,3},{16,8},{17,9},{1... | collective-permute-start | bytes 1327112 | tf_op jit(solution)/shard_map/ppermute | solution.py:150
  728.6 23.5 %collective-permute-start.35 = (bf16[64,3456]{1,0:T(8,128)(2,1)S(1)}, bf16[64,3456]{1,0:T(8,128)(2,1)S(1)}, u32[]{:S(2)}, u32[]{:S(2)}) collective-permute-start(bf16[64,3456]{1,0:T(8,128)(2,1)S(1)} %fusion.24), channel_id=1, source_target_pairs={{0,4},{1,5},{2,6},{3,7},{8,0},{9,1},{10,2},{11,3},{16,8},{17,9},{1... | collective-permute-start | bytes 1327112 | tf_op jit(solution)/shard_map/ppermute | solution.py:150
  744.5 57.5 %collective-permute-start.92 = (bf16[8,160,1024]{2,1,0:T(8,128)(2,1)S(1)}, bf16[8,160,1024]{2,1,0:T(8,128)(2,1)S(1)}, u32[]{:S(2)}, u32[]{:S(2)}) collective-permute-start(bf16[8,160,1024]{2,1,0:T(8,128)(2,1)S(1)} %dynamic-slice_bitcast_fusion.1), channel_id=1, source_target_pairs={{0,2},{1,3},{2,0},{3,1},{4,6},{5,7},{6,4},{7,5},{8,10},{9,11},{10,... | collective-permute-start | bytes 7864328 | tf_op jit(solution)/shard_map/ppermute | solution.py:133
  759.7 32.2 %collective-permute-start.69 = (bf16[32,4096]{1,0:T(8,128)(2,1)S(1)}, bf16[32,4096]{1,0:T(8,128)(2,1)S(1)}, u32[]{:S(2)}, u32[]{:S(2)}) collective-permute-start(bf16[32,4096]{1,0:T(8,128)(2,1)S(1)} %dynamic-slice_bitcast_fusion.27), channel_id=1, source_target_pairs={{0,2},{1,3},{2,0},{3,1},{4,6},{5,7},{6,4},{7,5},{8,10},{9,11},{10,... | collective-permute-start | bytes 786440 | tf_op jit(solution)/shard_map/ppermute | solution.py:133
  766.6 30.6 %collective-permute-start.53 = (bf16[48,3456]{1,0:T(8,128)(2,1)S(1)}, bf16[48,3456]{1,0:T(8,128)(2,1)S(1)}, u32[]{:S(2)}, u32[]{:S(2)}) collective-permute-start(bf16[48,3456]{1,0:T(8,128)(2,1)S(1)} %get-tuple-element.141), channel_id=1, source_target_pairs={{0,3},{1,2},{2,1},{3,0},{4,7},{5,6},{6,5},{7,4},{8,11},{9,10},{10,... | collective-permute-start | bytes 995336 | tf_op jit(solution)/shard_map/ppermute | solution.py:133
  766.7 32.6 %collective-permute-start.52 = (bf16[48,3456]{1,0:T(8,128)(2,1)S(1)}, bf16[48,3456]{1,0:T(8,128)(2,1)S(1)}, u32[]{:S(2)}, u32[]{:S(2)}) collective-permute-start(bf16[48,3456]{1,0:T(8,128)(2,1)S(1)} %get-tuple-element.140), channel_id=1, source_target_pairs={{0,2},{1,3},{2,0},{3,1},{4,6},{5,7},{6,4},{7,5},{8,10},{9,11},{10,... | collective-permute-start | bytes 995336 | tf_op jit(solution)/shard_map/ppermute | solution.py:133
  766.7 32.5 %collective-permute-start.51 = (bf16[48,3456]{1,0:T(8,128)(2,1)S(1)}, bf16[48,3456]{1,0:T(8,128)(2,1)S(1)}, u32[]{:S(2)}, u32[]{:S(2)}) collective-permute-start(bf16[48,3456]{1,0:T(8,128)(2,1)S(1)} %get-tuple-element.139), channel_id=1, source_target_pairs={{0,1},{1,0},{2,3},{3,2},{4,5},{5,4},{6,7},{7,6},{8,9},{9,8},{10,11... | collective-permute-start | bytes 995336 | tf_op jit(solution)/shard_map/ppermute | solution.py:133
  796.9 36.1 %collective-permute-start.79 = (bf16[16,4096]{1,0:T(8,128)(2,1)S(1)}, bf16[16,4096]{1,0:T(8,128)(2,1)S(1)}, u32[]{:S(2)}, u32[]{:S(2)}) collective-permute-start(bf16[16,4096]{1,0:T(8,128)(2,1)S(1)} %get-tuple-element.133), channel_id=1, source_target_pairs={{0,4},{1,5},{2,6},{3,7},{8,0},{9,1},{10,2},{11,3},{16,8},{17,9},{1... | collective-permute-start | bytes 393224 | tf_op jit(solution)/shard_map/ppermute | solution.py:150
  833.7 38.8 %collective-permute-start.78 = (bf16[16,4096]{1,0:T(8,128)(2,1)S(1)}, bf16[16,4096]{1,0:T(8,128)(2,1)S(1)}, u32[]{:S(2)}, u32[]{:S(2)}) collective-permute-start(bf16[16,4096]{1,0:T(8,128)(2,1)S(1)} %get-tuple-element.130), channel_id=1, source_target_pairs={{0,8},{1,9},{2,10},{3,11},{8,16},{9,17},{10,18},{11,19},{16,24},{1... | collective-permute-start | bytes 393224 | tf_op jit(solution)/shard_map/ppermute | solution.py:150
  (195 other events, 1328.4 us)

commit v3 on v2

--- a/solution.py
+++ b/solution.py
@@ -133,61 +133,12 @@
     return lax.ppermute(values, AXES, [(i, i ^ mask) for i in range(device_total())])
 
 
-def ring_order():
-    total = device_total() // GROUP
-    return list(range(0, total, 2)) + list(range(total - 1, 0, -2))
-
-
-def shift(values, step):
-    order = ring_order()
-    total = len(order)
-    pairs = []
-    for place in range(total):
-        for quarter in range(GROUP):
-            pairs.append(
-                (order[place] * GROUP + quarter, order[(place + step) % total] * GROUP + quarter)
-            )
-    return lax.ppermute(values, AXES, pairs)
-
-
-def ring_place():
-    order = ring_order()
-    inverse = [order.index(t) for t in range(len(order))]
-    return jnp.array(inverse, jnp.int32)[device_index() // GROUP]
-
-
-def ring_owner(step):
-    order = ring_order()
-    return jnp.array(order, jnp.int32)[(ring_place() - step) % len(order)]
-
-
 def same_quarter():
     return [[d for d in range(lax.axis_size("dp")) if d % 2 == odd] for odd in range(2)]
 
 
 def pick(blocks, index):
     return lax.dynamic_index_in_dim(blocks, index, 0, keepdims=False)
-
-
-def ring_scatter(blocks):
-    total = device_total() // GROUP
-    if total > NARROW:
-        full = jnp.zeros_like(blocks)
-        for s in range(total):
-            full = lax.dynamic_update_index_in_dim(full, blocks[s], ring_owner(s), 0)
-        return lax.psum_scatter(
-            full, "dp", axis_index_groups=same_quarter(), scatter_dimension=0, tiled=False
-        )
-    half = blocks.shape[1] // 2
-    top, bottom = blocks[1, :half], blocks[total - 1, half:]
-    for s in range(2, total + 1):
-        top = shift(top, 1)
-        bottom = shift(bottom, -1)
-        top = wide(top) + wide(blocks[s % total, :half])
-        bottom = wide(bottom) + wide(blocks[(total - s) % total, half:])
-        if s < total:
-            top, bottom = low(top), low(bottom)
-    return jnp.concatenate([top, bottom])
 
 
 def group_exchange(blocks, quarter):
@@ -238,28 +189,6 @@
         values = keep + swap(give, mask)
         mask *= 2
     return values[0, 0]
-
-
-def by_ring(blocks):
-    return jnp.stack([pick(blocks, ring_owner(s)) for s in range(blocks.shape[0])])
-
-
-def halves_scatter(values, rows, ring_first):
-    total = device_total() // GROUP
-    me = device_index()
-    core, side = me % 2, (me // 2) % 2
-    split = values.reshape(total, 2, 2, rows, values.shape[1])
-    keep = lax.dynamic_index_in_dim(split, core, 2, keepdims=False)
-    give = lax.dynamic_index_in_dim(split, 1 - core, 2, keepdims=False)
-    chip = low(wide(keep) + wide(swap(low(give), 1)))
-    if ring_first:
-        ringed = jnp.stack([pick(chip, ring_owner(s)) for s in range(total)])
-        pair = low(ring_scatter(ringed.reshape(total, 2 * rows, -1)).reshape(2, rows, -1))
-        return wide(pick(pair, side)) + wide(swap(pick(pair, 1 - side), 2))
-    keep = lax.dynamic_index_in_dim(chip, side, 1, keepdims=False)
-    give = lax.dynamic_index_in_dim(chip, 1 - side, 1, keepdims=False)
-    both = low(wide(keep) + wide(swap(give, 2)))
-    return wide(ring_scatter(jnp.stack([pick(both, ring_owner(s)) for s in range(total)])))
 
 
 MESH = pl.DeviceIdType.MESH
@@ -457,6 +386,245 @@
         ),
         name="gather_weights",
     )(*operands)
+
+
+def add_rows(target, first, second, dtype):
+    rows, columns = target.shape
+    step = min(rows, 16 if columns > 2048 else 32)
+
+    @pl.loop(0, rows // step)
+    def _(i):
+        part = pl.ds(pl.multiple_of(i * step, step), step)
+        target[part, :] = (wide(first[part, :]) + wide(second[part, :])).astype(dtype)
+
+
+def scatter_kernel(total, *refs):
+    (embed, decoder, joint, output, encoder, up, down, cells) = refs[:8]
+    (embed_out, decoder_out, cells_out) = refs[8:11]
+    (joint_out, output_out, encoder_out, up_out, down_out) = refs[11:16]
+    (chip_joint, chip_output, chip_encoder, chip_up, chip_down) = refs[16:21]
+    (stage_up, stage_down) = refs[21:23]
+    (sum_output, sum_encoder, sum_up, sum_down) = refs[23:27]
+    (hop_embed, hop_decoder, hop_joint) = refs[27:30]
+    (hop_output, hop_encoder, hop_up, hop_down) = refs[30:34]
+    (local_embed, local_decoder) = refs[34:36]
+    (last_embed, last_decoder, last_joint, other_joint) = refs[36:40]
+    here = Where(total)
+    copies = Copies(*refs[40:])
+    here.meet()
+    x, core, last = here.x, here.core, total - 1
+    towards = {1: here.right, -1: here.left}
+    flying = {}
+
+    tables = []
+    for term, hops, local, result in (
+        (embed, hop_embed, local_embed, last_embed),
+        (decoder, hop_decoder, local_decoder, last_decoder),
+    ):
+        for way in (1, -1):
+            tables.append((term, hops, local, result, way, 0 if way == 1 else 1))
+
+    def table_block(term, way, side, h):
+        return term.at[here.owner(way * h), pl.ds(2 * side, 2)]
+
+    def fetch(n, h):
+        term, _, local, _, way, side = tables[n]
+        flying["local", n, h] = copies.local(
+            table_block(term, way, side, h + 1), local.at[h % 2, side]
+        )
+
+    for n, (term, hops, _, _, way, side) in enumerate(tables):
+        flying["table", n] = copies.send(
+            table_block(term, way, side, 1), hops.at[0, side], towards[way]
+        )
+    halves = {}
+    for name, term, chip in (
+        ("up", up, chip_up),
+        ("down", down, chip_down),
+        ("output", output, chip_output),
+        ("encoder", encoder, chip_encoder),
+        ("joint", joint, chip_joint),
+    ):
+        halves[name] = copies.send(term.at[:, :, 1 - core], chip, here.peers[1])
+    loads = {
+        "up": copies.local(up.at[:, :, core], stage_up),
+        "down": copies.local(down.at[:, :, core], stage_down),
+    }
+    for h in (1, 2):
+        for n in range(len(tables)):
+            fetch(n, h)
+
+    def table_hop(h):
+        for n, (term, hops, local, result, way, side) in enumerate(tables):
+            flying["table", n].wait_recv()
+            flying["local", n, h].wait()
+            for row in range(2):
+                arrived = hops.at[h - 1, side, row]
+                target = arrived if h < last else result.at[2 * side + row]
+                add_rows(target, arrived, local.at[h % 2, side, row], jnp.bfloat16)
+            if h < last:
+                flying["table", n] = copies.send(
+                    hops.at[h - 1, side], hops.at[h, side], towards[way]
+                )
+            if h + 2 <= last:
+                fetch(n, h + 2)
+
+    def chip_sum(name, chip, staged):
+        halves[name].wait_recv()
+        loads[name].wait()
+
+        @pl.loop(0, total)
+        def _(t):
+            for side in range(2):
+                add_rows(chip.at[t, side], chip.at[t, side], staged.at[t, side], jnp.bfloat16)
+
+    across = {}
+
+    def cross(name, chip, sums):
+        across[name] = copies.send(chip.at[:, 1 - x], sums, here.peers[2])
+
+    chip_sum("up", chip_up, stage_up)
+    cross("up", chip_up, sum_up)
+    staged_joint = stage_up.at[:, :, :, pl.ds(0, joint.shape[-1])]
+    loads["joint"] = copies.local(joint.at[:, :, core], staged_joint)
+    chip_sum("down", chip_down, stage_down)
+    cross("down", chip_down, sum_down)
+    slim = output.shape[3]
+    staged_output = stage_down.at[:, :, pl.ds(0, slim)]
+    staged_encoder = stage_down.at[:, :, pl.ds(slim, slim)]
+    loads["output"] = copies.local(output.at[:, :, core], staged_output)
+    loads["encoder"] = copies.local(encoder.at[:, :, core], staged_encoder)
+    table_hop(1)
+    chip_sum("joint", chip_joint, staged_joint)
+    for side, way in ((0, 1), (1, -1)):
+        flying["joint", side] = copies.send(
+            chip_joint.at[here.owner(way), side], hop_joint.at[0, side], towards[way]
+        )
+    chip_sum("output", chip_output, staged_output)
+    cross("output", chip_output, sum_output)
+    chip_sum("encoder", chip_encoder, staged_encoder)
+    cross("encoder", chip_encoder, sum_encoder)
+    moves = [copies.send(cells.at[m], cells_out.at[here.quarter], here.peers[m]) for m in (2, 3, 1)]
+    own = [copies.local(cells.at[0], cells_out.at[here.quarter])]
+
+    def joint_hop(h):
+        for side, way in ((0, 1), (1, -1)):
+            flying["joint", side].wait_recv()
+            arrived = hop_joint.at[h - 1, side]
+            target = arrived if h < last else last_joint.at[side]
+            local = chip_joint.at[here.owner(way * (h + 1)), side]
+            add_rows(target, arrived, local, jnp.bfloat16)
+            if h < last:
+                flying["joint", side] = copies.send(arrived, hop_joint.at[h, side], towards[way])
+
+    late = [
+        ("up", sum_up, chip_up, hop_up, up_out, 1),
+        ("down", sum_down, chip_down, hop_down, down_out, -1),
+        ("output", sum_output, chip_output, hop_output, output_out, 1),
+        ("encoder", sum_encoder, chip_encoder, hop_encoder, encoder_out, -1),
+    ]
+
+    def late_start():
+        for name, sums, chip, hops, _, way in late:
+            across[name].wait_recv()
+
+            @pl.loop(0, total)
+            def _(t):
+                add_rows(sums.at[t], sums.at[t], chip.at[t, x], jnp.bfloat16)
+
+            flying["late", name] = copies.send(sums.at[here.owner(way)], hops.at[0], towards[way])
+
+    def late_hop(h):
+        for name, sums, _, hops, result, way in late:
+            flying["late", name].wait_recv()
+            local = sums.at[here.owner(way * (h + 1))]
+            if h < last:
+                add_rows(hops.at[h - 1], hops.at[h - 1], local, jnp.bfloat16)
+                flying["late", name] = copies.send(hops.at[h - 1], hops.at[h], towards[way])
+            else:
+                add_rows(result, hops.at[h - 1], local, jnp.float32)
+
+    joint_hop(1)
+    for h in range(2, last + 1):
+        table_hop(h)
+        joint_hop(h)
+    for result, out in ((last_embed, embed_out), (last_decoder, decoder_out)):
+        for m in (2, 3, 1):
+            moves.append(
+                copies.send(
+                    result.at[here.quarters[m]], out.at[here.quarter], here.peers[m]
+                )
+            )
+        own.append(copies.local(result.at[here.quarter], out.at[here.quarter]))
+    joint_move = copies.send(last_joint.at[1 - x], other_joint, here.peers[2])
+    late_start()
+    for h in range(1, last + 1):
+        late_hop(h)
+    joint_move.wait_recv()
+    add_rows(joint_out, last_joint.at[x], other_joint, jnp.float32)
+    for copy in moves:
+        copy.wait_recv()
+    for copy in own:
+        copy.wait()
+    copies.finish()
+
+
+def scatter_sums(embed, decoder, joint, output, encoder, up, down, cells):
+    total = device_total() // GROUP
+    last = total - 1
+    operands = [embed, decoder, joint, output, encoder, up, down, cells]
+    middle = [joint, output, encoder, up, down]
+    thin = jnp.bfloat16
+    out_shape = [jax.ShapeDtypeStruct(v.shape[1:], thin) for v in (embed, decoder)]
+    out_shape += [jax.ShapeDtypeStruct(cells.shape, thin)]
+    out_shape += [jax.ShapeDtypeStruct(v.shape[3:], jnp.float32) for v in middle]
+    chips = [(total, 2) + v.shape[3:] for v in middle]
+    sums = [(total,) + v.shape[3:] for v in middle[1:]]
+    hops = [(last, 2, 2) + v.shape[2:] for v in (embed, decoder)]
+    hops += [(last, 2) + joint.shape[3:]] + [(last,) + v.shape[3:] for v in middle[1:]]
+    local = [(2, 2, 2) + v.shape[2:] for v in (embed, decoder)]
+    results = [v.shape[1:] for v in (embed, decoder)] + [(2,) + joint.shape[3:], joint.shape[3:]]
+    buffers = chips + [chips[3], chips[4]] + sums + hops + local + results
+    remote, here = 12 + 6 * last + 4 * last + 7, 4 * last + 8
+    return pl.pallas_call(
+        functools.partial(scatter_kernel, total),
+        out_shape=out_shape,
+        in_specs=[pl.BlockSpec(memory_space=pl.ANY)] * len(operands),
+        out_specs=[pl.BlockSpec(memory_space=pl.ANY)] * 3
+        + [pl.BlockSpec(memory_space=pltpu.VMEM)] * 5,
+        scratch_shapes=[pltpu.VMEM(shape, thin) for shape in buffers]
+        + [
+            pltpu.SemaphoreType.DMA((remote,)),
+            pltpu.SemaphoreType.DMA((remote,)),
+            pltpu.SemaphoreType.DMA((here,)),
+        ],
+        compiler_params=pltpu.CompilerParams(
+            collective_id=2, has_side_effects=True, vmem_limit_bytes=60 * 2**20
+        ),
+        name="scatter_sums",
+    )(*operands)
+
+
+def scatter_plain(embed, decoder, joint, output, encoder, up, down, cells):
+    quarter = device_index() % GROUP
+
+    def sent(blocks):
+        pieces = [pick(blocks, 0)] + [swap(blocks[m], m) for m in range(1, GROUP)]
+        return jnp.stack(by_quarter(pieces, quarter))
+
+    def table(term):
+        block = lax.psum_scatter(
+            term, "dp", axis_index_groups=same_quarter(), scatter_dimension=0, tiled=False
+        )
+        return sent(jnp.stack(by_quarter(list(block), quarter)))
+
+    def middle(term):
+        rows = term.reshape((device_total(),) + term.shape[3:])
+        return wide(lax.psum_scatter(rows, AXES, scatter_dimension=0, tiled=False))
+
+    return [table(embed), table(decoder), sent(cells)] + [
+        middle(v) for v in (joint, output, encoder, up, down)
+    ]
 
 
 def gather_plain(cells, embed, decoder, *own):
@@ -604,7 +772,6 @@
     ratio = cell_total / count
     recon_grad = low(ratio * live_group[:, None] * miss)
     decoder_term = low(contract_rows(latent_group, recon_grad))
-    decoder_block = low(ring_scatter(by_ring(decoder_term.reshape(total, GROUP * thin, CHUNK))))
     latent_grad = low(across(recon_grad, decoder_cols))
     latent_grad = latent_grad.reshape(GROUP, row_count, LATENT)
     latent_grad = wide(low(group_scatter(latent_grad)))
@@ -628,20 +795,10 @@
     encoder_bias_grad = jnp.sum(encoded_grad.astype(jnp.float32), axis=0)
     down_term = low(contract_rows(active, branch_grad))
     down_bias_grad = jnp.sum(branch_grad.astype(jnp.float32), axis=0)
-    down_pack = jnp.concatenate(
-        [
-            encoder_term.reshape(devices, rows, D),
-            down_term.reshape(devices, 4 * rows, D),
-        ],
-        axis=1,
-    ).reshape(-1, D)
-    down_pack = halves_scatter(down_pack, 5 * rows, False)
-    encoder_weight_grad = down_pack[:rows]
-    down_weight_grad = down_pack[rows:]
     active_grad = across(branch_grad, down_full)
     gelu_value, gelu_back = jax.vjp(lambda value: jax.nn.gelu(value, approximate=True), pre)
     pre_grad = gelu_back(active_grad)[0].astype(jnp.bfloat16)
-    up_weight_grad = halves_scatter(low(contract_rows(normed_second, pre_grad)), rows, False)
+    up_term = low(contract_rows(normed_second, pre_grad))
     up_bias_grad = jnp.sum(pre_grad.astype(jnp.float32), axis=0)
     second_out_grad = across(pre_grad, up_full)
     norm_value, second_back = jax.vjp(layer_norm, middle_state, gain_second, shift_second)
@@ -652,9 +809,6 @@
     context_grad = across(attend_grad, output_full).astype(jnp.bfloat16)
     joint_grad = attention_backward(joint, allowed, logsum, context_grad)
     joint_term = low(contract_rows(normed_first, joint_grad))
-    joint_pack = halves_scatter(jnp.concatenate([joint_term, output_term], axis=1), rows, True)
-    joint_weight_grad = joint_pack[:, : 3 * D]
-    output_weight_grad = joint_pack[:, 3 * D :]
     first_out_grad = across(joint_grad, joint_full)
     first_value, first_back = jax.vjp(layer_norm, start_state, gain_first, shift_first)
     start_part, first_gain_grad, first_shift_grad = first_back(first_out_grad)
@@ -662,20 +816,36 @@
     start_low = start_grad.astype(jnp.bfloat16)
     start_group = group_gather(start_low).reshape(GROUP * row_count, D)
     embed_term = low(contract_rows(start_group, cells_group))
-    embed_block = low(ring_scatter(by_ring(embed_term.reshape(total, GROUP * rows, CHUNK))))
     cells_half = low(matmul(start_group, embed_cols) - wide(recon_grad))
 
-    def to_owners(blocks):
-        pieces = [blocks[0]] + [swap(blocks[m], m) for m in range(1, GROUP)]
-        return jnp.concatenate(by_quarter(pieces, quarter), axis=1)[:, :GENES]
-
-    cells_grad = to_owners(cells_half.reshape(GROUP, row_count, CHUNK))
-    embed_block = embed_block.reshape(GROUP, rows, CHUNK)
-    decoder_block = decoder_block.reshape(GROUP, thin, CHUNK)
-    blocks = jnp.concatenate([embed_block, decoder_block], axis=1)
-    blocks = [pick(blocks, quarter ^ m) for m in range(GROUP)]
-    weight_grads = wide(to_owners(jnp.stack(blocks)))
-    embed_grad, decoder_grad = weight_grads[:rows], weight_grads[rows:]
+    def by_device(term):
+        return term.reshape(total, 2, 2, term.shape[0] // devices, term.shape[1])
+
+    scatter = scatter_sums if total <= NARROW else scatter_plain
+    embed_grad, decoder_grad, cells_grad, *middle_grads = scatter(
+        embed_term.reshape(total, GROUP, rows, CHUNK),
+        decoder_term.reshape(total, GROUP, thin, CHUNK),
+        by_device(joint_term),
+        by_device(output_term),
+        by_device(encoder_term),
+        by_device(up_term),
+        by_device(down_term),
+        cells_half.reshape(GROUP, row_count, CHUNK),
+    )
+
+    def all_genes(chunks):
+        return jnp.concatenate(list(chunks), axis=1)[:, :GENES]
+
+    cells_grad = all_genes(cells_grad)
+    embed_grad = wide(all_genes(embed_grad))
+    decoder_grad = wide(all_genes(decoder_grad))
+    (
+        joint_weight_grad,
+        output_weight_grad,
+        encoder_weight_grad,
+        up_weight_grad,
+        down_weight_grad,
+    ) = middle_grads
 
     def prior_rows(values):
         return values.reshape(kinds, devices, -1).transpose(1, 0, 2).reshape(devices, -1)

time: 898 us -> 671 us (0.75)
  waiting for transfers between devices: 249 us -> 28.6 us
  Pallas kernels: 230 us -> 420 us
  starting transfers between devices: 95.6 us -> 23.8 us
  other arithmetic: 93.5 us -> 25.2 us
  local copies, waits for them, and re-layouts: 97.5 us -> 63.7 us
  between operations: 29.6 us -> 7.62 us
    ppermute x70 -> x0, waiting for transfers between devices: 211 us -> none  [shift(): return lax.ppermute(values, AXES, pairs)]
    pallas_call x0 -> x1, Pallas kernels: none -> 190 us  [scatter_sums(): pl.pallas_call(functools.partial(scatter_kernel, total), out_shape=out_sh...]
    ppermute x70 -> x0, starting transfers between devices: 66.3 us -> none  [shift(): return lax.ppermute(values, AXES, pairs)]
    convert_element_type x55 -> x0, other arithmetic: 39.2 us -> none  [low(): return values.astype(jnp.bfloat16)]
    concatenate x9 -> x1, other arithmetic: 21.8 us -> 1.87 us  [all_genes(): return jnp.concatenate(list(chunks), axis=1)[:, :GENES]]
    dynamic_slice x4 -> x0, local copies, waits for them, and re-layouts: 9.88 us -> none  [the longest x1 6.35 us: halves_scatter(): keep = lax.dynamic_index_in_dim(split, core, 2, keepdims=False)]
    ppermute x37 -> x25, waiting for transfers between devices: 37.7 us -> 28.6 us  [swap(): lax.ppermute(values, AXES, [(i, i ^ mask) for i in range(device_total())])]
    ppermute x37 -> x25, starting transfers between devices: 29.3 us -> 23.8 us  [swap(): lax.ppermute(values, AXES, [(i, i ^ mask) for i in range(device_total())])]
  transfers between devices with their start and end apart: 107 -> 25, of which waited for: 63 -> 14; matrix products, arithmetic and copies ran while one was open for 29% -> 13% of each run, Pallas kernels for 26% -> 35%
where the time goes in v3:
time: 671 us; the launch traced here: 660 us
  Pallas kernels  420 us (63%)
  matrix products  91.4 us (14%)
  local copies, waits for them, and re-layouts  63.7 us (9%)
  waiting for transfers between devices  28.6 us (4%)
  other arithmetic  25.2 us (4%)
  starting transfers between devices  23.8 us (4%)
  between operations  7.62 us (1%)
    pallas_call x1, Pallas kernels, gather_weights(): pl.pallas_call(functools.partial(gather_kernel, total), out_shape=[jax.Sh...  230 us
    pallas_call x1, Pallas kernels, scatter_sums(): pl.pallas_call(functools.partial(scatter_kernel, total), out_shape=out_sh...  190 us
    dot_general x7, matrix products, contract_rows(): lax.dot_general(left, right, (((0,), (0,)), ((), ())), preferred_element_...  34.8 us
    dot_general x7, matrix products, across(): lax.dot_general(left, right, (((1,), (1,)), ((), ())), preferred_element_...  28.8 us
    ppermute x25, waiting for transfers between devices, swap(): lax.ppermute(values, AXES, [(i, i ^ mask) for i in range(device_total())])  28.6 us
    unnamed x218, local copies, waits for them, and re-layouts  28 us
    ppermute x25, starting transfers between devices, swap(): lax.ppermute(values, AXES, [(i, i ^ mask) for i in range(device_total())])  23.8 us
    dot_general x7, matrix products, matmul(): return jnp.dot(left, right, preferred_element_type=jnp.float32)  20.1 us
  transfers between devices with their start and end apart: 25, of which 14 were waited for; matrix products, arithmetic and copies ran while one was open for 13% of the time, Pallas kernels for 35%

profile of v3, /device:TPU:0, one launch (start us, length us, event | category | flops | bytes accessed | tf_op | source)
XLA Modules:
  0.0 660.5 jit_solution(1857559280127858757)
XLA Ops:
  0.7 3.0 collective-permute-start
  5.0 5.8 copy.66
  10.7 3.2 slice_bitcast_fusion.2
  19.4 230.4 %gather_weights.1 = (bf16[4,128,3456]{2,1,0:T(8,128)(2,1)S(1)}, bf16[8,4,32,3456]{3,2,1,0:T(8,128)(2,1)S(1)}, bf16[8,4,16,3456]{3,2,1,0:T(8,128)(2,1)S(1)}, bf16...) custom-call(bf16[4,128,3456]{2,1,0:T(8,128)(2,1)S(1)} %pad_maximum_f, ...), custom_call_target="tpu_custom_call" | custom-call | tf_op jit(solution)/shard_map/gather_weights/pallas_call | solution.py:374
  249.8 3.3 copy-done
  253.1 3.3 copy-done.9
  258.2 8.7 %convolution_convert_fusion.7 = bf16[512,1024]{1,0:T(8,128)(2,1)S(1)} fusion(bf16[512,3456]{1,0:T(8,128)(2,1)} %bitcast.254, bf16[1024,3456]{1,0:T(8,128)(2,1)S(1)} %bitcast.250), kind=kOutput, calls=%fused_computation.29 | convolution fusion | flops 3624402944 | bytes 11665408 | tf_op jit(solution)/shard_map/dot_general | solution.py:44
  281.9 5.5 collective-permute-done.3
  288.9 3.9 convolution_convert_fusion.4
  298.4 5.8 convolution_add_fusion
  309.9 2.6 collective-permute-done.12
  319.7 2.5 collective-permute-start.15
  325.9 2.4 multiply_convert_fusion
  355.7 2.5 collective-permute-start.10
  361.6 6.1 convolution_convert_fusion.2
  371.9 2.6 fusion.47
  374.5 8.0 %convert_reduce_fusion = (f32[4096]{0:T(1024)}, bf16[128,4096]{1,0:T(8,128)(2,1)S(1)}) fusion(f32[128,4096]{1,0:T(8,128)S(1)} %copy-done.22, bf16[4096,1024]{1,0:T(8,128)(2,1)} %bitcast.246, f32[128,1024]{1,0:T(8,128)S(1)} %fusion.47), kind=kOutput, calls=%fused_computation.25 | convolution fusion | flops 1085403136 | bytes 12075008 | tf_op jit(solution)/shard_map/dot_general | solution.py:44
  382.6 3.6 multiply_reduce_fusion.2
  394.6 5.7 convolution_convert_fusion
  400.4 5.8 convolution_convert_fusion.1
  406.2 2.2 convolution_convert_fusion.6
  408.5 2.3 multiply_reduce_fusion.3
  410.9 4.7 convolution_convert_fusion.3
  418.8 3.1 collective-permute-done.21
  422.7 3.0 collective-permute-done.22
  427.1 2.4 collective-permute-done.23
  431.7 2.4 collective-permute-done.24
  437.0 8.3 %bitcast_convert_fusion = bf16[1024,3456]{1,0:T(8,128)(2,1)} fusion(bf16[4,128,3456]{2,1,0:T(8,128)(2,1)} %copy-done.11, bf16[1,128,1024]{2,1,0:T(8,128)(2,1)S(1)} %get-tuple-element.140, bf16[1,128,1024]{2,1,0:T(8,128)(2,1)S(1)} %bitcast.294, bf16[1,128,1024]{2,1,0:T(8,128)(2,1)S(1)} %get-tuple-element.139, bf16[1,128,1024]{2,1,0:T(8,128)(2,1)S(1)} %bitcast.274), kind=kOutput, calls=%fused_computation | convolution fusion | flops 3628990464 | bytes 11665408 | tf_op jit(solution)/shard_map/dot_general | solution.py:50
  445.3 5.5 subtract_convert_fusion
  450.8 189.8 %scatter_sums.1 = (bf16[4,32,3456]{2,1,0:T(8,128)(2,1)}, bf16[4,16,3456]{2,1,0:T(8,128)(2,1)}, bf16[4,128,3456]{2,1,0:T(8,128)(2,1)}, f32[32,3072]{1,0:T(8,128)}...) custom-call(bf16[8,4,32,3456]{3,2,1,0:T(8,128)(2,1)} %bitcast.264, ...), custom_call_target="tpu_custom_call" | custom-call | tf_op jit(solution)/shard_map/scatter_sums/pallas_call | solution.py:589
  643.0 2.2 slice_bitcast_fusion.6
  647.1 5.9 copy.90
  (401 shorter events, 106.6 us)
Async XLA Ops:
  0.7 281.2 %collective-permute-start = (s32[1,128]{1,0:T(1,128)}, s32[1,128]{1,0:T(1,128)S(1)}, u32[]{:S(2)}, u32[]{:S(2)}) collective-permute-start(s32[1,128]{1,0:T(1,128)} %param.26), channel_id=1, source_target_pairs={{0,2},{1,3},{2,0},{3,1},{4,6},{5,7},{6,4},{7,5},{8,10},{9,11},{10,... | collective-permute-start | bytes 1544 | tf_op jit(solution)/shard_map/ppermute | solution.py:133
  268.6 8.0 %collective-permute-start.2 = (bf16[2,128,1024]{2,1,0:T(8,128)(2,1)}, bf16[2,128,1024]{2,1,0:T(8,128)(2,1)}, u32[]{:S(2)}, u32[]{:S(2)}) collective-permute-start(bf16[2,128,1024]{2,1,0:T(8,128)(2,1)} %pad_maximum_fusion.10), channel_id=1, source_target_pairs={{0,1},{1,0},{2,3},{3,2},{4,5},{5,4},{6,7},{7,6},{8,9},{9,8},{10,11... | collective-permute-start | bytes 1572872 | tf_op jit(solution)/shard_map/ppermute | solution.py:133
  270.3 54.6 %copy-start.79 = (f32[128]{0:T(128)}, f32[128]{0:T(128)S(1)}, u32[]{:S(2)}) copy-start(f32[128]{0:T(128)S(1)} %convert_bitcast_fusion) | copy-start | bytes 1540
  279.0 8.4 %collective-permute-start.3 = (bf16[128,1024]{1,0:T(8,128)(2,1)S(1)}, bf16[128,1024]{1,0:T(8,128)(2,1)}, u32[]{:S(2)}, u32[]{:S(2)}) collective-permute-start(bf16[128,1024]{1,0:T(8,128)(2,1)S(1)} %fusion.32), channel_id=1, source_target_pairs={{0,2},{1,3},{2,0},{3,1},{4,6},{5,7},{6,4},{7,5},{8,10},{9,11},{10,... | collective-permute-start | bytes 786440 | tf_op jit(solution)/shard_map/ppermute | solution.py:133
  281.8 25.9 %collective-permute-start.1 = (s32[2,1,128]{2,1,0:T(1,128)S(1)}, s32[2,1,128]{2,1,0:T(1,128)S(1)}, u32[]{:S(2)}, u32[]{:S(2)}) collective-permute-start(s32[2,1,128]{2,1,0:T(1,128)S(1)} %pad_add_fusion), channel_id=1, source_target_pairs={{0,1},{1,0},{2,3},{3,2},{4,5},{5,4},{6,7},{7,6},{8,9},{9,8},{10,11... | collective-permute-start | bytes 3080 | tf_op jit(solution)/shard_map/ppermute | solution.py:133
  306.0 19.9 %copy-start.47 = (bf16[128,1024]{1,0:T(8,128)(2,1)}, bf16[128,1024]{1,0:T(8,128)(2,1)S(1)}, u32[]{:S(2)}) copy-start(bf16[128,1024]{1,0:T(8,128)(2,1)S(1)} %fusion.9) | copy-start | bytes 786436
  306.6 19.3 %copy-start.12 = (bf16[4,128,3456]{2,1,0:T(8,128)(2,1)S(1)}, bf16[4,128,3456]{2,1,0:T(8,128)(2,1)}, u32[]{:S(2)}) copy-start(bf16[4,128,3456]{2,1,0:T(8,128)(2,1)} %copy-done.11) | copy-start | bytes 10616836
  306.6 19.3 %copy-start.14 = (bf16[8,4,16,3456]{3,2,1,0:T(8,128)(2,1)S(1)}, bf16[8,4,16,3456]{3,2,1,0:T(8,128)(2,1)}, u32[]{:S(2)}) copy-start(bf16[8,4,16,3456]{3,2,1,0:T(8,128)(2,1)} %copy-done.13) | copy-start | bytes 10616836
  307.1 17.7 %copy-start.28 = (f32[128,1024]{1,0:T(8,128)}, f32[128,1024]{1,0:T(8,128)S(1)}, u32[]{:S(2)}) copy-start(f32[128,1024]{1,0:T(8,128)S(1)} %convolution_add_fusion.1) | copy-start | bytes 1572868
  307.7 31.7 %copy-start.31 = (f32[128,512]{1,0:T(8,128)}, f32[128,512]{1,0:T(8,128)S(1)}, u32[]{:S(2)}) copy-start(f32[128,512]{1,0:T(8,128)S(1)} %get-tuple-element.181) | copy-start | bytes 786436
  307.7 1.2 collective-permute-start.11
  308.9 3.6 collective-permute-start.12
  312.5 3.6 collective-permute-start.13
  313.9 8.3 %collective-permute-start.4 = (bf16[128,512]{1,0:T(8,128)(2,1)S(1)}, bf16[128,512]{1,0:T(8,128)(2,1)S(1)}, u32[]{:S(2)}, u32[]{:S(2)}) collective-permute-start(bf16[128,512]{1,0:T(8,128)(2,1)S(1)} %get-tuple-element.146), channel_id=1, source_target_pairs={{0,2},{1,3},{2,0},{3,1},{4,6},{5,7},{6,4},{7,5},{8,10},{9,11},{10,... | collective-permute-start | bytes 393224 | tf_op jit(solution)/shard_map/ppermute | solution.py:133
  316.1 3.6 collective-permute-start.14
  319.7 4.5 collective-permute-start.15
  322.2 3.6 collective-permute-start.5
  331.8 1.2 collective-permute-start.6
  333.6 3.6 collective-permute-start.7
  335.4 22.8 %collective-permute-start.16 = (bf16[2,128,512]{2,1,0:T(8,128)(2,1)}, bf16[2,128,512]{2,1,0:T(8,128)(2,1)}, u32[]{:S(2)}, u32[]{:S(2)}) collective-permute-start(bf16[2,128,512]{2,1,0:T(8,128)(2,1)} %pad_maximum_fusion.20), channel_id=1, source_target_pairs={{0,1},{1,0},{2,3},{3,2},{4,5},{5,4},{6,7},{7,6},{8,9},{9,8},{10,11... | collective-permute-start | bytes 786440 | tf_op jit(solution)/shard_map/ppermute | solution.py:133
  337.9 3.6 collective-permute-start.8
  342.0 13.1 %collective-permute-start.9 = (f32[1,128]{1,0:T(1,128)}, f32[1,128]{1,0:T(1,128)}, u32[]{:S(2)}, u32[]{:S(2)}) collective-permute-start(f32[1,128]{1,0:T(1,128)} %add.295), channel_id=1, source_target_pairs={{0,8},{1,9},{2,10},{3,11},{4,12},{5,13},{6,14},{7,15},{8,0},{9,1},... | collective-permute-start | bytes 1544 | tf_op jit(solution)/shard_map/ppermute | solution.py:133
  355.7 12.0 %collective-permute-start.10 = (f32[1,128]{1,0:T(1,128)S(1)}, f32[1,128]{1,0:T(1,128)S(1)}, u32[]{:S(2)}, u32[]{:S(2)}) collective-permute-start(f32[1,128]{1,0:T(1,128)S(1)} %add.296), channel_id=1, source_target_pairs={{0,16},{1,17},{2,18},{3,19},{4,20},{5,21},{6,22},{7,23},{8,24},{9,... | collective-permute-start | bytes 1544 | tf_op jit(solution)/shard_map/ppermute | solution.py:133
  360.1 9.5 %collective-permute-start.17 = (bf16[128,512]{1,0:T(8,128)(2,1)S(1)}, bf16[128,512]{1,0:T(8,128)(2,1)}, u32[]{:S(2)}, u32[]{:S(2)}) collective-permute-start(bf16[128,512]{1,0:T(8,128)(2,1)S(1)} %fusion.39), channel_id=1, source_target_pairs={{0,2},{1,3},{2,0},{3,1},{4,6},{5,7},{6,4},{7,5},{8,10},{9,11},{10,... | collective-permute-start | bytes 393224 | tf_op jit(solution)/shard_map/ppermute | solution.py:133
  393.6 14.9 %slice-start.2 = ((s8[6291456]{0:T(1024)(128)(4,1)}), s8[4194304]{0:T(1024)(128)(4,1)S(1)}, s32[]{:S(2)}) async-start(s8[6291456]{0:T(1024)(128)(4,1)} %bitcast.243), calls=%async_computation.2 | async-start | bytes 8388608
  416.5 1.3 collective-permute-start.20
  418.0 3.9 collective-permute-start.21
  422.0 3.8 collective-permute-start.22
  425.8 3.7 collective-permute-start.23
  426.4 7.7 %collective-permute-start.18 = (bf16[128,1024]{1,0:T(8,128)(2,1)S(1)}, bf16[128,1024]{1,0:T(8,128)(2,1)S(1)}, u32[]{:S(2)}, u32[]{:S(2)}) collective-permute-start(bf16[128,1024]{1,0:T(8,128)(2,1)S(1)} %add_convert_fusion), channel_id=1, source_target_pairs={{0,2},{1,3},{2,0},{3,1},{4,6},{5,7},{6,4},{7,5},{8,10},{9,11},{10,... | collective-permute-start | bytes 786440 | tf_op jit(solution)/shard_map/ppermute | solution.py:133
  429.5 4.6 collective-permute-start.24
  434.2 2.6 collective-permute-start.19
  (98 other events, 468.1 us)

commit v4 on v3

--- a/solution.py
+++ b/solution.py
@@ -174,21 +174,6 @@
         values = values + swap(values, mask)
         mask *= 2
     return values
-
-
-def scatter_all(values):
-    me = device_index()
-    mask = 1
-    values = values[None]
-    while mask < device_total():
-        bit = (me // mask) % 2
-        rows = values.shape[1]
-        split = values.reshape(values.shape[0], rows // 2, 2, values.shape[2])
-        keep = lax.dynamic_index_in_dim(split, bit, 2, keepdims=False)
-        give = lax.dynamic_index_in_dim(split, 1 - bit, 2, keepdims=False)
-        values = keep + swap(give, mask)
-        mask *= 2
-    return values[0, 0]
 
 
 MESH = pl.DeviceIdType.MESH
@@ -224,9 +209,17 @@
         y = place // (self.total // 2)
         return 2 * (place + y * (self.total - 1 - 2 * place)) + y
 
-    def meet(self):
+    def same(self, step):
+        t = (self.t + step) % self.total
+        return t, (2 * t + self.x, self.core)
+
+    def meet(self, everyone=False):
         barrier = pltpu.get_barrier_semaphore()
-        others = self.peers[1:] + [self.right, self.left]
+        others = self.peers[1:]
+        if everyone:
+            others = others + [self.same(step)[1] for step in range(1, self.total)]
+        else:
+            others = others + [self.right, self.left]
         for other in others:
             pl.semaphore_signal(barrier, inc=1, device_id=other, device_id_type=MESH)
         pl.semaphore_wait(barrier, len(others))
@@ -268,47 +261,52 @@
 def gather_kernel(total, *refs):
     (cells, embed, decoder, joint, small, output, encoder, up, down) = refs[:9]
     (cells_all, embed_all, decoder_all, joint_all, small_all) = refs[9:14]
-    (output_all, encoder_all, up_all, down_all) = refs[14:18]
+    (output_all, encoder_all, up_all, down_all, embedded) = refs[14:19]
+    (held_cells, held_embed, partial, other_core, for_x, other_x) = refs[19:25]
     here = Where(total)
-    copies = Copies(*refs[18:])
+    copies = Copies(*refs[25:])
     here.meet()
     t, x, core = here.t, here.x, here.core
     last = total - 1
-
-    late = [(up, up_all, 1), (output, output_all, 1), (down, down_all, -1), (encoder, encoder_all, -1)]
     towards = {1: here.right, -1: here.left}
     flying = {}
+
+    late = [(up, up_all, 1), (output, output_all, 1), (down, down_all, -1), (encoder, encoder_all, -1)]
+    shares = {
+        name: [
+            copies.send(own.at[here.quarters[m]], full.at[t, here.quarter], here.peers[m])
+            for m in (2, 3, 1)
+        ]
+        for name, own, full in (("embed", embed, embed_all), ("decoder", decoder, decoder_all))
+    }
     for n, (own, full, way) in enumerate(late):
         flying["late", n] = copies.send(own, full.at[t, x, core], towards[way])
-    shares = []
-    for m in (2, 3, 1):
-        to, chunk = here.peers[m], here.quarters[m]
-        shares.append(copies.send(embed.at[chunk], embed_all.at[t, here.quarter], to))
-        shares.append(copies.send(decoder.at[chunk], decoder_all.at[t, here.quarter], to))
-    pairs = [
+    across_x = [copies.send(own, full.at[t, x, core], here.peers[2]) for own, full, _ in late]
+    own_cells = copies.local(cells.at[here.quarter], cells_all.at[0])
+    cell_moves = [
+        copies.send(cells.at[here.quarters[m]], cells_all.at[m], here.peers[m]) for m in (2, 3, 1)
+    ]
+    shares["early"] = [
         copies.send(own, full.at[t, x, core], here.peers[2])
         for own, full in ((joint, joint_all), (small, small_all))
     ]
-    cell_moves = [
-        copies.send(cells.at[here.quarters[m]], cells_all.at[m], here.peers[m]) for m in (2, 3, 1)
-    ]
-    own_table = [
-        copies.local(embed.at[here.quarter], embed_all.at[t, here.quarter]),
-        copies.local(decoder.at[here.quarter], decoder_all.at[t, here.quarter]),
-    ]
-    own_early = [
-        copies.local(own, full.at[t, x, core])
-        for own, full in ((joint, joint_all), (small, small_all))
-    ]
+    own_copies = {
+        "embed": [copies.local(embed.at[here.quarter], embed_all.at[t, here.quarter])],
+        "decoder": [copies.local(decoder.at[here.quarter], decoder_all.at[t, here.quarter])],
+        "early": [
+            copies.local(own, full.at[t, x, core])
+            for own, full in ((joint, joint_all), (small, small_all))
+        ],
+    }
     own_late = [copies.local(own, full.at[t, x, core]) for own, full, _ in late]
-    own_cells = copies.local(cells.at[here.quarter], cells_all.at[0])
 
     def late_step(s):
         for n, (_, full, way) in enumerate(late):
             flying["late", n].wait_recv()
+            block = full.at[here.owner(way * s), x, core]
             if s < last:
-                block = full.at[here.owner(way * s), x, core]
                 flying["late", n] = copies.send(block, block, towards[way])
+            across_x.append(copies.send(block, block, here.peers[2]))
 
     def early_block(full, way, s):
         return full.at[here.owner(way * s), 0 if way == 1 else 1, core]
@@ -316,47 +314,83 @@
     def table_block(full, way, s):
         return full.at[here.owner(way * s), pl.ds(0 if way == 1 else 2, 2)]
 
-    early = [(full, way, early_block) for full in (joint_all, small_all) for way in (1, -1)]
-    tables = [(full, way, table_block) for full in (embed_all, decoder_all) for way in (1, -1)]
-
-    def step(name, items, s):
+    rings = {
+        "embed": [(embed_all, way, table_block) for way in (1, -1)],
+        "decoder": [(decoder_all, way, table_block) for way in (1, -1)],
+        "early": [(full, way, early_block) for full in (joint_all, small_all) for way in (1, -1)],
+    }
+
+    def step(name, s):
         if s == 0:
-            for copy in {"early": own_early, "table": own_table}[name]:
+            for copy in own_copies[name]:
                 copy.wait()
-            for copy in {"early": pairs, "table": shares}[name]:
+            for copy in shares[name]:
                 copy.wait_recv()
-        for n, (full, way, block_of) in enumerate(items):
+        for n, (full, way, block_of) in enumerate(rings[name]):
             if s > 0:
                 flying[name, n].wait_recv()
             if s < last:
                 block = block_of(full, way, s)
                 flying[name, n] = copies.send(block, block, towards[way])
 
-    across_x, across_core = [], []
-    for slot in range(1, last + 7):
-        if slot <= last:
-            late_step(slot)
-        if slot == last:
-            for copy in own_late:
-                copy.wait()
-            for _, full, _ in late:
-                block = full.at[:, x, core]
-                across_x.append(copies.send(block, block, here.peers[2]))
-        if 0 <= slot - 2 <= last:
-            step("early", early, slot - 2)
-        if slot - 2 == last:
-            for full in (joint_all, small_all):
-                block = full.at[:, :, core]
-                across_core.append(copies.send(block, block, here.peers[1]))
-        if 0 <= slot - 3 <= last:
-            step("table", tables, slot - 3)
-    for copy, (_, full, _) in zip(across_x, late):
+    holds = {}
+
+    def hold(block):
+        holds[block] = copies.local(embed_all.at[block], held_embed.at[block % 2])
+
+    def multiply(block):
+        holds[block].wait()
+        features = held_embed.shape[1] * held_embed.shape[2]
+        table = held_embed[block % 2].reshape(features, held_embed.shape[3])
+        for row in range(2):
+            for column in range(2):
+                partial[row, column, :, pl.ds(block * features, features)] = low(
+                    across(held_cells[2 * row + column], table)
+                )
+        if block + 2 < total:
+            hold(block + 2)
+
+    across_core = []
+    step("embed", 0)
+    for s in range(1, last + 1):
+        late_step(s)
+        step("embed", s)
+        if s == last - 1:
+            step("early", 0)
+            step("decoder", 0)
+    hold(0)
+    hold(1)
+    for copy in cell_moves:
         copy.wait_recv()
+    own_cells.wait()
+    held = copies.local(cells_all, held_cells)
+    step("early", 1)
+    step("decoder", 1)
+    held.wait()
+    for s in range(2, last + 1):
+        multiply(s - 2)
+        step("early", s)
+        step("decoder", s)
+    for block in range(last - 1, total):
+        multiply(block)
+    sums = copies.send(partial.at[:, 1], other_core, here.peers[1])
+    for copy in own_late:
+        copy.wait()
+    for full in (joint_all, small_all):
         block = full.at[:, :, core]
         across_core.append(copies.send(block, block, here.peers[1]))
-    for copy in cell_moves + across_core:
+    sums.wait_recv()
+    for_x[...] = low(wide(partial[1, 0]) + wide(other_core[1]))
+    sums = copies.send(for_x, other_x, here.peers[2])
+    for copy in across_x:
         copy.wait_recv()
-    own_cells.wait()
+    for _, full, _ in late:
+        block = full.at[:, :, core]
+        across_core.append(copies.send(block, block, here.peers[1]))
+    sums.wait_recv()
+    embedded[...] = wide(partial[0, 0]) + wide(other_core[0]) + wide(other_x[...])
+    for copy in across_core:
+        copy.wait_recv()
     copies.finish()
 
 
@@ -370,19 +404,32 @@
         + [(total,) + v.shape for v in tables]
         + [(total, 2, 2) + v.shape for v in own]
     )
-    remote = 15 + 12 * (total - 1) + 10
+    remote = 15 + 12 * (total - 1) + 4 * total + 8
+    cell_rows, genes = cells.shape[1:]
+    features = total * GROUP * embed.shape[1]
+    buffers = [
+        cells.shape,
+        (2,) + embed.shape,
+        (2, 2, cell_rows, features),
+        (2, cell_rows, features),
+        (cell_rows, features),
+        (cell_rows, features),
+    ]
     return pl.pallas_call(
         functools.partial(gather_kernel, total),
-        out_shape=[jax.ShapeDtypeStruct(s, jnp.bfloat16) for s in shapes],
+        out_shape=[jax.ShapeDtypeStruct(s, jnp.bfloat16) for s in shapes]
+        + [jax.ShapeDtypeStruct((cell_rows, features), jnp.float32)],
         in_specs=[pl.BlockSpec(memory_space=pl.ANY)] * len(operands),
-        out_specs=[pl.BlockSpec(memory_space=pl.ANY)] * len(operands),
-        scratch_shapes=[
+        out_specs=[pl.BlockSpec(memory_space=pl.ANY)] * len(operands)
+        + [pl.BlockSpec(memory_space=pltpu.VMEM)],
+        scratch_shapes=[pltpu.VMEM(shape, jnp.bfloat16) for shape in buffers]
+        + [
             pltpu.SemaphoreType.DMA((remote,)),
             pltpu.SemaphoreType.DMA((remote,)),
-            pltpu.SemaphoreType.DMA((9,)),
+            pltpu.SemaphoreType.DMA((10 + total,)),
         ],
         compiler_params=pltpu.CompilerParams(
-            collective_id=1, has_side_effects=True, vmem_limit_bytes=8 * 2**20
+            collective_id=1, has_side_effects=True, vmem_limit_bytes=32 * 2**20
         ),
         name="gather_weights",
     )(*operands)
@@ -399,18 +446,21 @@
 
 
 def scatter_kernel(total, *refs):
+    (small, recon, *refs) = refs
     (embed, decoder, joint, output, encoder, up, down, cells) = refs[:8]
     (embed_out, decoder_out, cells_out) = refs[8:11]
-    (joint_out, output_out, encoder_out, up_out, down_out) = refs[11:16]
-    (chip_joint, chip_output, chip_encoder, chip_up, chip_down) = refs[16:21]
-    (stage_up, stage_down) = refs[21:23]
-    (sum_output, sum_encoder, sum_up, sum_down) = refs[23:27]
-    (hop_embed, hop_decoder, hop_joint) = refs[27:30]
-    (hop_output, hop_encoder, hop_up, hop_down) = refs[30:34]
-    (local_embed, local_decoder) = refs[34:36]
-    (last_embed, last_decoder, last_joint, other_joint) = refs[36:40]
+    (joint_out, output_out, encoder_out, up_out, down_out, small_out, recon_out) = refs[11:18]
+    (chip_small, stage_small, sum_small, hop_small, group_recon, all_recon) = refs[18:24]
+    refs = refs[24:]
+    (chip_joint, chip_output, chip_encoder, chip_up, chip_down) = refs[:5]
+    (stage_up, stage_down) = refs[5:7]
+    (sum_output, sum_encoder, sum_up, sum_down) = refs[7:11]
+    (hop_embed, hop_decoder, hop_joint) = refs[11:14]
+    (hop_output, hop_encoder, hop_up, hop_down) = refs[14:18]
+    (local_embed, local_decoder) = refs[18:20]
+    (last_embed, last_decoder, last_joint, other_joint) = refs[20:24]
     here = Where(total)
-    copies = Copies(*refs[40:])
+    copies = Copies(*refs[24:])
     here.meet()
     x, core, last = here.x, here.core, total - 1
     towards = {1: here.right, -1: here.left}
@@ -444,9 +494,13 @@
         ("output", output, chip_output),
         ("encoder", encoder, chip_encoder),
         ("joint", joint, chip_joint),
+        ("small", small, chip_small),
     ):
         halves[name] = copies.send(term.at[:, :, 1 - core], chip, here.peers[1])
+    group_recon[here.quarter] = recon[...]
+    recons = [copies.send(recon, group_recon.at[here.quarter], here.peers[m]) for m in (2, 3, 1)]
     loads = {
+        "small": copies.local(small.at[:, :, core], stage_small),
         "up": copies.local(up.at[:, :, core], stage_up),
         "down": copies.local(down.at[:, :, core], stage_down),
     }
@@ -476,7 +530,7 @@
         @pl.loop(0, total)
         def _(t):
             for side in range(2):
-                add_rows(chip.at[t, side], chip.at[t, side], staged.at[t, side], jnp.bfloat16)
+                add_rows(chip.at[t, side], chip.at[t, side], staged.at[t, side], chip.dtype)
 
     across = {}
 
@@ -504,8 +558,21 @@
     cross("output", chip_output, sum_output)
     chip_sum("encoder", chip_encoder, staged_encoder)
     cross("encoder", chip_encoder, sum_encoder)
+    chip_sum("small", chip_small, stage_small)
+    cross("small", chip_small, sum_small)
+    for copy in recons:
+        copy.wait_recv()
+    all_recon[here.t] = group_recon[0] + group_recon[1] + group_recon[2] + group_recon[3]
+    own_recon = all_recon.at[here.t]
+    flying["recon"] = copies.send(own_recon, own_recon, here.right)
     moves = [copies.send(cells.at[m], cells_out.at[here.quarter], here.peers[m]) for m in (2, 3, 1)]
     own = [copies.local(cells.at[0], cells_out.at[here.quarter])]
+
+    def recon_hop(h):
+        flying["recon"].wait_recv()
+        if h < last:
+            arrived = all_recon.at[here.owner(h)]
+            flying["recon"] = copies.send(arrived, arrived, here.right)
 
     def joint_hop(h):
         for side, way in ((0, 1), (1, -1)):
@@ -522,6 +589,7 @@
         ("down", sum_down, chip_down, hop_down, down_out, -1),
         ("output", sum_output, chip_output, hop_output, output_out, 1),
         ("encoder", sum_encoder, chip_encoder, hop_encoder, encoder_out, -1),
+        ("small", sum_small, chip_small, hop_small, small_out, 1),
     ]
 
     def late_start():
@@ -530,7 +598,7 @@
 
             @pl.loop(0, total)
             def _(t):
-                add_rows(sums.at[t], sums.at[t], chip.at[t, x], jnp.bfloat16)
+                add_rows(sums.at[t], sums.at[t], chip.at[t, x], sums.dtype)
 
             flying["late", name] = copies.send(sums.at[here.owner(way)], hops.at[0], towards[way])
 
@@ -539,7 +607,7 @@
             flying["late", name].wait_recv()
             local = sums.at[here.owner(way * (h + 1))]
             if h < last:
-                add_rows(hops.at[h - 1], hops.at[h - 1], local, jnp.bfloat16)
+                add_rows(hops.at[h - 1], hops.at[h - 1], local, hops.dtype)
                 flying["late", name] = copies.send(hops.at[h - 1], hops.at[h], towards[way])
             else:
                 add_rows(result, hops.at[h - 1], local, jnp.float32)
@@ -560,6 +628,11 @@
     late_start()
     for h in range(1, last + 1):
         late_hop(h)
+        recon_hop(h)
+    summed = all_recon[0]
+    for t in range(1, total):
+        summed = summed + all_recon[t]
+    recon_out[...] = summed
     joint_move.wait_recv()
     add_rows(joint_out, last_joint.at[x], other_joint, jnp.float32)
     for copy in moves:
@@ -569,15 +642,19 @@
     copies.finish()
 
 
-def scatter_sums(embed, decoder, joint, output, encoder, up, down, cells):
+def scatter_sums(embed, decoder, joint, output, encoder, up, down, small, recon, cells):
     total = device_total() // GROUP
     last = total - 1
-    operands = [embed, decoder, joint, output, encoder, up, down, cells]
+    operands = [small, recon, embed, decoder, joint, output, encoder, up, down, cells]
     middle = [joint, output, encoder, up, down]
     thin = jnp.bfloat16
     out_shape = [jax.ShapeDtypeStruct(v.shape[1:], thin) for v in (embed, decoder)]
     out_shape += [jax.ShapeDtypeStruct(cells.shape, thin)]
     out_shape += [jax.ShapeDtypeStruct(v.shape[3:], jnp.float32) for v in middle]
+    out_shape += [jax.ShapeDtypeStruct(v, jnp.float32) for v in (small.shape[3:], recon.shape)]
+    block = small.shape[3:]
+    exact = [(total, 2) + block, (total, 2) + block, (total,) + block, (last,) + block]
+    exact += [(GROUP,) + recon.shape, (total,) + recon.shape]
     chips = [(total, 2) + v.shape[3:] for v in middle]
     sums = [(total,) + v.shape[3:] for v in middle[1:]]
     hops = [(last, 2, 2) + v.shape[2:] for v in (embed, decoder)]
@@ -585,14 +662,16 @@
     local = [(2, 2, 2) + v.shape[2:] for v in (embed, decoder)]
     results = [v.shape[1:] for v in (embed, decoder)] + [(2,) + joint.shape[3:], joint.shape[3:]]
     buffers = chips + [chips[3], chips[4]] + sums + hops + local + results
-    remote, here = 12 + 6 * last + 4 * last + 7, 4 * last + 8
+    remote, here = 12 + 6 * last + 4 * last + 7 + 5 + 2 * last, 4 * last + 9
     return pl.pallas_call(
         functools.partial(scatter_kernel, total),
         out_shape=out_shape,
-        in_specs=[pl.BlockSpec(memory_space=pl.ANY)] * len(operands),
+        in_specs=[pl.BlockSpec(memory_space=pl.ANY), pl.BlockSpec(memory_space=pltpu.VMEM)]
+        + [pl.BlockSpec(memory_space=pl.ANY)] * (len(operands) - 2),
         out_specs=[pl.BlockSpec(memory_space=pl.ANY)] * 3
-        + [pl.BlockSpec(memory_space=pltpu.VMEM)] * 5,
-        scratch_shapes=[pltpu.VMEM(shape, thin) for shape in buffers]
+        + [pl.BlockSpec(memory_space=pltpu.VMEM)] * 7,
+        scratch_shapes=[pltpu.VMEM(shape, jnp.float32) for shape in exact]
+        + [pltpu.VMEM(shape, thin) for shape in buffers]
         + [
             pltpu.SemaphoreType.DMA((remote,)),
             pltpu.SemaphoreType.DMA((remote,)),
@@ -605,7 +684,7 @@
     )(*operands)
 
 
-def scatter_plain(embed, decoder, joint, output, encoder, up, down, cells):
+def scatter_plain(embed, decoder, joint, output, encoder, up, down, small, recon, cells):
     quarter = device_index() % GROUP
 
     def sent(blocks):
@@ -623,8 +702,134 @@
         return wide(lax.psum_scatter(rows, AXES, scatter_dimension=0, tiled=False))
 
     return [table(embed), table(decoder), sent(cells)] + [
-        middle(v) for v in (joint, output, encoder, up, down)
+        middle(v) for v in (joint, output, encoder, up, down, small)
+    ] + [sum_all(recon)]
+
+
+SLICE = 384
+
+
+def latent_kernel(total, *refs):
+    (message, spread, ratio, decoder, cells) = refs[:5]
+    (recon_grad, decoder_term, latent_grad, spread_sum, recon_sum) = refs[5:10]
+    (latents, held_decoder, held_cells, held_grad, held_term, turned, partial) = refs[10:17]
+    (leaving, arriving, group_spread, all_spread) = refs[17:21]
+    here = Where(total)
+    copies = Copies(*refs[21:])
+    here.meet(everyone=True)
+    moves = [copies.send(message, latents.at[m], here.peers[m]) for m in (2, 3, 1)]
+    spreads = [copies.send(spread, group_spread.at[here.quarter], here.peers[m]) for m in (2, 3, 1)]
+    loads = [
+        copies.local(message, latents.at[0]),
+        copies.local(decoder, held_decoder),
+        copies.local(cells, held_cells),
     ]
+    group_spread[here.quarter] = spread[...]
+    for copy in spreads:
+        copy.wait_recv()
+    all_spread[here.t] = (
+        group_spread[0] + group_spread[1] + group_spread[2] + group_spread[3]
+    )
+    spreads = []
+    for away in range(1, total):
+        own = all_spread.at[here.t]
+        spreads.append(copies.send(own, own, here.same(away)[1]))
+    for copy in loads:
+        copy.wait()
+    for copy in moves:
+        copy.wait_recv()
+    rows = message.shape[0]
+    size = held_decoder.shape[0]
+    for m in range(GROUP):
+        turned[:, m * rows : (m + 1) * rows] = low(wide(latents[m, :, :size]).T)
+    partial[...] = jnp.zeros_like(partial)
+    recon_sum[...] = jnp.zeros_like(recon_sum)
+
+    @pl.loop(0, CHUNK // SLICE)
+    def _(i):
+        part = pl.ds(pl.multiple_of(i * SLICE, 128), SLICE)
+        table = held_decoder[:, part]
+        for m in range(GROUP):
+            live = wide(latents[m, :, size : size + 128])
+            live = jnp.concatenate([live] * (SLICE // 128), axis=1)
+            miss = matmul(latents[m, :, :size], table) - wide(held_cells[m, :, part])
+            weighted = live * miss
+            recon_sum[...] += jnp.sum((weighted * miss).reshape(rows // 8, 8, SLICE), axis=0)
+            grad = low(ratio[0, 0] * weighted)
+            held_grad[m, :, part] = grad
+            partial[m] += across(grad, table)
+        held_term[:, part] = low(matmul(turned[...], held_grad[:, :, part].reshape(GROUP * rows, SLICE)))
+
+    leaving[...] = low(partial[...])
+    moves = [copies.send(leaving.at[m], arriving.at[m - 1], here.peers[m]) for m in (2, 3, 1)]
+    stores = [copies.local(held_grad, recon_grad), copies.local(held_term, decoder_term)]
+    for copy in spreads:
+        copy.wait_recv()
+    summed = all_spread[0]
+    for t in range(1, total):
+        summed = summed + all_spread[t]
+    spread_sum[...] = summed
+    for copy in moves:
+        copy.wait_recv()
+    latent_grad[...] = (
+        (partial[0] + wide(arriving[0])) + (wide(arriving[1]) + wide(arriving[2]))
+    )
+    for copy in stores:
+        copy.wait()
+    copies.finish()
+
+
+def latent_step(message, spread, ratio, decoder, cells):
+    total = device_total() // GROUP
+    rows, size = message.shape[0], decoder.shape[0]
+    thin = jnp.bfloat16
+    vmem = pl.BlockSpec(memory_space=pltpu.VMEM)
+    anywhere = pl.BlockSpec(memory_space=pl.ANY)
+    remote = 9 + total - 1
+    return pl.pallas_call(
+        functools.partial(latent_kernel, total),
+        out_shape=[
+            jax.ShapeDtypeStruct(cells.shape, thin),
+            jax.ShapeDtypeStruct(decoder.shape, thin),
+            jax.ShapeDtypeStruct((rows, size), jnp.float32),
+            jax.ShapeDtypeStruct(spread.shape, jnp.float32),
+            jax.ShapeDtypeStruct((8, SLICE), jnp.float32),
+        ],
+        in_specs=[vmem, vmem, pl.BlockSpec(memory_space=pltpu.SMEM), anywhere, anywhere],
+        out_specs=[anywhere, anywhere, vmem, vmem, vmem],
+        scratch_shapes=[
+            pltpu.VMEM((GROUP,) + message.shape, thin),
+            pltpu.VMEM(decoder.shape, thin),
+            pltpu.VMEM(cells.shape, thin),
+            pltpu.VMEM(cells.shape, thin),
+            pltpu.VMEM(decoder.shape, thin),
+            pltpu.VMEM((size, GROUP * rows), thin),
+            pltpu.VMEM((GROUP, rows, size), jnp.float32),
+            pltpu.VMEM((GROUP, rows, size), thin),
+            pltpu.VMEM((GROUP - 1, rows, size), thin),
+            pltpu.VMEM((GROUP,) + spread.shape, jnp.float32),
+            pltpu.VMEM((total,) + spread.shape, jnp.float32),
+            pltpu.SemaphoreType.DMA((remote,)),
+            pltpu.SemaphoreType.DMA((remote,)),
+            pltpu.SemaphoreType.DMA((5,)),
+        ],
+        compiler_params=pltpu.CompilerParams(
+            collective_id=3, has_side_effects=True, vmem_limit_bytes=40 * 2**20
+        ),
+        name="latent_step",
+    )(message, spread, ratio, decoder, cells)
+
+
+def latent_plain(message, spread, ratio, decoder, cells):
+    size = decoder.shape[0]
+    gathered = group_gather(message).reshape(-1, message.shape[1])
+    latents, live = gathered[:, :size], wide(gathered[:, size : size + 1])
+    miss = matmul(latents, decoder) - wide(cells.reshape(-1, CHUNK))
+    grad = low(ratio[0, 0] * live * miss)
+    recon_sum = jnp.sum((live * miss * miss).reshape(-1, 8, CHUNK), axis=0)
+    latent_grad = group_scatter(low(across(grad, decoder)).reshape(GROUP, -1, size))
+    term = low(contract_rows(latents, grad))
+    return grad.reshape(cells.shape), term, latent_grad, sum_all(spread), recon_sum
 
 
 def gather_plain(cells, embed, decoder, *own):
@@ -637,9 +842,12 @@
         return lax.all_gather(block, "dp", axis_index_groups=groups, axis=0, tiled=False)
 
     cells_all = jnp.stack(group_exchange(cells, quarter))
-    return [cells_all, table(embed), table(decoder)] + [
-        lax.all_gather(v, AXES, axis=0, tiled=False) for v in own
-    ]
+    embed_all = table(embed)
+    rows, genes = cells.shape[1:]
+    embedded = low(across(cells_all.reshape(-1, genes), embed_all.reshape(-1, genes)))
+    embedded = group_scatter(embedded.reshape(GROUP, rows, -1))
+    middle = [lax.all_gather(v, AXES, axis=0, tiled=False) for v in own]
+    return [cells_all, embed_all, table(decoder)] + middle + [embedded]
 
 
 def shards(
@@ -685,7 +893,6 @@
         components[:, None] == jnp.arange(prior_mean.shape[0], dtype=jnp.int32)[None, :]
     ).astype(jnp.float32)
 
-    live_group = group_gather(live_mask).reshape(-1).astype(jnp.float32)
     small = jnp.concatenate(
         [
             up_bias.reshape(rows, 4),
@@ -695,8 +902,7 @@
             second_gain.reshape(rows, 1),
             second_shift.reshape(rows, 1),
             encoder_bias.reshape(rows, 1),
-            prior_mean.reshape(rows, 8),
-            prior_logvar.reshape(rows, 8),
+            jnp.concatenate([prior_mean, prior_logvar]).reshape(rows, 16),
             jnp.full((rows, 1), jnp.sum(live), jnp.bfloat16),
         ],
         axis=1,
@@ -704,7 +910,7 @@
     small_columns = small.shape[1]
     small = jnp.pad(small, ((0, 0), (0, 128 - small_columns)))
     gather = gather_weights if total <= NARROW else gather_plain
-    cells_group, embed_cols, decoder_cols, *middle = gather(
+    cells_group, embed_cols, decoder_cols, *middle, embedded = gather(
         gene_chunks(cells),
         gene_chunks(embed_weight),
         gene_chunks(decoder_weight),
@@ -715,7 +921,7 @@
         up_weight,
         down_weight,
     )
-    cells_group = cells_group.reshape(GROUP * row_count, CHUNK)
+    cells_rows = cells_group.reshape(GROUP * row_count, CHUNK)
     embed_cols = embed_cols.reshape(-1, CHUNK)
     decoder_cols = decoder_cols.reshape(-1, CHUNK)
     middle = [full.reshape(-1, full.shape[-1]) for full in middle]
@@ -730,16 +936,11 @@
     encoder_bias_full = small_full[:, 9]
     kinds = prior_mean.shape[0]
 
-    def prior_full(columns):
-        return columns.reshape(devices, kinds, -1).transpose(1, 0, 2).reshape(kinds, LATENT)
-
-    prior_mean_full = prior_full(small_full[:, 10:18])
-    prior_logvar_full = prior_full(small_full[:, 18:26])
+    prior_full = small_full[:, 10:26].reshape(devices, 2 * kinds, -1)
+    prior_full = prior_full.transpose(1, 0, 2).reshape(2 * kinds, LATENT)
+    prior_mean_full, prior_logvar_full = prior_full[:kinds], prior_full[kinds:]
     count = jnp.sum(small_full.reshape(devices, rows, 128)[:, 0, 26])
 
-    embedded = low(across(cells_group, embed_cols))
-    embedded = embedded.reshape(GROUP, row_count, D)
-    embedded = group_scatter(embedded)
     start_state = embedded + positions(coordinates)
     normed_first = layer_norm(start_state, gain_first, shift_first).astype(jnp.bfloat16)
     joint = matmul(normed_first, joint_full).astype(jnp.bfloat16)
@@ -754,27 +955,25 @@
     latent_mean = encoded[:, :LATENT]
     latent_logvar = encoded[:, LATENT:]
     latent = (latent_mean + jnp.exp(0.5 * latent_logvar) * noise).astype(jnp.bfloat16)
-    latent_group = group_gather(latent).reshape(GROUP * row_count, LATENT)
-
     center = jnp.dot(onehot, prior_mean_full, precision=lax.Precision.HIGHEST)
     scale = jnp.dot(onehot, prior_logvar_full, precision=lax.Precision.HIGHEST)
     gap = latent_mean - center
     inverse = jnp.exp(-scale)
     grown = jnp.exp(latent_logvar)
     diverge = 0.5 * (scale - latent_logvar + (grown + gap * gap) * inverse - 1.0)
-    kl_mean = sum_all(jnp.sum(live[:, None] * diverge, axis=0, keepdims=True))[0] / count
-
-    recon = matmul(latent_group, decoder_cols)
-    miss = recon - wide(cells_group)
-    recon_local = jnp.sum(live_group * (0.5 * jnp.sum(miss * miss, axis=1)))
+    ratio = cell_total / count
+    spread = jnp.broadcast_to(jnp.sum(live[:, None] * diverge, axis=0, keepdims=True), (8, LATENT))
+    message = jnp.concatenate(
+        [latent, jnp.broadcast_to(low(live)[:, None], (row_count, 128))], axis=1
+    )
+    latent_pass = latent_step if total <= NARROW else latent_plain
+    recon_grad, decoder_term, latent_grad, spread_sum, recon_sum = latent_pass(
+        message, spread, ratio.reshape(1, 1), decoder_cols, cells_group
+    )
+    kl_mean = spread_sum[0] / count
     shifted = (kl_mean - FREE_FLOOR) / FREE_TEMP
     free = FREE_FLOOR + FREE_TEMP * jax.nn.softplus(shifted)
-    ratio = cell_total / count
-    recon_grad = low(ratio * live_group[:, None] * miss)
-    decoder_term = low(contract_rows(latent_group, recon_grad))
-    latent_grad = low(across(recon_grad, decoder_cols))
-    latent_grad = latent_grad.reshape(GROUP, row_count, LATENT)
-    latent_grad = wide(low(group_scatter(latent_grad)))
+    latent_grad = wide(low(latent_grad))
 
     kl_scale = ratio * ramp_weight * jax.nn.sigmoid(shifted)[None, :] * live[:, None]
     pulled = kl_scale * gap * inverse
@@ -815,14 +1014,32 @@
     start_grad = middle_grad + start_part
     start_low = start_grad.astype(jnp.bfloat16)
     start_group = group_gather(start_low).reshape(GROUP * row_count, D)
-    embed_term = low(contract_rows(start_group, cells_group))
-    cells_half = low(matmul(start_group, embed_cols) - wide(recon_grad))
+    embed_term = low(contract_rows(start_group, cells_rows))
+    cells_half = low(
+        matmul(start_group, embed_cols) - wide(recon_grad.reshape(GROUP * row_count, CHUNK))
+    )
+
+    vectors = [
+        up_bias_grad,
+        down_bias_grad,
+        first_gain_grad,
+        first_shift_grad,
+        second_gain_grad,
+        second_shift_grad,
+        encoder_bias_grad,
+    ]
+    priors = jnp.concatenate([prior_mean_grad, prior_logvar_grad])
+    priors = priors.reshape(2 * kinds, devices, -1).transpose(1, 0, 2).reshape(devices, -1)
+    prior_size = priors.shape[1]
+    packed = jnp.concatenate([v.reshape(devices, -1) for v in vectors] + [priors], axis=1)
+    packed = jnp.pad(packed, ((0, 0), (0, 1024 - packed.shape[1])))
+    packed = packed.reshape(total, 2, 2, 8, 128)
 
     def by_device(term):
         return term.reshape(total, 2, 2, term.shape[0] // devices, term.shape[1])
 
     scatter = scatter_sums if total <= NARROW else scatter_plain
-    embed_grad, decoder_grad, cells_grad, *middle_grads = scatter(
+    embed_grad, decoder_grad, cells_grad, *middle_grads, small_sum, recon_total = scatter(
         embed_term.reshape(total, GROUP, rows, CHUNK),
         decoder_term.reshape(total, GROUP, thin, CHUNK),
         by_device(joint_term),
@@ -830,6 +1047,8 @@
         by_device(encoder_term),
         by_device(up_term),
         by_device(down_term),
+        packed,
+        recon_sum,
         cells_half.reshape(GROUP, row_count, CHUNK),
     )
 
@@ -847,32 +1066,13 @@
         down_weight_grad,
     ) = middle_grads
 
-    def prior_rows(values):
-        return values.reshape(kinds, devices, -1).transpose(1, 0, 2).reshape(devices, -1)
-
-    vectors = [
-        up_bias_grad,
-        down_bias_grad,
-        first_gain_grad,
-        first_shift_grad,
-        second_gain_grad,
-        second_shift_grad,
-        encoder_bias_grad,
-    ]
-    packed = jnp.concatenate(
-        [vector.reshape(devices, -1) for vector in vectors]
-        + [prior_rows(prior_mean_grad), prior_rows(prior_logvar_grad)],
-        axis=1,
-    )
-    packed = scatter_all(packed)
     ends = [0]
     for vector in vectors:
         ends.append(ends[-1] + vector.shape[0] // devices)
+    packed = small_sum.reshape(-1)
     vector_grads = [packed[ends[i] : ends[i + 1]] for i in range(len(vectors))]
-    prior_size = kinds * LATENT // devices
-    prior_mean_out = packed[ends[-1] : ends[-1] + prior_size].reshape(kinds, -1)
-    prior_logvar_out = packed[ends[-1] + prior_size :].reshape(kinds, -1)
-    recon_total = sum_all(jnp.full((1, 128), recon_local, jnp.float32))[0, 0]
+    prior_out = packed[ends[-1] : ends[-1] + prior_size].reshape(2, kinds, -1)
+    recon_total = 0.5 * jnp.sum(recon_total)
     loss = (recon_total / count + ramp_weight * jnp.sum(free)) / GENES
     return (
         loss,
@@ -890,8 +1090,8 @@
         vector_grads[5],
         encoder_weight_grad,
         vector_grads[6],
-        prior_mean_out,
-        prior_logvar_out,
+        prior_out[0],
+        prior_out[1],
         decoder_grad,
     )
 

time: 671 us -> 616 us (0.918); the launches traced: 660 us -> 612 us
  waiting for transfers between devices: 28.6 us -> 0.01 us
  starting transfers between devices: 23.8 us -> 1.63 us
  Pallas kernels: 420 us -> 442 us
  matrix products: 91.4 us -> 75.3 us
    pallas_call x0 -> x1, Pallas kernels: none -> 34.6 us  [latent_step(): pl.pallas_call(functools.partial(latent_kernel, total), out_shape=[jax.Sh...]
    ppermute x25 -> x2, waiting for transfers between devices: 28.6 us -> 0.01 us  [swap(): lax.ppermute(values, AXES, [(i, i ^ mask) for i in range(device_total())])]
    ppermute x25 -> x2, starting transfers between devices: 23.8 us -> 1.63 us  [swap(): lax.ppermute(values, AXES, [(i, i ^ mask) for i in range(device_total())])]
    pallas_call x1, Pallas kernels: 230 us -> 216 us  [gather_weights(): pl.pallas_call(functools.partial(gather_kernel, total), out_shape=[jax.Sh...]
    dot_general x7 -> x5, matrix products: 28.8 us -> 18.1 us  [across(): lax.dot_general(left, right, (((1,), (1,)), ((), ())), preferred_element_...]
    dot_general x7 -> x6, matrix products: 34.8 us -> 28.8 us  [contract_rows(): lax.dot_general(left, right, (((0,), (0,)), ((), ())), preferred_element_...]
    unnamed x218 -> x207, local copies, waits for them, and re-layouts: 28 us -> 25.4 us
    dot_general x7 -> x6, matrix products: 20.1 us -> 21.3 us  [matmul(): return jnp.dot(left, right, preferred_element_type=jnp.float32)]
  transfers between devices with their start and end apart: 25 -> 2, of which waited for: 14 -> 0; matrix products, arithmetic and copies ran while one was open for 13% -> 4% of each run, Pallas kernels for 35% -> 0%
where the time goes in v4:
time: 616 us; the launch traced here: 612 us
  Pallas kernels  442 us (72%)
  matrix products  75.3 us (12%)
  local copies, waits for them, and re-layouts  65.8 us (11%)
  other arithmetic  20.3 us (3%)
  between operations  6.73 us (1%)
    pallas_call x1, Pallas kernels, gather_weights(): pl.pallas_call(functools.partial(gather_kernel, total), out_shape=[jax.Sh...  216 us
    pallas_call x1, Pallas kernels, scatter_sums(): pl.pallas_call(functools.partial(scatter_kernel, total), out_shape=out_sh...  192 us
    pallas_call x1, Pallas kernels, latent_step(): pl.pallas_call(functools.partial(latent_kernel, total), out_shape=[jax.Sh...  34.6 us
    dot_general x6, matrix products, contract_rows(): lax.dot_general(left, right, (((0,), (0,)), ((), ())), preferred_element_...  28.8 us
    unnamed x207, local copies, waits for them, and re-layouts  25.4 us
    dot_general x6, matrix products, matmul(): return jnp.dot(left, right, preferred_element_type=jnp.float32)  21.3 us
    dot_general x5, matrix products, across(): lax.dot_general(left, right, (((1,), (1,)), ((), ())), preferred_element_...  18.1 us
  transfers between devices with their start and end apart: 2, of which 0 were waited for; matrix products, arithmetic and copies ran while one was open for 4% of the time, Pallas kernels for 0%

profile of v4, /device:TPU:0, one launch (start us, length us, event | category | flops | bytes accessed | tf_op | source)
XLA Modules:
  0.0 612.2 jit_solution(1018143616215127666)
XLA Ops:
  3.6 4.3 copy.126
  8.0 1.9 slice_bitcast_fusion.2
  25.1 215.5 %gather_weights.1 = (bf16[4,128,3456]{2,1,0:T(8,128)(2,1)S(1)}, bf16[8,4,32,3456]{3,2,1,0:T(8,128)(2,1)}, bf16[8,4,16,3456]{3,2,1,0:T(8,128)(2,1)S(1)}, bf16[8,2...) custom-call(bf16[4,128,3456]{2,1,0:T(8,128)(2,1)S(1)} %pad_maximum_f, ...), custom_call_target="tpu_custom_call" | custom-call | tf_op jit(solution)/shard_map/gather_weights/pallas_call | solution.py:418
  242.0 1.8 copy-done.4
  243.7 1.7 copy-done.6
  249.3 3.9 convolution_convert_fusion.3
  258.0 1.8 copy.137
  264.2 1.9 add.159
  273.2 5.3 convolution_add_fusion
  278.6 5.8 fusion.10
  287.3 2.0 copy-done.7
  289.3 34.6 %latent_step.1 = (bf16[4,128,3456]{2,1,0:T(8,128)(2,1)S(1)}, bf16[512,3456]{1,0:T(8,128)(2,1)S(1)}, f32[128,512]{1,0:T(8,128)S(1)}, f32[8,512]{1,0:T(8,128)S(1)}, f32[8,384]{1,0:T(8,128)S(1)}) custom-call(bf16[128,640]{1,0:T(8,128)(2,1)S(1)} %pad_maximum_fusion.18.refs_0_, f32[8,512]{1,0:T(8,128)S(1)} %broadcast_in_dim.34.refs_1_, f32[1,1]{1,0:T(1,128)} %bitcast.42.refs_2_, ...), custom_call_target="tpu_custom_call" | custom-call | tf_op jit(solution)/shard_map/latent_step/pallas_call | solution.py:789
  323.9 1.8 copy-done.14
  328.6 7.6 %convert_reduce_fusion = (f32[4096]{0:T(1024)S(1)}, bf16[128,4096]{1,0:T(8,128)(2,1)S(1)}) fusion(f32[128,4096]{1,0:T(8,128)S(1)} %copy-done.24, bf16[4096,1024]{1,0:T(8,128)(2,1)} %bitcast.236, f32[128,1024]{1,0:T(8,128)S(1)} %fusion.42), kind=kOutput, calls=%fused_computation.22 | convolution fusion | flops 1085403136 | bytes 12075008 | tf_op jit(solution)/shard_map/dot_general | solution.py:44
  336.3 3.0 multiply_reduce_fusion.2
  346.6 5.1 multiply_reduce_fusion.1
  352.2 1.6 collective-permute-start
  353.8 6.0 convolution_convert_fusion.1
  359.7 2.1 convolution_convert_fusion.5
  361.8 4.7 convolution_convert_fusion.2
  368.3 3.2 convolution_convert_fusion.4
  371.4 1.8 pad_maximum_fusion.10
  375.3 5.7 convolution_convert_fusion
  382.3 7.2 %bitcast_convert_fusion = bf16[1024,3456]{1,0:T(8,128)(2,1)} fusion(bf16[4,128,3456]{2,1,0:T(8,128)(2,1)S(1)} %copy-done.5, bf16[1,128,1024]{2,1,0:T(8,128)(2,1)S(1)} %get-tuple-element.176, bf16[1,128,1024]{2,1,0:T(8,128)(2,1)} %bitcast.57, bf16[1,128,1024]{2,1,0:T(8,128)(2,1)S(1)} %get-tuple-element.175, bf16[1,128,1024]{2,1,0:T(8,128)(2,1)S(1)} %bitcast.192), kind=kOutput, calls=%fused_computation | convolution fusion | flops 3628990464 | bytes 11665408 | tf_op jit(solution)/shard_map/dot_general | solution.py:50
  389.5 5.4 fusion
  394.9 192.4 %scatter_sums.1 = (bf16[4,32,3456]{2,1,0:T(8,128)(2,1)}, bf16[4,16,3456]{2,1,0:T(8,128)(2,1)}, bf16[4,128,3456]{2,1,0:T(8,128)(2,1)}, f32[32,3072]{1,0:T(8,128)}...) custom-call(f32[8,2,2,8,128]{4,3,2,1,0:T(8,128)} %bitcast.207, ...), custom_call_target="tpu_custom_call" | custom-call | tf_op jit(solution)/shard_map/scatter_sums/pallas_call | solution.py:666
  589.2 1.8 slice_bitcast_fusion.17
  591.0 2.2 slice_bitcast_fusion.10
  593.2 2.2 slice_bitcast_fusion.6
  595.7 3.6 copy.153
  602.5 2.1 fusion.19
  604.5 2.6 fusion.15
  (304 shorter events, 63.1 us)
Async XLA Ops:
  9.9 10.5 %copy-start.82 = (bf16[16,16]{1,0:T(8,128)(2,1)S(1)}, bf16[16,16]{1,0:T(8,128)(2,1)}, u32[]{:S(2)}) copy-start(bf16[16,16]{1,0:T(8,128)(2,1)} %param.44) | copy-start | bytes 1540
  9.9 10.5 %copy-start.83 = (bf16[16,16]{1,0:T(8,128)(2,1)S(1)}, bf16[16,16]{1,0:T(8,128)(2,1)}, u32[]{:S(2)}) copy-start(bf16[16,16]{1,0:T(8,128)(2,1)} %param.43) | copy-start | bytes 1540
  9.9 13.3 %copy-start.40 = (bf16[1,128,3456]{2,1,0:T(8,128)(2,1)S(1)}, bf16[1,128,3456]{2,1,0:T(8,128)(2,1)}, u32[]{:S(2)}) copy-start(bf16[1,128,3456]{2,1,0:T(8,128)(2,1)} %get-tuple-element.158) | copy-start | bytes 2654212
  9.9 13.3 %copy-start.41 = (bf16[1,128,3456]{2,1,0:T(8,128)(2,1)S(1)}, bf16[1,128,3456]{2,1,0:T(8,128)(2,1)}, u32[]{:S(2)}) copy-start(bf16[1,128,3456]{2,1,0:T(8,128)(2,1)} %get-tuple-element.159) | copy-start | bytes 2654212
  9.9 13.3 %copy-start.42 = (bf16[1,128,3456]{2,1,0:T(8,128)(2,1)S(1)}, bf16[1,128,3456]{2,1,0:T(8,128)(2,1)}, u32[]{:S(2)}) copy-start(bf16[1,128,3456]{2,1,0:T(8,128)(2,1)} %get-tuple-element.160) | copy-start | bytes 2654212
  9.9 13.3 %copy-start.43 = (bf16[1,128,3456]{2,1,0:T(8,128)(2,1)S(1)}, bf16[1,128,3456]{2,1,0:T(8,128)(2,1)}, u32[]{:S(2)}) copy-start(bf16[1,128,3456]{2,1,0:T(8,128)(2,1)} %get-tuple-element.161) | copy-start | bytes 2654212
  25.1 221.8 %copy-start.94 = (s32[1,128]{1,0:T(1,128)S(1)}, s32[1,128]{1,0:T(1,128)}, u32[]{:S(2)}) copy-start(s32[1,128]{1,0:T(1,128)} %param.26) | copy-start | bytes 1540
  25.1 222.8 %copy-start.86 = (f32[2,128]{1,0:T(2,128)S(1)}, f32[2,128]{1,0:T(2,128)}, u32[]{:S(2)}) copy-start(f32[2,128]{1,0:T(2,128)} %param.24) | copy-start | bytes 3076
  25.1 222.8 %copy-start.85 = (f32[256]{0:T(256)S(1)}, f32[256]{0:T(256)}, u32[]{:S(2)}) copy-start(f32[256]{0:T(256)} %multiply_exponential_fusion.1) | copy-start | bytes 3076
  289.3 37.1 %copy-start.29 = (f32[128,512]{1,0:T(8,128)S(1)}, f32[128,512]{1,0:T(8,128)}, u32[]{:S(2)}) copy-start(f32[128,512]{1,0:T(8,128)} %copy-done.28) | copy-start | bytes 786436
  289.3 37.2 %copy-start.34 = (f32[128,1024]{1,0:T(8,128)S(1)}, f32[128,1024]{1,0:T(8,128)}, u32[]{:S(2)}) copy-start(f32[128,1024]{1,0:T(8,128)} %copy-done.33) | copy-start | bytes 1572868
  289.3 37.2 %copy-start.38 = (f32[128,512]{1,0:T(8,128)S(1)}, f32[128,512]{1,0:T(8,128)}, u32[]{:S(2)}) copy-start(f32[128,512]{1,0:T(8,128)} %get-tuple-element.219) | copy-start | bytes 786436
  289.3 37.2 %copy-start.49 = (f32[128,512]{1,0:T(8,128)S(1)}, f32[128,512]{1,0:T(8,128)}, u32[]{:S(2)}) copy-start(f32[128,512]{1,0:T(8,128)} %param.28) | copy-start | bytes 786436
  289.3 37.2 %copy-start.80 = (f32[128]{0:T(128)S(1)}, f32[128]{0:T(128)}, u32[]{:S(2)}) copy-start(f32[128]{0:T(128)} %get-tuple-element.214) | copy-start | bytes 1540
  289.3 37.4 %copy-start.2 = (bf16[8,2,2,32,1024]{4,3,2,1,0:T(8,128)(2,1)S(1)}, bf16[8,2,2,32,1024]{4,3,2,1,0:T(8,128)(2,1)}, u32[]{:S(2)}) copy-start(bf16[8,2,2,32,1024]{4,3,2,1,0:T(8,128)(2,1)} %copy-done) | copy-start | bytes 6291460
  326.7 9.5 %slice-start = ((s8[8388608]{0:T(1024)(128)(4,1)}), s8[4194304]{0:T(1024)(128)(4,1)S(1)}, s32[]{:S(2)}) async-start(s8[8388608]{0:T(1024)(128)(4,1)} %bitcast.173), calls=%async_computation | async-start | bytes 8388608
  328.6 11.0 %copy-start.31 = (f32[128,1024]{1,0:T(8,128)}, f32[128,1024]{1,0:T(8,128)S(1)}, u32[]{:S(2)}) copy-start(f32[128,1024]{1,0:T(8,128)S(1)} %fusion.42) | copy-start | bytes 1572868
  328.6 7.6 %slice-start.1 = ((s8[8388608]{0:T(1024)(128)(4,1)}), s8[4194304]{0:T(1024)(128)(4,1)S(1)}, s32[]{:S(2)}) async-start(s8[8388608]{0:T(1024)(128)(4,1)} %bitcast.173), calls=%async_computation.1 | async-start | bytes 8388608
  328.6 7.6 %copy-start.18 = (f32[128,1024]{1,0:T(8,128)S(1)}, f32[128,1024]{1,0:T(8,128)}, u32[]{:S(2)}) copy-start(f32[128,1024]{1,0:T(8,128)} %copy-done.16) | copy-start | bytes 1572868
  328.6 7.7 %copy-start.70 = (f32[128]{0:T(128)S(1)}, f32[128]{0:T(128)}, u32[]{:S(2)}) copy-start(f32[128]{0:T(128)} %copy-done.69) | copy-start | bytes 1540
  328.6 7.7 %copy-start.71 = (f32[128]{0:T(128)S(1)}, f32[128]{0:T(128)}, u32[]{:S(2)}) copy-start(f32[128]{0:T(128)} %fusion.55) | copy-start | bytes 1540
  352.2 7.6 %copy-start.52 = (bf16[16,64,128]{2,1,0:T(8,128)(2,1)S(1)}, bf16[16,64,128]{2,1,0:T(8,128)(2,1)}, u32[]{:S(2)}) copy-start(bf16[16,64,128]{2,1,0:T(8,128)(2,1)} %copy-done.51) | copy-start | bytes 786436
  352.2 19.2 %collective-permute-start = (bf16[128,1024]{1,0:T(8,128)(2,1)S(1)}, bf16[128,1024]{1,0:T(8,128)(2,1)}, u32[]{:S(2)}, u32[]{:S(2)}) collective-permute-start(bf16[128,1024]{1,0:T(8,128)(2,1)S(1)} %add_convert_fusion), channel_id=1, source_target_pairs={{0,2},{1,3},{2,0},{3,1},{4,6},{5,7},{6,4},{7,5},{8,10},{9,11},{10,... | collective-permute-start | bytes 786440 | tf_op jit(solution)/shard_map/ppermute | solution.py:133
  368.2 7.0 %copy-start.25 = (f32[128,4096]{1,0:T(8,128)S(1)}, f32[128,4096]{1,0:T(8,128)}, u32[]{:S(2)}) copy-start(f32[128,4096]{1,0:T(8,128)} %copy-done.23) | copy-start | bytes 6291460
  368.2 7.0 %copy-start.32 = (f32[128,1024]{1,0:T(8,128)S(1)}, f32[128,1024]{1,0:T(8,128)}, u32[]{:S(2)}) copy-start(f32[128,1024]{1,0:T(8,128)} %copy-done.31) | copy-start | bytes 1572868
  373.2 7.7 %collective-permute-start.1 = (bf16[2,128,1024]{2,1,0:T(8,128)(2,1)}, bf16[2,128,1024]{2,1,0:T(8,128)(2,1)S(1)}, u32[]{:S(2)}, u32[]{:S(2)}) collective-permute-start(bf16[2,128,1024]{2,1,0:T(8,128)(2,1)} %pad_maximum_fusion.10), channel_id=1, source_target_pairs={{0,1},{1,0},{2,3},{3,2},{4,5},{5,4},{6,7},{7,6},{8,9},{9,8},{10,11... | collective-permute-start | bytes 1572872 | tf_op jit(solution)/shard_map/ppermute | solution.py:133
  375.2 7.0 %copy-start.5 = (bf16[4,128,3456]{2,1,0:T(8,128)(2,1)S(1)}, bf16[4,128,3456]{2,1,0:T(8,128)(2,1)}, u32[]{:S(2)}) copy-start(bf16[4,128,3456]{2,1,0:T(8,128)(2,1)} %copy-done.4) | copy-start | bytes 10616836
  381.0 8.5 %slice-start.2 = ((s8[7077888]{0:T(1024)(128)(4,1)}), s8[4194304]{0:T(1024)(128)(4,1)S(1)}, s32[]{:S(2)}) async-start(s8[7077888]{0:T(1024)(128)(4,1)} %bitcast.237), calls=%async_computation.2 | async-start | bytes 8388608
  382.2 7.2 %copy-start.15 = (bf16[4,128,3456]{2,1,0:T(8,128)(2,1)S(1)}, bf16[4,128,3456]{2,1,0:T(8,128)(2,1)}, u32[]{:S(2)}) copy-start(bf16[4,128,3456]{2,1,0:T(8,128)(2,1)} %copy-done.14) | copy-start | bytes 10616836
  382.3 7.2 %slice-start.3 = ((s8[7077888]{0:T(1024)(128)(4,1)}), s8[2883584]{0:T(1024)(128)(4,1)S(1)}, s32[]{:S(2)}) async-start(s8[7077888]{0:T(1024)(128)(4,1)} %bitcast.237), calls=%async_computation.3 | async-start | bytes 5767168
  595.7 6.1 %copy-start.75 = (f32[8,128]{1,0:T(8,128)S(1)}, f32[8,128]{1,0:T(8,128)}, u32[]{:S(2)}) copy-start(f32[8,128]{1,0:T(8,128)} %get-tuple-element.64) | copy-start | bytes 12292
  599.3 7.9 %copy-start.63 = (f32[32,3072]{1,0:T(8,128)S(1)}, f32[32,3072]{1,0:T(8,128)}, u32[]{:S(2)}) copy-start(f32[32,3072]{1,0:T(8,128)} %get-tuple-element.247) | copy-start | bytes 1179652
  (69 other events, 171.4 us)

commit v5 on v4

--- a/solution.py
+++ b/solution.py
@@ -110,6 +110,7 @@
 AXES = ("dp", "fsdp")
 GROUP = 4
 CHUNK = 3456
+SLICE = 384
 NARROW = 8
 
 
@@ -252,6 +253,10 @@
         copy = pltpu.make_async_copy(source, target, self.local_sems.at[at])
         copy.start()
         return copy
+
+    def free(self, copy):
+        copy.wait_send()
+        self.sent = [other for other in self.sent if other is not copy]
 
     def finish(self):
         for copy in self.sent:
@@ -351,15 +356,34 @@
             hold(block + 2)
 
     across_core = []
-    step("embed", 0)
+
+    def to_core(copies_of, block_of):
+        for copy, (_, full, way) in zip(copies_of, late):
+            copy.wait_recv()
+            block = block_of(full, way)
+            across_core.append(copies.send(block, block, here.peers[1]))
+
+    def crossed(s):
+        to_core(
+            across_x[len(late) * s : len(late) * (s + 1)],
+            lambda full, way: full.at[here.owner(way * s), 1 - x, core],
+        )
+
     for s in range(1, last + 1):
         late_step(s)
+        if s == 1:
+            step("embed", 0)
         step("embed", s)
         if s == last - 1:
             step("early", 0)
             step("decoder", 0)
     hold(0)
     hold(1)
+    for copy in own_late:
+        copy.wait()
+    for _, full, _ in late:
+        block = full.at[:, x, core]
+        across_core.append(copies.send(block, block, here.peers[1]))
     for copy in cell_moves:
         copy.wait_recv()
     own_cells.wait()
@@ -371,22 +395,18 @@
         multiply(s - 2)
         step("early", s)
         step("decoder", s)
+        crossed(s - 2)
     for block in range(last - 1, total):
         multiply(block)
     sums = copies.send(partial.at[:, 1], other_core, here.peers[1])
-    for copy in own_late:
-        copy.wait()
     for full in (joint_all, small_all):
         block = full.at[:, :, core]
         across_core.append(copies.send(block, block, here.peers[1]))
     sums.wait_recv()
     for_x[...] = low(wide(partial[1, 0]) + wide(other_core[1]))
     sums = copies.send(for_x, other_x, here.peers[2])
-    for copy in across_x:
-        copy.wait_recv()
-    for _, full, _ in late:
-        block = full.at[:, :, core]
-        across_core.append(copies.send(block, block, here.peers[1]))
+    for s in range(last - 1, total):
+        crossed(s)
     sums.wait_recv()
     embedded[...] = wide(partial[0, 0]) + wide(other_core[0]) + wide(other_x[...])
     for copy in across_core:
@@ -404,7 +424,7 @@
         + [(total,) + v.shape for v in tables]
         + [(total, 2, 2) + v.shape for v in own]
     )
-    remote = 15 + 12 * (total - 1) + 4 * total + 8
+    remote = 15 + 12 * (total - 1) + 8 * total + 8
     cell_rows, genes = cells.shape[1:]
     features = total * GROUP * embed.shape[1]
     buffers = [
@@ -445,128 +465,256 @@
         target[part, :] = (wide(first[part, :]) + wide(second[part, :])).astype(dtype)
 
 
+def product(target, left, right, accumulate):
+    total, _, rows, columns = target.shape
+    step = 256 // (2 * rows)
+    width = 512
+
+    @pl.loop(0, total // step)
+    def _(i):
+        blocks = pl.ds(i * step, step)
+        part = left(i * 2 * step, 2 * step)
+
+        @pl.loop(0, columns // width)
+        def _(n):
+            across_columns = pl.ds(pl.multiple_of(n * width, width), width)
+            value = matmul(part, right[:, across_columns]).reshape(step, 2, rows, width)
+            if accumulate:
+                value = value + wide(target[blocks, :, :, across_columns])
+            target[blocks, :, :, across_columns] = low(value)
+
+
+MIDDLE = ("joint", "output", "encoder", "up", "down")
+
+
 def scatter_kernel(total, *refs):
-    (small, recon, *refs) = refs
-    (embed, decoder, joint, output, encoder, up, down, cells) = refs[:8]
-    (embed_out, decoder_out, cells_out) = refs[8:11]
-    (joint_out, output_out, encoder_out, up_out, down_out, small_out, recon_out) = refs[11:18]
-    (chip_small, stage_small, sum_small, hop_small, group_recon, all_recon) = refs[18:24]
-    refs = refs[24:]
-    (chip_joint, chip_output, chip_encoder, chip_up, chip_down) = refs[:5]
-    (stage_up, stage_down) = refs[5:7]
-    (sum_output, sum_encoder, sum_up, sum_down) = refs[7:11]
-    (hop_embed, hop_decoder, hop_joint) = refs[11:14]
-    (hop_output, hop_encoder, hop_up, hop_down) = refs[14:18]
-    (local_embed, local_decoder) = refs[18:20]
-    (last_embed, last_decoder, last_joint, other_joint) = refs[20:24]
+    (recon, start, small, decoder, cells, table, grads) = refs[:7]
+    left = dict(zip(MIDDLE, refs[7:12]))
+    right = dict(zip(MIDDLE, refs[12:17]))
+    (embed_out, decoder_out, cells_out, embed, back) = refs[17:22]
+    results = dict(zip(MIDDLE, refs[22:27]))
+    (small_out, recon_out) = refs[27:29]
+    (chip_small, stage_small, sum_small, hop_small, group_recon, all_recon) = refs[29:35]
+    chip = dict(zip(MIDDLE, refs[35:40]))
+    (send_up, send_down) = refs[40:42]
+    sums = dict(zip(MIDDLE[1:], refs[42:46]))
+    (hop_embed, hop_decoder, hop_joint) = refs[46:49]
+    hops_of = dict(zip(MIDDLE[1:], refs[49:53]))
+    (local_embed, local_decoder) = refs[53:55]
+    (other_joint, starts, turned) = refs[55:58]
+    (in_cells, in_table, in_grads, out_term, out_back, blocks) = refs[58:64]
     here = Where(total)
-    copies = Copies(*refs[24:])
+    copies = Copies(*refs[64:67])
+    stream_sems = refs[67]
     here.meet()
     x, core, last = here.x, here.core, total - 1
     towards = {1: here.right, -1: here.left}
     flying = {}
 
-    tables = []
-    for term, hops, local, result in (
-        (embed, hop_embed, local_embed, last_embed),
-        (decoder, hop_decoder, local_decoder, last_decoder),
-    ):
-        for way in (1, -1):
-            tables.append((term, hops, local, result, way, 0 if way == 1 else 1))
+    def lanes(term, hops, local):
+        return [(term, hops, local, way, side) for side, way in ((0, 1), (1, -1))]
+
+    tables = {
+        "embed": lanes(embed, hop_embed, local_embed),
+        "decoder": lanes(decoder, hop_decoder, local_decoder),
+    }
 
     def table_block(term, way, side, h):
         return term.at[here.owner(way * h), pl.ds(2 * side, 2)]
 
-    def fetch(n, h):
-        term, _, local, _, way, side = tables[n]
-        flying["local", n, h] = copies.local(
-            table_block(term, way, side, h + 1), local.at[h % 2, side]
-        )
-
-    for n, (term, hops, _, _, way, side) in enumerate(tables):
-        flying["table", n] = copies.send(
-            table_block(term, way, side, 1), hops.at[0, side], towards[way]
-        )
-    halves = {}
-    for name, term, chip in (
-        ("up", up, chip_up),
-        ("down", down, chip_down),
-        ("output", output, chip_output),
-        ("encoder", encoder, chip_encoder),
-        ("joint", joint, chip_joint),
-        ("small", small, chip_small),
-    ):
-        halves[name] = copies.send(term.at[:, :, 1 - core], chip, here.peers[1])
+    def fetch(name, h):
+        for n, (term, _, local, way, side) in enumerate(tables[name]):
+            flying["local", name, n, h] = copies.local(
+                table_block(term, way, side, h + 1), local.at[h % 2, side]
+            )
+
+    def table_start(name):
+        for n, (term, hops, _, way, side) in enumerate(tables[name]):
+            flying[name, n] = copies.send(
+                table_block(term, way, side, 1), hops.at[0, side], towards[way]
+            )
+        fetch(name, 1)
+        fetch(name, 2)
+
+    def table_hop(name, h):
+        for n, (_, hops, local, way, side) in enumerate(tables[name]):
+            flying[name, n].wait_recv()
+            flying["local", name, n, h].wait()
+            for row in range(2):
+                arrived = hops.at[h - 1, side, row]
+                add_rows(arrived, arrived, local.at[h % 2, side, row], jnp.bfloat16)
+            if h < last:
+                flying[name, n] = copies.send(hops.at[h - 1, side], hops.at[h, side], towards[way])
+        if h + 2 <= last:
+            fetch(name, h + 2)
+
+    table_start("decoder")
+    moves = [copies.send(start, starts.at[m], here.peers[m]) for m in (2, 3, 1)]
+    starts[0] = start[...]
     group_recon[here.quarter] = recon[...]
     recons = [copies.send(recon, group_recon.at[here.quarter], here.peers[m]) for m in (2, 3, 1)]
-    loads = {
-        "small": copies.local(small.at[:, :, core], stage_small),
-        "up": copies.local(up.at[:, :, core], stage_up),
-        "down": copies.local(down.at[:, :, core], stage_down),
-    }
-    for h in (1, 2):
-        for n in range(len(tables)):
-            fetch(n, h)
-
-    def table_hop(h):
-        for n, (term, hops, local, result, way, side) in enumerate(tables):
-            flying["table", n].wait_recv()
-            flying["local", n, h].wait()
-            for row in range(2):
-                arrived = hops.at[h - 1, side, row]
-                target = arrived if h < last else result.at[2 * side + row]
-                add_rows(target, arrived, local.at[h % 2, side, row], jnp.bfloat16)
-            if h < last:
-                flying["table", n] = copies.send(
-                    hops.at[h - 1, side], hops.at[h, side], towards[way]
-                )
-            if h + 2 <= last:
-                fetch(n, h + 2)
-
-    def chip_sum(name, chip, staged):
+    halves = {"small": copies.send(small.at[:, :, 1 - core], chip_small, here.peers[1])}
+    own_small = copies.local(small.at[:, :, core], stage_small)
+
+    def half(name, which):
+        source = left[name]
+        if results[name].shape[0] == 128:
+
+            def wide_blocks(first, size):
+                lanes = [
+                    pl.ds(pl.multiple_of((2 * (first + n) + which) * 128, 128), 128)
+                    for n in range(size)
+                ]
+                return jnp.concatenate([low(wide(source[:, part]).T) for part in lanes])
+
+            return wide_blocks
+        blocks[...] = low(wide(source[...]).T).reshape(blocks.shape)
+
+        def narrow_blocks(first, size):
+            return blocks[pl.ds(first, size), which].reshape(-1, blocks.shape[-1])
+
+        return narrow_blocks
+
+    def give(name, buffer):
+        product(buffer, half(name, 1 - core), right[name], False)
+        halves[name] = copies.send(buffer, chip[name], here.peers[1])
+
+    across = {}
+
+    def cross(name, held, target):
+        across[name] = copies.send(held.at[:, 1 - x], target, here.peers[2])
+
+    def take(name):
         halves[name].wait_recv()
-        loads[name].wait()
-
-        @pl.loop(0, total)
-        def _(t):
-            for side in range(2):
-                add_rows(chip.at[t, side], chip.at[t, side], staged.at[t, side], chip.dtype)
-
-    across = {}
-
-    def cross(name, chip, sums):
-        across[name] = copies.send(chip.at[:, 1 - x], sums, here.peers[2])
-
-    chip_sum("up", chip_up, stage_up)
-    cross("up", chip_up, sum_up)
-    staged_joint = stage_up.at[:, :, :, pl.ds(0, joint.shape[-1])]
-    loads["joint"] = copies.local(joint.at[:, :, core], staged_joint)
-    chip_sum("down", chip_down, stage_down)
-    cross("down", chip_down, sum_down)
-    slim = output.shape[3]
-    staged_output = stage_down.at[:, :, pl.ds(0, slim)]
-    staged_encoder = stage_down.at[:, :, pl.ds(slim, slim)]
-    loads["output"] = copies.local(output.at[:, :, core], staged_output)
-    loads["encoder"] = copies.local(encoder.at[:, :, core], staged_encoder)
-    table_hop(1)
-    chip_sum("joint", chip_joint, staged_joint)
+        product(chip[name], half(name, core), right[name], True)
+        if name in sums:
+            cross(name, chip[name], sums[name])
+
+    give("up", send_up)
+    give("down", send_down)
+    table_hop("decoder", 1)
+    take("up")
+    copies.free(halves["up"])
+    give("joint", send_up.at[:, :, :, pl.ds(0, right["joint"].shape[1])])
+    table_hop("decoder", 2)
+    take("down")
+    copies.free(halves["down"])
+    slim = results["output"].shape[0]
+    give("output", send_down.at[:, :, pl.ds(0, slim)])
+    give("encoder", send_down.at[:, :, pl.ds(slim, slim)])
+    table_hop("decoder", 3)
+    take("joint")
     for side, way in ((0, 1), (1, -1)):
         flying["joint", side] = copies.send(
-            chip_joint.at[here.owner(way), side], hop_joint.at[0, side], towards[way]
+            chip["joint"].at[here.owner(way), side], hop_joint.at[0, side], towards[way]
         )
-    chip_sum("output", chip_output, staged_output)
-    cross("output", chip_output, sum_output)
-    chip_sum("encoder", chip_encoder, staged_encoder)
-    cross("encoder", chip_encoder, sum_encoder)
-    chip_sum("small", chip_small, stage_small)
+    take("output")
+    take("encoder")
+    own_small.wait()
+    halves["small"].wait_recv()
+
+    @pl.loop(0, total)
+    def _(t):
+        for side in range(2):
+            held = chip_small.at[t, side]
+            add_rows(held, held, stage_small.at[t, side], jnp.float32)
+
     cross("small", chip_small, sum_small)
     for copy in recons:
         copy.wait_recv()
     all_recon[here.t] = group_recon[0] + group_recon[1] + group_recon[2] + group_recon[3]
     own_recon = all_recon.at[here.t]
     flying["recon"] = copies.send(own_recon, own_recon, here.right)
-    moves = [copies.send(cells.at[m], cells_out.at[here.quarter], here.peers[m]) for m in (2, 3, 1)]
-    own = [copies.local(cells.at[0], cells_out.at[here.quarter])]
+    table_hop("decoder", 4)
+
+    for copy in moves:
+        copy.wait_recv()
+    moves = []
+    rows, rows_of_t = start.shape[0], turned.shape[0] // total
+    for m in range(GROUP):
+        turned[:, m * rows : (m + 1) * rows] = low(wide(starts[m]).T)
+
+    def moved(i, pairs, first):
+        part = pl.ds(pl.multiple_of(i * SLICE, 128), SLICE)
+        slot = i % 2
+        return [
+            pltpu.make_async_copy(*ends(part, slot), stream_sems.at[first + n, slot])
+            for n, ends in enumerate(pairs)
+        ]
+
+    def loads_of(i):
+        return moved(
+            i,
+            [
+                lambda part, slot: (cells.at[:, :, part], in_cells.at[slot]),
+                lambda part, slot: (table.at[:, part], in_table.at[slot]),
+                lambda part, slot: (grads.at[:, :, part], in_grads.at[slot]),
+            ],
+            0,
+        )
+
+    def stores_of(i):
+        return moved(
+            i,
+            [
+                lambda part, slot: (out_term.at[slot], embed.at[:, :, :, part]),
+                lambda part, slot: (out_back.at[slot], back.at[:, :, part]),
+            ],
+            3,
+        )
+
+    count = CHUNK // SLICE
+    for copy in loads_of(0):
+        copy.start()
+
+    def stream(first, end):
+        @pl.loop(first, end)
+        def _(i):
+            slot = i % 2
+            @pl.when(i + 1 < count)
+            def _():
+                for copy in loads_of(i + 1):
+                    copy.start()
+
+            for copy in loads_of(i):
+                copy.wait()
+
+            @pl.when(i >= 2)
+            def _():
+                for copy in stores_of(i - 2):
+                    copy.wait()
+
+            for t in range(total):
+                term = matmul(
+                    turned[pl.ds(t * rows_of_t, rows_of_t), :],
+                    in_cells[slot].reshape(GROUP * rows, SLICE),
+                )
+                out_term[slot, t] = low(term).reshape(out_term.shape[2:])
+            for m in range(GROUP):
+                out_back[slot, m] = low(matmul(starts[m], in_table[slot]) - wide(in_grads[slot, m]))
+            for copy in stores_of(i):
+                copy.start()
+
+    stream(0, count // 3)
+    table_hop("decoder", 5)
+    stream(count // 3, 2 * count // 3)
+    table_hop("decoder", 6)
+    stream(2 * count // 3, count)
+    for i in (count - 2, count - 1):
+        for copy in stores_of(i):
+            copy.wait()
+    table_start("embed")
+    moves = [copies.send(back.at[m], cells_out.at[here.quarter], here.peers[m]) for m in (2, 3, 1)]
+    own = [copies.local(back.at[0], cells_out.at[here.quarter])]
+    table_hop("decoder", last)
+
+    def send_back(hops, out):
+        done = [hops.at[last - 1, quarter // 2, quarter % 2] for quarter in here.quarters]
+        for m in (2, 3, 1):
+            moves.append(copies.send(done[m], out.at[here.quarter], here.peers[m]))
+        own.append(copies.local(done[0], out.at[here.quarter]))
+
+    send_back(hop_decoder, decoder_out)
 
     def recon_hop(h):
         flying["recon"].wait_recv()
@@ -578,63 +726,52 @@
         for side, way in ((0, 1), (1, -1)):
             flying["joint", side].wait_recv()
             arrived = hop_joint.at[h - 1, side]
-            target = arrived if h < last else last_joint.at[side]
-            local = chip_joint.at[here.owner(way * (h + 1)), side]
-            add_rows(target, arrived, local, jnp.bfloat16)
+            local = chip["joint"].at[here.owner(way * (h + 1)), side]
+            add_rows(arrived, arrived, local, jnp.bfloat16)
             if h < last:
                 flying["joint", side] = copies.send(arrived, hop_joint.at[h, side], towards[way])
 
     late = [
-        ("up", sum_up, chip_up, hop_up, up_out, 1),
-        ("down", sum_down, chip_down, hop_down, down_out, -1),
-        ("output", sum_output, chip_output, hop_output, output_out, 1),
-        ("encoder", sum_encoder, chip_encoder, hop_encoder, encoder_out, -1),
-        ("small", sum_small, chip_small, hop_small, small_out, 1),
-    ]
+        (name, sums[name], chip[name], hops_of[name], results[name], way)
+        for name, way in (("up", 1), ("down", -1), ("output", 1), ("encoder", -1))
+    ] + [("small", sum_small, chip_small, hop_small, small_out, 1)]
 
     def late_start():
-        for name, sums, chip, hops, _, way in late:
+        for name, summed, held, hops, _, way in late:
             across[name].wait_recv()
 
             @pl.loop(0, total)
             def _(t):
-                add_rows(sums.at[t], sums.at[t], chip.at[t, x], sums.dtype)
-
-            flying["late", name] = copies.send(sums.at[here.owner(way)], hops.at[0], towards[way])
+                add_rows(summed.at[t], summed.at[t], held.at[t, x], summed.dtype)
+
+            flying["late", name] = copies.send(summed.at[here.owner(way)], hops.at[0], towards[way])
 
     def late_hop(h):
-        for name, sums, _, hops, result, way in late:
+        for name, summed, _, hops, result, way in late:
             flying["late", name].wait_recv()
-            local = sums.at[here.owner(way * (h + 1))]
+            local = summed.at[here.owner(way * (h + 1))]
             if h < last:
                 add_rows(hops.at[h - 1], hops.at[h - 1], local, hops.dtype)
                 flying["late", name] = copies.send(hops.at[h - 1], hops.at[h], towards[way])
             else:
                 add_rows(result, hops.at[h - 1], local, jnp.float32)
 
-    joint_hop(1)
-    for h in range(2, last + 1):
-        table_hop(h)
+    for h in range(1, last + 1):
         joint_hop(h)
-    for result, out in ((last_embed, embed_out), (last_decoder, decoder_out)):
-        for m in (2, 3, 1):
-            moves.append(
-                copies.send(
-                    result.at[here.quarters[m]], out.at[here.quarter], here.peers[m]
-                )
-            )
-        own.append(copies.local(result.at[here.quarter], out.at[here.quarter]))
-    joint_move = copies.send(last_joint.at[1 - x], other_joint, here.peers[2])
+        table_hop("embed", h)
+        recon_hop(h)
+    send_back(hop_embed, embed_out)
+    done_joint = hop_joint.at[last - 1]
+    joint_move = copies.send(done_joint.at[1 - x], other_joint, here.peers[2])
     late_start()
     for h in range(1, last + 1):
         late_hop(h)
-        recon_hop(h)
     summed = all_recon[0]
     for t in range(1, total):
         summed = summed + all_recon[t]
     recon_out[...] = summed
     joint_move.wait_recv()
-    add_rows(joint_out, last_joint.at[x], other_joint, jnp.float32)
+    add_rows(results["joint"], done_joint.at[x], other_joint, jnp.float32)
     for copy in moves:
         copy.wait_recv()
     for copy in own:
@@ -642,71 +779,90 @@
     copies.finish()
 
 
-def scatter_sums(embed, decoder, joint, output, encoder, up, down, small, recon, cells):
+def scatter_sums(pairs, start, decoder, cells, table, grads, small, recon):
     total = device_total() // GROUP
     last = total - 1
-    operands = [small, recon, embed, decoder, joint, output, encoder, up, down, cells]
-    middle = [joint, output, encoder, up, down]
+    rows, features = start.shape
     thin = jnp.bfloat16
-    out_shape = [jax.ShapeDtypeStruct(v.shape[1:], thin) for v in (embed, decoder)]
-    out_shape += [jax.ShapeDtypeStruct(cells.shape, thin)]
-    out_shape += [jax.ShapeDtypeStruct(v.shape[3:], jnp.float32) for v in middle]
-    out_shape += [jax.ShapeDtypeStruct(v, jnp.float32) for v in (small.shape[3:], recon.shape)]
+    share = features // (total * GROUP)
+    lefts, rights, shapes = [], [], []
+    for before, after in pairs:
+        block = before.shape[1] // device_total()
+        lefts.append(before)
+        rights.append(after)
+        shapes.append((block, after.shape[1]))
+    operands = [recon, start, small, decoder, cells, table, grads] + lefts + rights
+    decoder_share = decoder.shape[1:]
+    embed_share = (GROUP, share, CHUNK)
+    out_shape = [
+        jax.ShapeDtypeStruct(v, thin)
+        for v in (embed_share, decoder_share, cells.shape, (total,) + embed_share, cells.shape)
+    ]
     block = small.shape[3:]
+    out_shape += [jax.ShapeDtypeStruct(v, jnp.float32) for v in shapes + [block, recon.shape]]
     exact = [(total, 2) + block, (total, 2) + block, (total,) + block, (last,) + block]
     exact += [(GROUP,) + recon.shape, (total,) + recon.shape]
-    chips = [(total, 2) + v.shape[3:] for v in middle]
-    sums = [(total,) + v.shape[3:] for v in middle[1:]]
-    hops = [(last, 2, 2) + v.shape[2:] for v in (embed, decoder)]
-    hops += [(last, 2) + joint.shape[3:]] + [(last,) + v.shape[3:] for v in middle[1:]]
-    local = [(2, 2, 2) + v.shape[2:] for v in (embed, decoder)]
-    results = [v.shape[1:] for v in (embed, decoder)] + [(2,) + joint.shape[3:], joint.shape[3:]]
-    buffers = chips + [chips[3], chips[4]] + sums + hops + local + results
-    remote, here = 12 + 6 * last + 4 * last + 7 + 5 + 2 * last, 4 * last + 9
-    return pl.pallas_call(
+    chips = [(total, 2) + v for v in shapes]
+    buffers = chips + [chips[3], chips[4]] + [(total,) + v for v in shapes[1:]]
+    buffers += [(last, 2, 2) + v[1:] for v in (embed_share, decoder_share)]
+    buffers += [(last, 2) + shapes[0]] + [(last,) + v for v in shapes[1:]]
+    buffers += [(2, 2, 2) + v[1:] for v in (embed_share, decoder_share)]
+    buffers += [shapes[0], (GROUP,) + start.shape, (features, GROUP * rows)]
+    buffers += [(2, GROUP, rows, SLICE), (2, features, SLICE), (2, GROUP, rows, SLICE)]
+    buffers += [(2, total, GROUP, share, SLICE), (2, GROUP, rows, SLICE)]
+    buffers += [(2 * total, 2, shapes[0][0], rows)]
+    remote, here = 12 + 6 * last + 4 * last + 15 + 2 * last, 4 * last + 9
+    anywhere, vmem = pl.BlockSpec(memory_space=pl.ANY), pl.BlockSpec(memory_space=pltpu.VMEM)
+    outs = pl.pallas_call(
         functools.partial(scatter_kernel, total),
         out_shape=out_shape,
-        in_specs=[pl.BlockSpec(memory_space=pl.ANY), pl.BlockSpec(memory_space=pltpu.VMEM)]
-        + [pl.BlockSpec(memory_space=pl.ANY)] * (len(operands) - 2),
-        out_specs=[pl.BlockSpec(memory_space=pl.ANY)] * 3
-        + [pl.BlockSpec(memory_space=pltpu.VMEM)] * 7,
+        in_specs=[vmem] * 2 + [anywhere] * 5 + [vmem] * 10,
+        out_specs=[anywhere] * 5 + [vmem] * 7,
         scratch_shapes=[pltpu.VMEM(shape, jnp.float32) for shape in exact]
         + [pltpu.VMEM(shape, thin) for shape in buffers]
         + [
             pltpu.SemaphoreType.DMA((remote,)),
             pltpu.SemaphoreType.DMA((remote,)),
             pltpu.SemaphoreType.DMA((here,)),
+            pltpu.SemaphoreType.DMA((5, 2)),
         ],
         compiler_params=pltpu.CompilerParams(
             collective_id=2, has_side_effects=True, vmem_limit_bytes=60 * 2**20
         ),
         name="scatter_sums",
     )(*operands)
-
-
-def scatter_plain(embed, decoder, joint, output, encoder, up, down, small, recon, cells):
+    return outs[:3] + outs[5:]
+
+
+def scatter_plain(pairs, start, decoder, cells, table, grads, small, recon):
     quarter = device_index() % GROUP
+    total = device_total() // GROUP
+    starts = group_gather(start).reshape(-1, start.shape[1])
+    wide_cells = cells.reshape(-1, CHUNK)
+    embed = low(contract_rows(starts, wide_cells)).reshape(total, GROUP, -1, CHUNK)
+    back = low(matmul(starts, table) - wide(grads.reshape(-1, CHUNK))).reshape(cells.shape)
 
     def sent(blocks):
         pieces = [pick(blocks, 0)] + [swap(blocks[m], m) for m in range(1, GROUP)]
         return jnp.stack(by_quarter(pieces, quarter))
 
-    def table(term):
+    def table_sum(term):
         block = lax.psum_scatter(
             term, "dp", axis_index_groups=same_quarter(), scatter_dimension=0, tiled=False
         )
         return sent(jnp.stack(by_quarter(list(block), quarter)))
 
     def middle(term):
-        rows = term.reshape((device_total(),) + term.shape[3:])
+        rows = term.reshape((device_total(), -1) + term.shape[-1:])
         return wide(lax.psum_scatter(rows, AXES, scatter_dimension=0, tiled=False))
 
-    return [table(embed), table(decoder), sent(cells)] + [
-        middle(v) for v in (joint, output, encoder, up, down, small)
-    ] + [sum_all(recon)]
-
-
-SLICE = 384
+    terms = [low(contract_rows(before, after)) for before, after in pairs]
+    small = small.reshape((device_total(),) + small.shape[3:])
+    return (
+        [table_sum(embed), table_sum(decoder), sent(back)]
+        + [middle(term) for term in terms]
+        + [lax.psum_scatter(small, AXES, scatter_dimension=0, tiled=False), sum_all(recon)]
+    )
 
 
 def latent_kernel(total, *refs):
@@ -893,22 +1049,17 @@
         components[:, None] == jnp.arange(prior_mean.shape[0], dtype=jnp.int32)[None, :]
     ).astype(jnp.float32)
 
+    kinds = prior_mean.shape[0]
+    vectors = [down_bias, first_gain, first_shift, second_gain, second_shift, encoder_bias]
+    lone = jnp.full((1,), jnp.sum(live), jnp.bfloat16)
     small = jnp.concatenate(
         [
-            up_bias.reshape(rows, 4),
-            down_bias.reshape(rows, 1),
-            first_gain.reshape(rows, 1),
-            first_shift.reshape(rows, 1),
-            second_gain.reshape(rows, 1),
-            second_shift.reshape(rows, 1),
-            encoder_bias.reshape(rows, 1),
-            jnp.concatenate([prior_mean, prior_logvar]).reshape(rows, 16),
-            jnp.full((rows, 1), jnp.sum(live), jnp.bfloat16),
-        ],
-        axis=1,
-    )
-    small_columns = small.shape[1]
-    small = jnp.pad(small, ((0, 0), (0, 128 - small_columns)))
+            jnp.pad(v, ((0, 0), (0, 128 - v.shape[1])))
+            for v in [prior_mean, prior_logvar]
+            + [v.reshape(1, -1) for v in [up_bias] + vectors + [lone]]
+        ]
+    )
+    small = jnp.pad(small, ((0, 48 - small.shape[0]), (0, 0)))
     gather = gather_weights if total <= NARROW else gather_plain
     cells_group, embed_cols, decoder_cols, *middle, embedded = gather(
         gene_chunks(cells),
@@ -921,25 +1072,18 @@
         up_weight,
         down_weight,
     )
-    cells_rows = cells_group.reshape(GROUP * row_count, CHUNK)
     embed_cols = embed_cols.reshape(-1, CHUNK)
     decoder_cols = decoder_cols.reshape(-1, CHUNK)
     middle = [full.reshape(-1, full.shape[-1]) for full in middle]
     joint_full, small_full, output_full, encoder_full, up_full, down_full = middle
-    small_full = wide(small_full)
-    up_bias_full = small_full[:, 0:4].reshape(-1)
-    down_bias_full = small_full[:, 4]
-    gain_first = small_full[:, 5]
-    shift_first = small_full[:, 6]
-    gain_second = small_full[:, 7]
-    shift_second = small_full[:, 8]
-    encoder_bias_full = small_full[:, 9]
-    kinds = prior_mean.shape[0]
-
-    prior_full = small_full[:, 10:26].reshape(devices, 2 * kinds, -1)
+    small_full = wide(small_full.reshape(devices, 48, 128))
+    up_bias_full = small_full[:, 2 * kinds, : 4 * rows].reshape(1, -1)
+    vectors = small_full[:, 2 * kinds + 1 : 2 * kinds + 7, :rows].transpose(1, 0, 2).reshape(6, D)
+    down_bias_full, gain_first, shift_first, gain_second, shift_second, encoder_bias_full = vectors
+    prior_full = small_full[:, : 2 * kinds, : prior_mean.shape[1]]
     prior_full = prior_full.transpose(1, 0, 2).reshape(2 * kinds, LATENT)
     prior_mean_full, prior_logvar_full = prior_full[:kinds], prior_full[kinds:]
-    count = jnp.sum(small_full.reshape(devices, rows, 128)[:, 0, 26])
+    count = jnp.sum(small_full[:, 2 * kinds + 7, 0])
 
     start_state = embedded + positions(coordinates)
     normed_first = layer_norm(start_state, gain_first, shift_first).astype(jnp.bfloat16)
@@ -990,35 +1134,24 @@
     )
     end_grad = across(encoded_grad, encoder_full)
     branch_grad = end_grad.astype(jnp.bfloat16)
-    encoder_term = low(contract_rows(end_low, encoded_grad))
     encoder_bias_grad = jnp.sum(encoded_grad.astype(jnp.float32), axis=0)
-    down_term = low(contract_rows(active, branch_grad))
     down_bias_grad = jnp.sum(branch_grad.astype(jnp.float32), axis=0)
     active_grad = across(branch_grad, down_full)
     gelu_value, gelu_back = jax.vjp(lambda value: jax.nn.gelu(value, approximate=True), pre)
     pre_grad = gelu_back(active_grad)[0].astype(jnp.bfloat16)
-    up_term = low(contract_rows(normed_second, pre_grad))
     up_bias_grad = jnp.sum(pre_grad.astype(jnp.float32), axis=0)
     second_out_grad = across(pre_grad, up_full)
     norm_value, second_back = jax.vjp(layer_norm, middle_state, gain_second, shift_second)
     state_part, second_gain_grad, second_shift_grad = second_back(second_out_grad)
     middle_grad = end_grad + state_part
     attend_grad = middle_grad.astype(jnp.bfloat16)
-    output_term = low(contract_rows(context, attend_grad))
     context_grad = across(attend_grad, output_full).astype(jnp.bfloat16)
     joint_grad = attention_backward(joint, allowed, logsum, context_grad)
-    joint_term = low(contract_rows(normed_first, joint_grad))
     first_out_grad = across(joint_grad, joint_full)
     first_value, first_back = jax.vjp(layer_norm, start_state, gain_first, shift_first)
     start_part, first_gain_grad, first_shift_grad = first_back(first_out_grad)
     start_grad = middle_grad + start_part
     start_low = start_grad.astype(jnp.bfloat16)
-    start_group = group_gather(start_low).reshape(GROUP * row_count, D)
-    embed_term = low(contract_rows(start_group, cells_rows))
-    cells_half = low(
-        matmul(start_group, embed_cols) - wide(recon_grad.reshape(GROUP * row_count, CHUNK))
-    )
-
     vectors = [
         up_bias_grad,
         down_bias_grad,
@@ -1035,25 +1168,26 @@
     packed = jnp.pad(packed, ((0, 0), (0, 1024 - packed.shape[1])))
     packed = packed.reshape(total, 2, 2, 8, 128)
 
-    def by_device(term):
-        return term.reshape(total, 2, 2, term.shape[0] // devices, term.shape[1])
-
     scatter = scatter_sums if total <= NARROW else scatter_plain
     embed_grad, decoder_grad, cells_grad, *middle_grads, small_sum, recon_total = scatter(
-        embed_term.reshape(total, GROUP, rows, CHUNK),
+        [
+            (normed_first, joint_grad),
+            (context, attend_grad),
+            (end_low, encoded_grad),
+            (normed_second, pre_grad),
+            (active, branch_grad),
+        ],
+        start_low,
         decoder_term.reshape(total, GROUP, thin, CHUNK),
-        by_device(joint_term),
-        by_device(output_term),
-        by_device(encoder_term),
-        by_device(up_term),
-        by_device(down_term),
+        cells_group,
+        embed_cols,
+        recon_grad,
         packed,
         recon_sum,
-        cells_half.reshape(GROUP, row_count, CHUNK),
     )
 
     def all_genes(chunks):
-        return jnp.concatenate(list(chunks), axis=1)[:, :GENES]
+        return chunks.transpose(1, 0, 2).reshape(chunks.shape[1], -1)[:, :GENES]
 
     cells_grad = all_genes(cells_grad)
     embed_grad = wide(all_genes(embed_grad))

time: 616 us -> 572 us (0.929)
  matrix products: 75.3 us -> 41.6 us
  local copies, waits for them, and re-layouts: 65.8 us -> 51.4 us
    dot_general x6 -> x0, matrix products: 28.8 us -> none  [contract_rows(): lax.dot_general(left, right, (((0,), (0,)), ((), ())), preferred_element_...]
    pallas_call x1, Pallas kernels: 216 us -> 202 us  [gather_weights(): pl.pallas_call(functools.partial(gather_kernel, total), out_shape=[jax.Sh...]
    pallas_call x1, Pallas kernels: 192 us -> 204 us  [scatter_sums(): pl.pallas_call(functools.partial(scatter_kernel, total), out_shape=out_sh...]
    reshape x9 -> x5, local copies, waits for them, and re-layouts: 9.87 us -> 1.54 us  [the longest x2 1.1 us: all_genes(): return chunks.transpose(1, 0, 2).reshape(chunks.shape[1], -1)[:, :GENES]]
    dot_general x6 -> x5, matrix products: 21.3 us -> 14.5 us  [matmul(): return jnp.dot(left, right, preferred_element_type=jnp.float32)]
    unnamed x207 -> x131, local copies, waits for them, and re-layouts: 25.4 us -> 22.1 us
  transfers between devices with their start and end apart: 2 -> 0, of which waited for: 0 -> 0; matrix products, arithmetic and copies ran while one was open for 4% -> 0% of each run, Pallas kernels for 0% -> 0%
where the time goes in v5:
time: 572 us; the launch traced here: 562 us
  Pallas kernels  441 us (77%)
  local copies, waits for them, and re-layouts  51.4 us (9%)
  matrix products  41.6 us (7%)
  other arithmetic  21.7 us (4%)
  between operations  6.28 us (1%)
    pallas_call x1, Pallas kernels, scatter_sums(): pl.pallas_call(functools.partial(scatter_kernel, total), out_shape=out_sh...  204 us
    pallas_call x1, Pallas kernels, gather_weights(): pl.pallas_call(functools.partial(gather_kernel, total), out_shape=[jax.Sh...  202 us
    pallas_call x1, Pallas kernels, latent_step(): pl.pallas_call(functools.partial(latent_kernel, total), out_shape=[jax.Sh...  34.9 us
    unnamed x131, local copies, waits for them, and re-layouts  22.1 us
    dot_general x5, matrix products, across(): lax.dot_general(left, right, (((1,), (1,)), ((), ())), preferred_element_...  19.1 us
    dot_general x5, matrix products, matmul(): return jnp.dot(left, right, preferred_element_type=jnp.float32)  14.5 us

profile of v5, /device:TPU:0, one launch (start us, length us, event | category | flops | bytes accessed | tf_op | source)
XLA Modules:
  0.0 562.3 jit_solution(8663494858148507046)
XLA Ops:
  1.4 1.3 convert_reduce_fusion.3
  14.2 1.8 multiply_sine_fusion.1
  16.2 5.8 %copy.115 = bf16[128,13500]{1,0:T(8,128)(2,1)} copy(bf16[128,13500]{0,1:T(8,128)(2,1)} %param.23) | data formatting | bytes 6912000 | tf_op args[0]
  22.0 2.2 slice_bitcast_fusion.2
  25.4 202.2 %gather_weights.1 = (bf16[4,128,3456]{2,1,0:T(8,128)(2,1)S(1)}, bf16[8,4,32,3456]{3,2,1,0:T(8,128)(2,1)}, bf16[8,4,16,3456]{3,2,1,0:T(8,128)(2,1)S(1)}, bf16[8,2...) custom-call(bf16[4,128,3456]{2,1,0:T(8,128)(2,1)S(1)} %pad_maximum_f, ...), custom_call_target="tpu_custom_call" | custom-call | tf_op jit(solution)/shard_map/gather_weights/pallas_call | solution.py:438
  227.5 1.7 copy-done
  229.3 1.4 copy-done.1
  230.6 1.8 copy-done.4
  237.0 3.9 convolution_convert_fusion
  242.9 1.4 fusion.63
  245.4 1.8 copy.134.refs_8_
  247.2 1.7 fusion.64
  249.3 7.2 %multiply_convert_fusion = (bf16[128,4096]{1,0:T(8,128)(2,1)S(1)}, f32[128,4096]{1,0:T(8,128)}) fusion(f32[4096]{0:T(1024)S(1)} %bitcast.175, bf16[128,1024]{1,0:T(8,128)(2,1)S(1)} %add_convert_fusion.1.refs_10_, bf16[1024,4096]{1,0:T(8,128)(2,1)} %bitcast.144), kind=kOutput, calls=%fused_computation.14 | convolution fusion | flops 1078984704 | bytes 11812864 | tf_op jit(solution)/shard_map/dot_general | solution.py:40
  256.6 1.3 fusion.9.refs_9_
  261.0 34.9 %latent_step.1 = (bf16[4,128,3456]{2,1,0:T(8,128)(2,1)S(1)}, bf16[512,3456]{1,0:T(8,128)(2,1)S(1)}, f32[128,512]{1,0:T(8,128)S(1)}, f32[8,512]{1,0:T(8,128)S(1)}, f32[8,384]{1,0:T(8,128)S(1)}) custom-call(bf16[128,640]{1,0:T(8,128)(2,1)S(1)} %pad_maximum_fusion.5.refs_0_, f32[8,512]{1,0:T(8,128)S(1)} %broadcast_in_dim.31.refs_1_, f32[1,1]{1,0:T(1,128)} %bitcast.39.refs_2_, ...), custom_call_target="tpu_custom_call" | custom-call | tf_op jit(solution)/shard_map/latent_step/pallas_call | solution.py:945
  295.9 1.7 copy-done.6
  297.7 1.8 copy-done.7
  302.0 1.5 fusion.19
  303.5 1.6 fusion.24
  305.1 1.3 fusion.28
  306.4 1.6 convert_reduce_fusion.2
  308.1 7.8 %convert_reduce_fusion = (f32[4096]{0:T(1024)}, bf16[128,4096]{1,0:T(8,128)(2,1)S(1)}) fusion(f32[128,4096]{1,0:T(8,128)S(1)} %copy-done.56, bf16[128,1024]{1,0:T(8,128)(2,1)S(1)} %get-tuple-element.81.refs_16_, bf16[4096,1024]{1,0:T(8,128)(2,1)} %bitcast.137), kind=kOutput, calls=%fused_computation.13 | convolution fusion | flops 1085272064 | bytes 11812864 | tf_op jit(solution)/shard_map/dot_general | solution.py:44
  315.9 3.0 multiply_reduce_fusion.1
  323.6 1.3 fusion.36.refs_13_
  324.9 1.5 convolution_convert_fusion.2
  326.5 1.2 copy.124
  330.3 5.1 multiply_reduce_fusion.2
  338.8 204.2 %scatter_sums.1 = (bf16[4,32,3456]{2,1,0:T(8,128)(2,1)}, bf16[4,16,3456]{2,1,0:T(8,128)(2,1)}, bf16[4,128,3456]{2,1,0:T(8,128)(2,1)}, bf16[8,4,32,3456]{3,2,1,0:...) custom-call(f32[8,384]{1,0:T(8,128)} %copy-done.14, ...), custom_call_target="tpu_custom_call" | custom-call | tf_op jit(solution)/shard_map/scatter_sums/pallas_call | solution.py:816
  543.0 1.3 reduce_sum.226
  545.7 4.6 copy.135
  550.2 1.9 slice.208
  556.1 1.3 slice_convert_fusion
  (224 shorter events, 43.1 us)
Async XLA Ops:
  0.7 15.4 %copy-start.27 = (bf16[32,13500]{1,0:T(8,128)(2,1)S(1)}, bf16[32,13500]{1,0:T(8,128)(2,1)}, u32[]{:S(2)}) copy-start(bf16[32,13500]{1,0:T(8,128)(2,1)} %param.30) | copy-start | bytes 2592004
  25.3 207.1 %copy-start.41 = (f32[128,256]{1,0:T(8,128)S(1)}, f32[128,256]{1,0:T(8,128)}, u32[]{:S(2)}) copy-start(f32[128,256]{1,0:T(8,128)} %get-tuple-element.121) | copy-start | bytes 393220
  25.3 207.1 %copy-start.42 = (f32[128,256]{1,0:T(8,128)S(1)}, f32[128,256]{1,0:T(8,128)}, u32[]{:S(2)}) copy-start(f32[128,256]{1,0:T(8,128)} %get-tuple-element.122) | copy-start | bytes 393220
  25.3 207.1 %copy-start.43 = (f32[128,256]{1,0:T(8,128)S(1)}, f32[128,256]{1,0:T(8,128)}, u32[]{:S(2)}) copy-start(f32[128,256]{1,0:T(8,128)} %get-tuple-element.125) | copy-start | bytes 393220
  25.4 207.1 %copy-start.44 = (f32[128,256]{1,0:T(8,128)S(1)}, f32[128,256]{1,0:T(8,128)}, u32[]{:S(2)}) copy-start(f32[128,256]{1,0:T(8,128)} %get-tuple-element.126) | copy-start | bytes 393220
  232.6 4.3 copy-start.17
  232.8 3.7 copy-start.54
  233.2 3.9 copy-start.51
  237.0 3.9 copy-start.26
  241.2 4.3 copy-start.30
  248.9 7.6 %copy-start.15 = (f32[128,1024]{1,0:T(8,128)}, f32[128,1024]{1,0:T(8,128)S(1)}, u32[]{:S(2)}) copy-start(f32[128,1024]{1,0:T(8,128)S(1)} %get-tuple-element.134) | copy-start | bytes 1572868
  249.1 7.4 %slice-start = ((s8[8388608]{0:T(1024)(128)(4,1)}), s8[4194304]{0:T(1024)(128)(4,1)S(1)}, s32[]{:S(2)}) async-start(s8[8388608]{0:T(1024)(128)(4,1)} %bitcast.138), calls=%async_computation | async-start | bytes 8388608
  249.3 7.2 %copy-start.34 = (bf16[128,1024]{1,0:T(8,128)(2,1)}, bf16[128,1024]{1,0:T(8,128)(2,1)S(1)}, u32[]{:S(2)}) copy-start(bf16[128,1024]{1,0:T(8,128)(2,1)S(1)} %add_convert_fusion.1.refs_10_) | copy-start | bytes 786436
  249.3 7.2 %slice-start.1 = ((s8[8388608]{0:T(1024)(128)(4,1)}), s8[4194304]{0:T(1024)(128)(4,1)S(1)}, s32[]{:S(2)}) async-start(s8[8388608]{0:T(1024)(128)(4,1)} %bitcast.138), calls=%async_computation.1 | async-start | bytes 8388608
  256.6 2.4 copy-start.50
  256.6 2.7 copy-start.37
  258.5 2.5 copy-start.5
  302.0 3.1 copy-start.21
  302.0 4.4 copy-start.3
  303.5 4.5 copy-start.56
  306.4 9.5 %slice-start.2 = ((s8[8388608]{0:T(1024)(128)(4,1)}), s8[4194304]{0:T(1024)(128)(4,1)S(1)}, s32[]{:S(2)}) async-start(s8[8388608]{0:T(1024)(128)(4,1)} %bitcast.145), calls=%async_computation.2 | async-start | bytes 8388608
  308.1 7.8 %copy-start.33 = (bf16[128,1024]{1,0:T(8,128)(2,1)}, bf16[128,1024]{1,0:T(8,128)(2,1)S(1)}, u32[]{:S(2)}) copy-start(bf16[128,1024]{1,0:T(8,128)(2,1)S(1)} %get-tuple-element.81.refs_16_) | copy-start | bytes 786436
  308.1 7.8 %copy-start.16 = (f32[128,1024]{1,0:T(8,128)S(1)}, f32[128,1024]{1,0:T(8,128)}, u32[]{:S(2)}) copy-start(f32[128,1024]{1,0:T(8,128)} %copy-done.15) | copy-start | bytes 1572868
  308.1 7.8 %slice-start.3 = ((s8[8388608]{0:T(1024)(128)(4,1)}), s8[4194304]{0:T(1024)(128)(4,1)S(1)}, s32[]{:S(2)}) async-start(s8[8388608]{0:T(1024)(128)(4,1)} %bitcast.145), calls=%async_computation.3 | async-start | bytes 8388608
  315.9 3.1 copy-start.25
  324.9 3.2 copy-start.29
  330.3 6.1 %copy-start.55 = (f32[128]{0:T(128)S(1)}, f32[128]{0:T(128)}, u32[]{:S(2)}) copy-start(f32[128]{0:T(128)} %copy-done.54) | copy-start | bytes 1540
  552.1 3.8 copy-start.38
  556.0 2.1 copy-start.47
  556.0 2.7 copy-start.40
  556.0 3.5 copy-start.39
  557.4 3.0 copy-start.46
  (29 other events, 38.7 us)

commit v6 on v5

--- a/solution.py
+++ b/solution.py
@@ -449,7 +449,7 @@
             pltpu.SemaphoreType.DMA((10 + total,)),
         ],
         compiler_params=pltpu.CompilerParams(
-            collective_id=1, has_side_effects=True, vmem_limit_bytes=32 * 2**20
+            collective_id=1, has_side_effects=True, vmem_limit_bytes=20 * 2**20
         ),
         name="gather_weights",
     )(*operands)
@@ -549,7 +549,7 @@
             fetch(name, h + 2)
 
     table_start("decoder")
-    moves = [copies.send(start, starts.at[m], here.peers[m]) for m in (2, 3, 1)]
+    moves = [copies.send(start, starts.at[m], here.peers[m]) for m in (2, 1)]
     starts[0] = start[...]
     group_recon[here.quarter] = recon[...]
     recons = [copies.send(recon, group_recon.at[here.quarter], here.peers[m]) for m in (2, 3, 1)]
@@ -592,6 +592,8 @@
 
     give("up", send_up)
     give("down", send_down)
+    moves[0].wait_recv()
+    moves[0] = copies.send(starts.at[2], starts.at[3], here.peers[1])
     table_hop("decoder", 1)
     take("up")
     copies.free(halves["up"])
@@ -627,6 +629,15 @@
     flying["recon"] = copies.send(own_recon, own_recon, here.right)
     table_hop("decoder", 4)
 
+    def joint_hop(h):
+        for side, way in ((0, 1), (1, -1)):
+            flying["joint", side].wait_recv()
+            arrived = hop_joint.at[h - 1, side]
+            local = chip["joint"].at[here.owner(way * (h + 1)), side]
+            add_rows(arrived, arrived, local, jnp.bfloat16)
+            if h < last:
+                flying["joint", side] = copies.send(arrived, hop_joint.at[h, side], towards[way])
+
     for copy in moves:
         copy.wait_recv()
     moves = []
@@ -695,10 +706,13 @@
             for copy in stores_of(i):
                 copy.start()
 
+    joint_hop(1)
     stream(0, count // 3)
     table_hop("decoder", 5)
+    joint_hop(2)
     stream(count // 3, 2 * count // 3)
     table_hop("decoder", 6)
+    joint_hop(3)
     stream(2 * count // 3, count)
     for i in (count - 2, count - 1):
         for copy in stores_of(i):
@@ -721,15 +735,6 @@
         if h < last:
             arrived = all_recon.at[here.owner(h)]
             flying["recon"] = copies.send(arrived, arrived, here.right)
-
-    def joint_hop(h):
-        for side, way in ((0, 1), (1, -1)):
-            flying["joint", side].wait_recv()
-            arrived = hop_joint.at[h - 1, side]
-            local = chip["joint"].at[here.owner(way * (h + 1)), side]
-            add_rows(arrived, arrived, local, jnp.bfloat16)
-            if h < last:
-                flying["joint", side] = copies.send(arrived, hop_joint.at[h, side], towards[way])
 
     late = [
         (name, sums[name], chip[name], hops_of[name], results[name], way)
@@ -757,7 +762,8 @@
                 add_rows(result, hops.at[h - 1], local, jnp.float32)
 
     for h in range(1, last + 1):
-        joint_hop(h)
+        if h + 3 <= last:
+            joint_hop(h + 3)
         table_hop("embed", h)
         recon_hop(h)
     send_back(hop_embed, embed_out)
@@ -873,7 +879,7 @@
     here = Where(total)
     copies = Copies(*refs[21:])
     here.meet(everyone=True)
-    moves = [copies.send(message, latents.at[m], here.peers[m]) for m in (2, 3, 1)]
+    arrivals = {m: copies.send(message, latents.at[m], here.peers[m]) for m in (1, 2, 3)}
     spreads = [copies.send(spread, group_spread.at[here.quarter], here.peers[m]) for m in (2, 3, 1)]
     loads = [
         copies.local(message, latents.at[0]),
@@ -892,32 +898,49 @@
         spreads.append(copies.send(own, own, here.same(away)[1]))
     for copy in loads:
         copy.wait()
-    for copy in moves:
-        copy.wait_recv()
     rows = message.shape[0]
     size = held_decoder.shape[0]
-    for m in range(GROUP):
-        turned[:, m * rows : (m + 1) * rows] = low(wide(latents[m, :, :size]).T)
     partial[...] = jnp.zeros_like(partial)
     recon_sum[...] = jnp.zeros_like(recon_sum)
+
+    both = 2 * rows
+
+    def reconstruct(pair):
+        at = pl.ds(2 * pair, 2)
+        for m in (2 * pair, 2 * pair + 1):
+            turned[:, m * rows : (m + 1) * rows] = low(wide(latents[m, :, :size]).T)
+        values = latents[at, :, :size].reshape(both, size)
+        live = wide(latents[at, :, size : size + 128]).reshape(both, 128)
+        live = jnp.concatenate([live] * (SLICE // 128), axis=1)
+
+        @pl.loop(0, CHUNK // SLICE)
+        def _(i):
+            part = pl.ds(pl.multiple_of(i * SLICE, 128), SLICE)
+            table = held_decoder[:, part]
+            miss = matmul(values, table) - wide(held_cells[at, :, part]).reshape(both, SLICE)
+            weighted = live * miss
+            recon_sum[...] += jnp.sum((weighted * miss).reshape(both // 8, 8, SLICE), axis=0)
+            grad = low(ratio[0, 0] * weighted)
+            held_grad[at, :, part] = grad.reshape(2, rows, SLICE)
+            partial[at] += across(grad, table).reshape(2, rows, size)
+
+    arrivals[1].wait_recv()
+    reconstruct(0)
+    leaving[1] = low(partial[1])
+    returns = [copies.send(leaving.at[1], arriving.at[0], here.peers[1])]
+    for m in (2, 3):
+        arrivals[m].wait_recv()
+    reconstruct(1)
+    for m in (2, 3):
+        leaving[m] = low(partial[m])
+        returns.append(copies.send(leaving.at[m], arriving.at[m - 1], here.peers[m]))
 
     @pl.loop(0, CHUNK // SLICE)
     def _(i):
         part = pl.ds(pl.multiple_of(i * SLICE, 128), SLICE)
-        table = held_decoder[:, part]
-        for m in range(GROUP):
-            live = wide(latents[m, :, size : size + 128])
-            live = jnp.concatenate([live] * (SLICE // 128), axis=1)
-            miss = matmul(latents[m, :, :size], table) - wide(held_cells[m, :, part])
-            weighted = live * miss
-            recon_sum[...] += jnp.sum((weighted * miss).reshape(rows // 8, 8, SLICE), axis=0)
-            grad = low(ratio[0, 0] * weighted)
-            held_grad[m, :, part] = grad
-            partial[m] += across(grad, table)
-        held_term[:, part] = low(matmul(turned[...], held_grad[:, :, part].reshape(GROUP * rows, SLICE)))
-
-    leaving[...] = low(partial[...])
-    moves = [copies.send(leaving.at[m], arriving.at[m - 1], here.peers[m]) for m in (2, 3, 1)]
+        grads = held_grad[:, :, part].reshape(GROUP * rows, SLICE)
+        held_term[:, part] = low(matmul(turned[...], grads))
+
     stores = [copies.local(held_grad, recon_grad), copies.local(held_term, decoder_term)]
     for copy in spreads:
         copy.wait_recv()
@@ -925,7 +948,7 @@
     for t in range(1, total):
         summed = summed + all_spread[t]
     spread_sum[...] = summed
-    for copy in moves:
+    for copy in returns:
         copy.wait_recv()
     latent_grad[...] = (
         (partial[0] + wide(arriving[0])) + (wide(arriving[1]) + wide(arriving[2]))

time: 572 us -> 569 us (level)
  local copies, waits for them, and re-layouts: 51.4 us -> 57.9 us
  Pallas kernels: 441 us -> 435 us
    unnamed x131 -> x137, local copies, waits for them, and re-layouts: 22.1 us -> 27.9 us
where the time goes in v6:
time: 569 us; the launch traced here: 562 us
  Pallas kernels  435 us (76%)
  local copies, waits for them, and re-layouts  57.9 us (10%)
  matrix products  41.2 us (7%)
  other arithmetic  21.7 us (4%)
  between operations  6.49 us (1%)
    pallas_call x1, Pallas kernels, scatter_sums(): pl.pallas_call(functools.partial(scatter_kernel, total), out_shape=out_sh...  202 us
    pallas_call x1, Pallas kernels, gather_weights(): pl.pallas_call(functools.partial(gather_kernel, total), out_shape=[jax.Sh...  202 us
    pallas_call x1, Pallas kernels, latent_step(): pl.pallas_call(functools.partial(latent_kernel, total), out_shape=[jax.Sh...  31.4 us
    unnamed x137, local copies, waits for them, and re-layouts  27.9 us
    dot_general x5, matrix products, across(): lax.dot_general(left, right, (((1,), (1,)), ((), ())), preferred_element_...  19.1 us
    dot_general x5, matrix products, matmul(): return jnp.dot(left, right, preferred_element_type=jnp.float32)  14.1 us

profile of v6, /device:TPU:0, one launch (start us, length us, event | category | flops | bytes accessed | tf_op | source)
XLA Modules:
  0.0 562.5 jit_solution(5872280346152053630)
XLA Ops:
  14.2 1.8 multiply_sine_fusion.1
  16.2 5.9 %copy.115 = bf16[128,13500]{1,0:T(8,128)(2,1)} copy(bf16[128,13500]{0,1:T(8,128)(2,1)} %param.23) | data formatting | bytes 6912000 | tf_op args[0]
  22.1 2.2 slice_bitcast_fusion.2
  25.4 201.6 %gather_weights.1 = (bf16[4,128,3456]{2,1,0:T(8,128)(2,1)S(1)}, bf16[8,4,32,3456]{3,2,1,0:T(8,128)(2,1)S(1)}, bf16[8,4,16,3456]{3,2,1,0:T(8,128)(2,1)S(1)}, bf16...) custom-call(bf16[4,128,3456]{2,1,0:T(8,128)(2,1)S(1)} %pad_maximum_f, ...), custom_call_target="tpu_custom_call" | custom-call | tf_op jit(solution)/shard_map/gather_weights/pallas_call | solution.py:438
  227.0 2.7 copy-done
  229.7 1.7 copy-done.1
  231.5 1.3 copy-done.2
  232.8 2.9 copy-done.5
  235.7 1.8 copy-done.6
  242.1 3.9 convolution_convert_fusion
  248.0 1.4 fusion.63
  250.5 1.8 copy.134.refs_8_
  252.3 1.7 fusion.64
  254.4 6.8 %multiply_convert_fusion = (bf16[128,4096]{1,0:T(8,128)(2,1)S(1)}, f32[128,4096]{1,0:T(8,128)}) fusion(f32[4096]{0:T(1024)S(1)} %bitcast.175, bf16[128,1024]{1,0:T(8,128)(2,1)S(1)} %add_convert_fusion.1.refs_10_, bf16[1024,4096]{1,0:T(8,128)(2,1)} %bitcast.145), kind=kOutput, calls=%fused_computation.14 | convolution fusion | flops 1078984704 | bytes 11812864 | tf_op jit(solution)/shard_map/dot_general | solution.py:40
  261.3 1.3 fusion.9.refs_9_
  265.7 31.4 %latent_step.1 = (bf16[4,128,3456]{2,1,0:T(8,128)(2,1)S(1)}, bf16[512,3456]{1,0:T(8,128)(2,1)S(1)}, f32[128,512]{1,0:T(8,128)S(1)}, f32[8,512]{1,0:T(8,128)S(1)}, f32[8,384]{1,0:T(8,128)S(1)}) custom-call(bf16[128,640]{1,0:T(8,128)(2,1)S(1)} %pad_maximum_fusion.5.refs_0_, f32[8,512]{1,0:T(8,128)S(1)} %broadcast_in_dim.31.refs_1_, f32[1,1]{1,0:T(1,128)} %bitcast.39.refs_2_, ...), custom_call_target="tpu_custom_call" | custom-call | tf_op jit(solution)/shard_map/latent_step/pallas_call | solution.py:968
  297.2 1.8 copy-done.8
  298.9 1.8 copy-done.9
  303.3 1.5 fusion.19
  304.8 1.6 fusion.24
  306.4 1.3 fusion.28
  307.7 1.6 convert_reduce_fusion.2
  309.3 7.8 %convert_reduce_fusion = (f32[4096]{0:T(1024)}, bf16[128,4096]{1,0:T(8,128)(2,1)S(1)}) fusion(f32[128,4096]{1,0:T(8,128)S(1)} %copy-done.59, bf16[128,1024]{1,0:T(8,128)(2,1)S(1)} %get-tuple-element.81.refs_16_, bf16[4096,1024]{1,0:T(8,128)(2,1)} %bitcast.140), kind=kOutput, calls=%fused_computation.13 | convolution fusion | flops 1085272064 | bytes 11812864 | tf_op jit(solution)/shard_map/dot_general | solution.py:44
  317.2 3.0 multiply_reduce_fusion.1
  324.9 1.3 fusion.36.refs_13_
  326.2 1.5 convolution_convert_fusion.2
  332.3 5.1 multiply_reduce_fusion.2
  340.8 202.1 %scatter_sums.1 = (bf16[4,32,3456]{2,1,0:T(8,128)(2,1)}, bf16[4,16,3456]{2,1,0:T(8,128)(2,1)}, bf16[4,128,3456]{2,1,0:T(8,128)(2,1)}, bf16[8,4,32,3456]{3,2,1,0:...) custom-call(f32[8,384]{1,0:T(8,128)} %copy-done.16, ...), custom_call_target="tpu_custom_call" | custom-call | tf_op jit(solution)/shard_map/scatter_sums/pallas_call | solution.py:822
  542.9 1.3 reduce_sum.226
  545.5 4.6 copy.135
  550.1 1.9 slice.208
  555.9 1.3 slice_convert_fusion
  (230 shorter events, 46.3 us)
Async XLA Ops:
  0.7 15.4 %copy-start.29 = (bf16[32,13500]{1,0:T(8,128)(2,1)S(1)}, bf16[32,13500]{1,0:T(8,128)(2,1)}, u32[]{:S(2)}) copy-start(bf16[32,13500]{1,0:T(8,128)(2,1)} %param.30) | copy-start | bytes 2592004
  25.4 212.1 %copy-start.44 = (f32[128,256]{1,0:T(8,128)S(1)}, f32[128,256]{1,0:T(8,128)}, u32[]{:S(2)}) copy-start(f32[128,256]{1,0:T(8,128)} %get-tuple-element.121) | copy-start | bytes 393220
  25.4 212.1 %copy-start.45 = (f32[128,256]{1,0:T(8,128)S(1)}, f32[128,256]{1,0:T(8,128)}, u32[]{:S(2)}) copy-start(f32[128,256]{1,0:T(8,128)} %get-tuple-element.122) | copy-start | bytes 393220
  25.4 212.1 %copy-start.46 = (f32[128,256]{1,0:T(8,128)S(1)}, f32[128,256]{1,0:T(8,128)}, u32[]{:S(2)}) copy-start(f32[128,256]{1,0:T(8,128)} %get-tuple-element.125) | copy-start | bytes 393220
  25.4 212.1 %copy-start.47 = (f32[128,256]{1,0:T(8,128)S(1)}, f32[128,256]{1,0:T(8,128)}, u32[]{:S(2)}) copy-start(f32[128,256]{1,0:T(8,128)} %get-tuple-element.126) | copy-start | bytes 393220
  227.0 2.7 copy-start
  232.8 2.9 copy-start.5
  237.7 4.3 copy-start.19
  237.9 3.7 copy-start.57
  238.3 3.9 copy-start.54
  242.1 3.9 copy-start.28
  246.3 4.3 copy-start.32
  254.0 7.2 %copy-start.17 = (f32[128,1024]{1,0:T(8,128)}, f32[128,1024]{1,0:T(8,128)S(1)}, u32[]{:S(2)}) copy-start(f32[128,1024]{1,0:T(8,128)S(1)} %get-tuple-element.134) | copy-start | bytes 1572868
  254.2 7.0 %slice-start = ((s8[8388608]{0:T(1024)(128)(4,1)}), s8[4194304]{0:T(1024)(128)(4,1)S(1)}, s32[]{:S(2)}) async-start(s8[8388608]{0:T(1024)(128)(4,1)} %bitcast.141), calls=%async_computation | async-start | bytes 8388608
  254.4 6.8 %copy-start.36 = (bf16[128,1024]{1,0:T(8,128)(2,1)}, bf16[128,1024]{1,0:T(8,128)(2,1)S(1)}, u32[]{:S(2)}) copy-start(bf16[128,1024]{1,0:T(8,128)(2,1)S(1)} %add_convert_fusion.1.refs_10_) | copy-start | bytes 786436
  254.4 6.8 %slice-start.1 = ((s8[8388608]{0:T(1024)(128)(4,1)}), s8[4194304]{0:T(1024)(128)(4,1)S(1)}, s32[]{:S(2)}) async-start(s8[8388608]{0:T(1024)(128)(4,1)} %bitcast.141), calls=%async_computation.1 | async-start | bytes 8388608
  261.3 2.5 copy-start.53
  261.3 2.8 copy-start.40
  303.3 3.1 copy-start.23
  303.3 4.4 copy-start.4
  304.8 4.5 copy-start.59
  307.7 9.4 %slice-start.2 = ((s8[8388608]{0:T(1024)(128)(4,1)}), s8[4194304]{0:T(1024)(128)(4,1)S(1)}, s32[]{:S(2)}) async-start(s8[8388608]{0:T(1024)(128)(4,1)} %bitcast.146), calls=%async_computation.2 | async-start | bytes 8388608
  309.3 7.8 %copy-start.35 = (bf16[128,1024]{1,0:T(8,128)(2,1)}, bf16[128,1024]{1,0:T(8,128)(2,1)S(1)}, u32[]{:S(2)}) copy-start(bf16[128,1024]{1,0:T(8,128)(2,1)S(1)} %get-tuple-element.81.refs_16_) | copy-start | bytes 786436
  309.3 7.8 %copy-start.18 = (f32[128,1024]{1,0:T(8,128)S(1)}, f32[128,1024]{1,0:T(8,128)}, u32[]{:S(2)}) copy-start(f32[128,1024]{1,0:T(8,128)} %copy-done.17) | copy-start | bytes 1572868
  309.3 7.8 %slice-start.3 = ((s8[8388608]{0:T(1024)(128)(4,1)}), s8[4194304]{0:T(1024)(128)(4,1)S(1)}, s32[]{:S(2)}) async-start(s8[8388608]{0:T(1024)(128)(4,1)} %bitcast.146), calls=%async_computation.3 | async-start | bytes 8388608
  317.1 3.1 copy-start.27
  326.2 3.2 copy-start.31
  332.3 6.1 %copy-start.58 = (f32[128]{0:T(128)S(1)}, f32[128]{0:T(128)}, u32[]{:S(2)}) copy-start(f32[128]{0:T(128)} %copy-done.57) | copy-start | bytes 1540
  552.0 3.8 copy-start.41
  555.9 2.7 copy-start.43
  555.9 3.5 copy-start.42
  557.2 3.0 copy-start.49
  (32 other events, 44.2 us)

commit v7 on v6

--- a/solution.py
+++ b/solution.py
@@ -267,9 +267,9 @@
     (cells, embed, decoder, joint, small, output, encoder, up, down) = refs[:9]
     (cells_all, embed_all, decoder_all, joint_all, small_all) = refs[9:14]
     (output_all, encoder_all, up_all, down_all, embedded) = refs[14:19]
-    (held_cells, held_embed, partial, other_core, for_x, other_x) = refs[19:25]
+    (held_cells, held_embed, partial, other_core, for_x, other_x, raw, turned) = refs[19:27]
     here = Where(total)
-    copies = Copies(*refs[25:])
+    copies = Copies(*refs[27:])
     here.meet()
     t, x, core = here.t, here.x, here.core
     last = total - 1
@@ -287,10 +287,7 @@
     for n, (own, full, way) in enumerate(late):
         flying["late", n] = copies.send(own, full.at[t, x, core], towards[way])
     across_x = [copies.send(own, full.at[t, x, core], here.peers[2]) for own, full, _ in late]
-    own_cells = copies.local(cells.at[here.quarter], cells_all.at[0])
-    cell_moves = [
-        copies.send(cells.at[here.quarters[m]], cells_all.at[m], here.peers[m]) for m in (2, 3, 1)
-    ]
+    reads = [copies.local(cells.at[chunk], raw.at[chunk]) for chunk in range(2)]
     shares["early"] = [
         copies.send(own, full.at[t, x, core], here.peers[2])
         for own, full in ((joint, joint_all), (small, small_all))
@@ -357,6 +354,23 @@
 
     across_core = []
 
+    def send_cells():
+        for chunk in range(GROUP):
+            reads[chunk].wait()
+
+            @pl.loop(0, CHUNK // 128)
+            def _(i):
+                part = pl.ds(pl.multiple_of(i * 128, 128), 128)
+                turned[chunk, :, part] = low(wide(raw[chunk % 2, part, :]).T)
+
+            if chunk + 2 < GROUP:
+                reads.append(copies.local(cells.at[chunk + 2], raw.at[chunk % 2]))
+        own = copies.local(turned.at[here.quarter], cells_all.at[0])
+        return own, [
+            copies.send(turned.at[here.quarters[m]], cells_all.at[m], here.peers[m])
+            for m in (2, 3, 1)
+        ]
+
     def to_core(copies_of, block_of):
         for copy, (_, full, way) in zip(copies_of, late):
             copy.wait_recv()
@@ -373,6 +387,7 @@
         late_step(s)
         if s == 1:
             step("embed", 0)
+            own_cells, cell_moves = send_cells()
         step("embed", s)
         if s == last - 1:
             step("early", 0)
@@ -420,20 +435,23 @@
     tables = [embed, decoder]
     operands = [cells] + tables + own
     shapes = (
-        [cells.shape]
+        [(GROUP, cells.shape[2], cells.shape[1])]
         + [(total,) + v.shape for v in tables]
         + [(total, 2, 2) + v.shape for v in own]
     )
     remote = 15 + 12 * (total - 1) + 8 * total + 8
-    cell_rows, genes = cells.shape[1:]
+    genes, cell_rows = cells.shape[1:]
     features = total * GROUP * embed.shape[1]
+    by_cell = (GROUP, cell_rows, genes)
     buffers = [
-        cells.shape,
+        by_cell,
         (2,) + embed.shape,
         (2, 2, cell_rows, features),
         (2, cell_rows, features),
         (cell_rows, features),
         (cell_rows, features),
+        (2, genes, cell_rows),
+        by_cell,
     ]
     return pl.pallas_call(
         functools.partial(gather_kernel, total),
@@ -446,7 +464,7 @@
         + [
             pltpu.SemaphoreType.DMA((remote,)),
             pltpu.SemaphoreType.DMA((remote,)),
-            pltpu.SemaphoreType.DMA((10 + total,)),
+            pltpu.SemaphoreType.DMA((14 + total,)),
         ],
         compiler_params=pltpu.CompilerParams(
             collective_id=1, has_side_effects=True, vmem_limit_bytes=20 * 2**20
@@ -1020,6 +1038,7 @@
         block = jnp.stack(by_quarter(group_exchange(values, quarter), quarter))
         return lax.all_gather(block, "dp", axis_index_groups=groups, axis=0, tiled=False)
 
+    cells = cells.transpose(0, 2, 1)
     cells_all = jnp.stack(group_exchange(cells, quarter))
     embed_all = table(embed)
     rows, genes = cells.shape[1:]
@@ -1075,17 +1094,18 @@
     kinds = prior_mean.shape[0]
     vectors = [down_bias, first_gain, first_shift, second_gain, second_shift, encoder_bias]
     lone = jnp.full((1,), jnp.sum(live), jnp.bfloat16)
-    small = jnp.concatenate(
-        [
-            jnp.pad(v, ((0, 0), (0, 128 - v.shape[1])))
-            for v in [prior_mean, prior_logvar]
-            + [v.reshape(1, -1) for v in [up_bias] + vectors + [lone]]
-        ]
-    )
-    small = jnp.pad(small, ((0, 48 - small.shape[0]), (0, 0)))
+    row = jnp.arange(16)[:, None]
+    packs = jnp.where(row == 7, lone[None, :], jnp.zeros((16, rows), jnp.bfloat16))
+    for n, vector in enumerate(vectors):
+        packs = jnp.where(row == n + 1, vector[None, :], packs)
+    packs = jnp.pad(packs, ((0, 0), (0, 128 - rows)))
+    bias = jnp.pad(up_bias, (0, 128 - up_bias.shape[0]))
+    packs = jnp.where(row == 0, bias[None, :], packs)
+    priors = jnp.concatenate([prior_mean, prior_logvar])
+    small = jnp.concatenate([jnp.pad(priors, ((0, 0), (0, 128 - priors.shape[1]))), packs])
     gather = gather_weights if total <= NARROW else gather_plain
     cells_group, embed_cols, decoder_cols, *middle, embedded = gather(
-        gene_chunks(cells),
+        jnp.pad(cells.T, ((0, GROUP * CHUNK - GENES), (0, 0))).reshape(GROUP, CHUNK, row_count),
         gene_chunks(embed_weight),
         gene_chunks(decoder_weight),
         query_key_value,

time: 569 us -> 560 us (0.984)
  local copies, waits for them, and re-layouts: 57.9 us -> 47.6 us
    unnamed x137 -> x128, local copies, waits for them, and re-layouts: 27.9 us -> 23.8 us
where the time goes in v7:
time: 560 us; the launch traced here: 553 us
  Pallas kernels  436 us (78%)
  local copies, waits for them, and re-layouts  47.6 us (8%)
  matrix products  41.2 us (7%)
  other arithmetic  22.3 us (4%)
  between operations  6.55 us (1%)
    pallas_call x1, Pallas kernels, scatter_sums(): pl.pallas_call(functools.partial(scatter_kernel, total), out_shape=out_sh...  202 us
    pallas_call x1, Pallas kernels, gather_weights(): pl.pallas_call(functools.partial(gather_kernel, total), out_shape=[jax.Sh...  202 us
    pallas_call x1, Pallas kernels, latent_step(): pl.pallas_call(functools.partial(latent_kernel, total), out_shape=[jax.Sh...  31.4 us
    unnamed x128, local copies, waits for them, and re-layouts  23.8 us
    dot_general x5, matrix products, across(): lax.dot_general(left, right, (((1,), (1,)), ((), ())), preferred_element_...  19.1 us
    dot_general x5, matrix products, matmul(): return jnp.dot(left, right, preferred_element_type=jnp.float32)  14.1 us

profile of v7, /device:TPU:0, one launch (start us, length us, event | category | flops | bytes accessed | tf_op | source)
XLA Modules:
  0.0 553.1 jit_solution(3432730684362424112)
XLA Ops:
  1.4 1.3 convert_reduce_fusion.3
  11.7 1.8 copy-done.28
  13.5 1.6 pad.24
  15.1 201.6 %gather_weights.1 = (bf16[4,128,3456]{2,1,0:T(8,128)(2,1)S(1)}, bf16[8,4,32,3456]{3,2,1,0:T(8,128)(2,1)S(1)}, bf16[8,4,16,3456]{3,2,1,0:T(8,128)(2,1)S(1)}, bf16...) custom-call(bf16[4,3456,128]{2,1,0:T(8,128)(2,1)S(1)} %bitcast.118, ...), custom_call_target="tpu_custom_call" | custom-call | tf_op jit(solution)/shard_map/gather_weights/pallas_call | solution.py:456
  216.8 2.7 copy-done
  219.5 1.7 copy-done.1
  221.2 1.4 copy-done.2
  222.6 2.9 copy-done.5
  225.5 1.8 copy-done.6
  233.2 3.9 convolution_convert_fusion
  239.1 1.4 fusion.65
  241.6 1.8 copy.118.refs_8_
  243.4 1.7 fusion.66
  245.5 6.8 %multiply_convert_fusion = (bf16[128,4096]{1,0:T(8,128)(2,1)S(1)}, f32[128,4096]{1,0:T(8,128)}) fusion(f32[4096]{0:T(1024)S(1)} %bitcast.163, bf16[128,1024]{1,0:T(8,128)(2,1)S(1)} %add_convert_fusion.1.refs_10_, bf16[1024,4096]{1,0:T(8,128)(2,1)} %bitcast.132), kind=kOutput, calls=%fused_computation.12 | convolution fusion | flops 1078984704 | bytes 11812864 | tf_op jit(solution)/shard_map/dot_general | solution.py:40
  252.4 1.3 fusion.9.refs_9_
  256.8 31.4 %latent_step.1 = (bf16[4,128,3456]{2,1,0:T(8,128)(2,1)S(1)}, bf16[512,3456]{1,0:T(8,128)(2,1)S(1)}, f32[128,512]{1,0:T(8,128)S(1)}, f32[8,512]{1,0:T(8,128)S(1)}, f32[8,384]{1,0:T(8,128)S(1)}) custom-call(bf16[128,640]{1,0:T(8,128)(2,1)S(1)} %pad_maximum_fusion.4.refs_0_, f32[8,512]{1,0:T(8,128)S(1)} %broadcast_in_dim.192.refs_1_, f32[1,1]{1,0:T(1,128)} %bitcast.29.refs_2_, ...), custom_call_target="tpu_custom_call" | custom-call | tf_op jit(solution)/shard_map/latent_step/pallas_call | solution.py:986
  288.2 1.8 copy-done.8
  290.0 1.8 copy-done.9
  294.3 1.5 fusion.18
  295.9 1.6 fusion.23
  297.5 1.3 fusion.27
  298.8 1.6 convert_reduce_fusion.2
  300.4 7.8 %convert_reduce_fusion = (f32[4096]{0:T(1024)}, bf16[128,4096]{1,0:T(8,128)(2,1)S(1)}) fusion(f32[128,4096]{1,0:T(8,128)S(1)} %copy-done.55, bf16[128,1024]{1,0:T(8,128)(2,1)S(1)} %get-tuple-element.81.refs_16_, bf16[4096,1024]{1,0:T(8,128)(2,1)} %bitcast.127), kind=kOutput, calls=%fused_computation.11 | convolution fusion | flops 1085272064 | bytes 11812864 | tf_op jit(solution)/shard_map/dot_general | solution.py:44
  308.2 3.0 multiply_reduce_fusion.1
  315.9 1.3 fusion.35.refs_13_
  317.2 1.5 convolution_convert_fusion.2
  322.7 5.1 multiply_reduce_fusion.2
  331.1 202.4 %scatter_sums.1 = (bf16[4,32,3456]{2,1,0:T(8,128)(2,1)}, bf16[4,16,3456]{2,1,0:T(8,128)(2,1)}, bf16[4,128,3456]{2,1,0:T(8,128)(2,1)}, bf16[8,4,32,3456]{3,2,1,0:...) custom-call(f32[8,384]{1,0:T(8,128)} %copy-done.15, ...), custom_call_target="tpu_custom_call" | custom-call | tf_op jit(solution)/shard_map/scatter_sums/pallas_call | solution.py:840
  533.5 1.3 reduce_sum.226
  536.2 4.6 copy.119
  540.8 1.9 slice.186
  546.6 1.3 slice_convert_fusion
  (218 shorter events, 41.8 us)
Async XLA Ops:
  0.7 10.8 %copy-start.29 = (bf16[32,13500]{1,0:T(8,128)(2,1)S(1)}, bf16[32,13500]{1,0:T(8,128)(2,1)}, u32[]{:S(2)}) copy-start(bf16[32,13500]{1,0:T(8,128)(2,1)} %param.30) | copy-start | bytes 2592004
  11.5 2.0 copy-start.28
  216.8 2.7 copy-start
  222.6 2.9 copy-start.5
  227.4 5.7 %copy-start.18 = (f32[128,1024]{1,0:T(8,128)}, f32[128,1024]{1,0:T(8,128)S(1)}, u32[]{:S(2)}) copy-start(f32[128,1024]{1,0:T(8,128)S(1)} %get-tuple-element.91) | copy-start | bytes 1572868
  227.6 5.3 copy-start.53
  227.6 5.6 %copy-start.50 = (f32[128]{0:T(128)}, f32[128]{0:T(128)S(1)}, u32[]{:S(2)}) copy-start(f32[128]{0:T(128)S(1)} %fusion.49) | copy-start | bytes 1540
  233.2 3.9 copy-start.27
  237.4 4.3 copy-start.32
  245.1 7.2 %copy-start.16 = (f32[128,1024]{1,0:T(8,128)}, f32[128,1024]{1,0:T(8,128)S(1)}, u32[]{:S(2)}) copy-start(f32[128,1024]{1,0:T(8,128)S(1)} %get-tuple-element.130) | copy-start | bytes 1572868
  245.3 7.0 %slice-start = ((s8[8388608]{0:T(1024)(128)(4,1)}), s8[4194304]{0:T(1024)(128)(4,1)S(1)}, s32[]{:S(2)}) async-start(s8[8388608]{0:T(1024)(128)(4,1)} %bitcast.128), calls=%async_computation | async-start | bytes 8388608
  245.5 6.8 %copy-start.37 = (bf16[128,1024]{1,0:T(8,128)(2,1)}, bf16[128,1024]{1,0:T(8,128)(2,1)S(1)}, u32[]{:S(2)}) copy-start(bf16[128,1024]{1,0:T(8,128)(2,1)S(1)} %add_convert_fusion.1.refs_10_) | copy-start | bytes 786436
  245.5 6.8 %slice-start.1 = ((s8[8388608]{0:T(1024)(128)(4,1)}), s8[4194304]{0:T(1024)(128)(4,1)S(1)}, s32[]{:S(2)}) async-start(s8[8388608]{0:T(1024)(128)(4,1)} %bitcast.128), calls=%async_computation.1 | async-start | bytes 8388608
  252.3 2.0 copy-start.3
  252.4 2.4 copy-start.49
  252.4 2.7 copy-start.40
  254.3 2.5 copy-start.7
  294.3 3.1 copy-start.22
  294.3 4.4 copy-start.4
  295.9 4.5 copy-start.55
  298.7 9.4 %slice-start.2 = ((s8[8388608]{0:T(1024)(128)(4,1)}), s8[4194304]{0:T(1024)(128)(4,1)S(1)}, s32[]{:S(2)}) async-start(s8[8388608]{0:T(1024)(128)(4,1)} %bitcast.133), calls=%async_computation.2 | async-start | bytes 8388608
  300.4 7.8 %copy-start.36 = (bf16[128,1024]{1,0:T(8,128)(2,1)}, bf16[128,1024]{1,0:T(8,128)(2,1)S(1)}, u32[]{:S(2)}) copy-start(bf16[128,1024]{1,0:T(8,128)(2,1)S(1)} %get-tuple-element.81.refs_16_) | copy-start | bytes 786436
  300.4 7.8 %copy-start.17 = (f32[128,1024]{1,0:T(8,128)S(1)}, f32[128,1024]{1,0:T(8,128)}, u32[]{:S(2)}) copy-start(f32[128,1024]{1,0:T(8,128)} %copy-done.16) | copy-start | bytes 1572868
  300.4 7.8 %slice-start.3 = ((s8[8388608]{0:T(1024)(128)(4,1)}), s8[4194304]{0:T(1024)(128)(4,1)S(1)}, s32[]{:S(2)}) async-start(s8[8388608]{0:T(1024)(128)(4,1)} %bitcast.133), calls=%async_computation.3 | async-start | bytes 8388608
  308.2 3.1 copy-start.26
  317.2 3.2 copy-start.31
  322.6 6.1 %copy-start.54 = (f32[128]{0:T(128)S(1)}, f32[128]{0:T(128)}, u32[]{:S(2)}) copy-start(f32[128]{0:T(128)} %copy-done.53) | copy-start | bytes 1540
  542.7 3.8 copy-start.41
  546.6 2.1 copy-start.46
  546.6 2.7 copy-start.43
  546.6 3.5 copy-start.42
  547.9 3.0 copy-start.45
  (28 other events, 39.9 us)

commit v8 on v7

--- a/solution.py
+++ b/solution.py
@@ -687,7 +687,7 @@
             i,
             [
                 lambda part, slot: (out_term.at[slot], embed.at[:, :, :, part]),
-                lambda part, slot: (out_back.at[slot], back.at[:, :, part]),
+                lambda part, slot: (out_back.at[slot], back.at[:, part, :]),
             ],
             3,
         )
@@ -720,7 +720,8 @@
                 )
                 out_term[slot, t] = low(term).reshape(out_term.shape[2:])
             for m in range(GROUP):
-                out_back[slot, m] = low(matmul(starts[m], in_table[slot]) - wide(in_grads[slot, m]))
+                value = matmul(starts[m], in_table[slot]) - wide(in_grads[slot, m])
+                out_back[slot, m] = low(value.T)
             for copy in stores_of(i):
                 copy.start()
 
@@ -817,10 +818,10 @@
         shapes.append((block, after.shape[1]))
     operands = [recon, start, small, decoder, cells, table, grads] + lefts + rights
     decoder_share = decoder.shape[1:]
-    embed_share = (GROUP, share, CHUNK)
+    embed_share, by_gene = (GROUP, share, CHUNK), (GROUP, CHUNK, rows)
     out_shape = [
         jax.ShapeDtypeStruct(v, thin)
-        for v in (embed_share, decoder_share, cells.shape, (total,) + embed_share, cells.shape)
+        for v in (embed_share, decoder_share, by_gene, (total,) + embed_share, by_gene)
     ]
     block = small.shape[3:]
     out_shape += [jax.ShapeDtypeStruct(v, jnp.float32) for v in shapes + [block, recon.shape]]
@@ -833,7 +834,7 @@
     buffers += [(2, 2, 2) + v[1:] for v in (embed_share, decoder_share)]
     buffers += [shapes[0], (GROUP,) + start.shape, (features, GROUP * rows)]
     buffers += [(2, GROUP, rows, SLICE), (2, features, SLICE), (2, GROUP, rows, SLICE)]
-    buffers += [(2, total, GROUP, share, SLICE), (2, GROUP, rows, SLICE)]
+    buffers += [(2, total, GROUP, share, SLICE), (2, GROUP, SLICE, rows)]
     buffers += [(2 * total, 2, shapes[0][0], rows)]
     remote, here = 12 + 6 * last + 4 * last + 15 + 2 * last, 4 * last + 9
     anywhere, vmem = pl.BlockSpec(memory_space=pl.ANY), pl.BlockSpec(memory_space=pltpu.VMEM)
@@ -883,7 +884,7 @@
     terms = [low(contract_rows(before, after)) for before, after in pairs]
     small = small.reshape((device_total(),) + small.shape[3:])
     return (
-        [table_sum(embed), table_sum(decoder), sent(back)]
+        [table_sum(embed), table_sum(decoder), sent(back).transpose(0, 2, 1)]
         + [middle(term) for term in terms]
         + [lax.psum_scatter(small, AXES, scatter_dimension=0, tiled=False), sum_all(recon)]
     )
@@ -1232,7 +1233,7 @@
     def all_genes(chunks):
         return chunks.transpose(1, 0, 2).reshape(chunks.shape[1], -1)[:, :GENES]
 
-    cells_grad = all_genes(cells_grad)
+    cells_grad = cells_grad.reshape(GROUP * CHUNK, row_count)[:GENES].T
     embed_grad = wide(all_genes(embed_grad))
     decoder_grad = wide(all_genes(decoder_grad))
     (

time: 560 us -> 555 us (level)
    unnamed x128 -> x130, local copies, waits for them, and re-layouts: 23.8 us -> 23.8 us
where the time goes in v8:
time: 555 us; the launch traced here: 549 us
  Pallas kernels  435 us (78%)
  local copies, waits for them, and re-layouts  43.5 us (8%)
  matrix products  41.2 us (7%)
  other arithmetic  22.3 us (4%)
  between operations  6.56 us (1%)
    pallas_call x1, Pallas kernels, scatter_sums(): pl.pallas_call(functools.partial(scatter_kernel, total), out_shape=out_sh...  202 us
    pallas_call x1, Pallas kernels, gather_weights(): pl.pallas_call(functools.partial(gather_kernel, total), out_shape=[jax.Sh...  202 us
    pallas_call x1, Pallas kernels, latent_step(): pl.pallas_call(functools.partial(latent_kernel, total), out_shape=[jax.Sh...  31.4 us
    unnamed x130, local copies, waits for them, and re-layouts  23.8 us
    dot_general x5, matrix products, across(): lax.dot_general(left, right, (((1,), (1,)), ((), ())), preferred_element_...  19.1 us
    dot_general x5, matrix products, matmul(): return jnp.dot(left, right, preferred_element_type=jnp.float32)  14.1 us

profile of v8, /device:TPU:0, one launch (start us, length us, event | category | flops | bytes accessed | tf_op | source)
XLA Modules:
  0.0 548.8 jit_solution(10780334632414682686)
XLA Ops:
  1.4 1.3 convert_reduce_fusion.3
  11.7 1.8 copy-done.28
  13.5 1.6 pad.24
  15.1 201.6 %gather_weights.1 = (bf16[4,128,3456]{2,1,0:T(8,128)(2,1)S(1)}, bf16[8,4,32,3456]{3,2,1,0:T(8,128)(2,1)S(1)}, bf16[8,4,16,3456]{3,2,1,0:T(8,128)(2,1)S(1)}, bf16...) custom-call(bf16[4,3456,128]{2,1,0:T(8,128)(2,1)S(1)} %bitcast.119, ...), custom_call_target="tpu_custom_call" | custom-call | tf_op jit(solution)/shard_map/gather_weights/pallas_call | solution.py:456
  216.8 2.7 copy-done
  219.5 1.7 copy-done.1
  221.2 1.3 copy-done.2
  222.6 2.9 copy-done.5
  225.5 1.8 copy-done.6
  233.3 3.9 convolution_convert_fusion
  239.1 1.4 fusion.65
  241.7 1.8 copy.116.refs_8_
  243.5 1.7 fusion.66
  245.6 6.8 %multiply_convert_fusion = (bf16[128,4096]{1,0:T(8,128)(2,1)S(1)}, f32[128,4096]{1,0:T(8,128)}) fusion(f32[4096]{0:T(1024)S(1)} %bitcast.163, bf16[128,1024]{1,0:T(8,128)(2,1)S(1)} %add_convert_fusion.1.refs_10_, bf16[1024,4096]{1,0:T(8,128)(2,1)} %bitcast.132), kind=kOutput, calls=%fused_computation.13 | convolution fusion | flops 1078984704 | bytes 11812864 | tf_op jit(solution)/shard_map/dot_general | solution.py:40
  252.4 1.3 fusion.9.refs_9_
  256.8 31.4 %latent_step.1 = (bf16[4,128,3456]{2,1,0:T(8,128)(2,1)S(1)}, bf16[512,3456]{1,0:T(8,128)(2,1)S(1)}, f32[128,512]{1,0:T(8,128)S(1)}, f32[8,512]{1,0:T(8,128)S(1)}, f32[8,384]{1,0:T(8,128)S(1)}) custom-call(bf16[128,640]{1,0:T(8,128)(2,1)S(1)} %pad_maximum_fusion.4.refs_0_, f32[8,512]{1,0:T(8,128)S(1)} %broadcast_in_dim.192.refs_1_, f32[1,1]{1,0:T(1,128)} %bitcast.29.refs_2_, ...), custom_call_target="tpu_custom_call" | custom-call | tf_op jit(solution)/shard_map/latent_step/pallas_call | solution.py:987
  288.3 1.7 copy-done.8
  290.0 1.8 copy-done.9
  294.4 1.5 fusion.18
  295.9 1.6 fusion.23
  297.5 1.3 fusion.27
  298.8 1.6 convert_reduce_fusion.2
  300.4 7.8 %convert_reduce_fusion = (f32[4096]{0:T(1024)}, bf16[128,4096]{1,0:T(8,128)(2,1)S(1)}) fusion(f32[128,4096]{1,0:T(8,128)S(1)} %copy-done.56, bf16[128,1024]{1,0:T(8,128)(2,1)S(1)} %get-tuple-element.81.refs_16_, bf16[4096,1024]{1,0:T(8,128)(2,1)} %bitcast.128), kind=kOutput, calls=%fused_computation.12 | convolution fusion | flops 1085272064 | bytes 11812864 | tf_op jit(solution)/shard_map/dot_general | solution.py:44
  308.2 3.0 multiply_reduce_fusion.1
  315.9 1.3 fusion.35.refs_13_
  317.3 1.5 convolution_convert_fusion.2
  318.8 1.2 copy.106
  322.7 5.1 multiply_reduce_fusion.2
  331.1 202.2 %scatter_sums.1 = (bf16[4,32,3456]{2,1,0:T(8,128)(2,1)}, bf16[4,16,3456]{2,1,0:T(8,128)(2,1)}, bf16[4,3456,128]{2,1,0:T(8,128)(2,1)}, bf16[8,4,32,3456]{3,2,1,0:...) custom-call(f32[8,384]{1,0:T(8,128)} %copy-done.15, ...), custom_call_target="tpu_custom_call" | custom-call | tf_op jit(solution)/shard_map/scatter_sums/pallas_call | solution.py:841
  533.3 1.3 reduce_sum.226
  536.0 3.4 slice_bitcast_fusion
  542.3 1.3 slice_convert_fusion
  (219 shorter events, 39.6 us)
Async XLA Ops:
  0.7 10.8 %copy-start.29 = (bf16[32,13500]{1,0:T(8,128)(2,1)S(1)}, bf16[32,13500]{1,0:T(8,128)(2,1)}, u32[]{:S(2)}) copy-start(bf16[32,13500]{1,0:T(8,128)(2,1)} %param.30) | copy-start | bytes 2592004
  216.8 2.7 copy-start
  222.6 2.9 copy-start.5
  227.4 5.7 %copy-start.18 = (f32[128,1024]{1,0:T(8,128)}, f32[128,1024]{1,0:T(8,128)S(1)}, u32[]{:S(2)}) copy-start(f32[128,1024]{1,0:T(8,128)S(1)} %get-tuple-element.91) | copy-start | bytes 1572868
  227.6 5.3 copy-start.54
  227.6 5.6 %copy-start.51 = (f32[128]{0:T(128)}, f32[128]{0:T(128)S(1)}, u32[]{:S(2)}) copy-start(f32[128]{0:T(128)S(1)} %fusion.49) | copy-start | bytes 1540
  233.2 3.9 copy-start.27
  237.4 4.3 copy-start.32
  245.1 7.2 %copy-start.16 = (f32[128,1024]{1,0:T(8,128)}, f32[128,1024]{1,0:T(8,128)S(1)}, u32[]{:S(2)}) copy-start(f32[128,1024]{1,0:T(8,128)S(1)} %get-tuple-element.130) | copy-start | bytes 1572868
  245.4 7.0 %slice-start = ((s8[8388608]{0:T(1024)(128)(4,1)}), s8[4194304]{0:T(1024)(128)(4,1)S(1)}, s32[]{:S(2)}) async-start(s8[8388608]{0:T(1024)(128)(4,1)} %bitcast.129), calls=%async_computation | async-start | bytes 8388608
  245.5 6.8 %copy-start.37 = (bf16[128,1024]{1,0:T(8,128)(2,1)}, bf16[128,1024]{1,0:T(8,128)(2,1)S(1)}, u32[]{:S(2)}) copy-start(bf16[128,1024]{1,0:T(8,128)(2,1)S(1)} %add_convert_fusion.1.refs_10_) | copy-start | bytes 786436
  245.5 6.8 %slice-start.1 = ((s8[8388608]{0:T(1024)(128)(4,1)}), s8[4194304]{0:T(1024)(128)(4,1)S(1)}, s32[]{:S(2)}) async-start(s8[8388608]{0:T(1024)(128)(4,1)} %bitcast.129), calls=%async_computation.1 | async-start | bytes 8388608
  252.4 2.4 copy-start.50
  252.4 2.7 copy-start.40
  254.3 2.5 copy-start.7
  294.3 3.1 copy-start.22
  294.3 4.4 copy-start.4
  295.9 4.5 copy-start.56
  298.8 9.5 %slice-start.2 = ((s8[8388608]{0:T(1024)(128)(4,1)}), s8[4194304]{0:T(1024)(128)(4,1)S(1)}, s32[]{:S(2)}) async-start(s8[8388608]{0:T(1024)(128)(4,1)} %bitcast.133), calls=%async_computation.2 | async-start | bytes 8388608
  300.4 7.8 %copy-start.36 = (bf16[128,1024]{1,0:T(8,128)(2,1)}, bf16[128,1024]{1,0:T(8,128)(2,1)S(1)}, u32[]{:S(2)}) copy-start(bf16[128,1024]{1,0:T(8,128)(2,1)S(1)} %get-tuple-element.81.refs_16_) | copy-start | bytes 786436
  300.4 7.8 %copy-start.17 = (f32[128,1024]{1,0:T(8,128)S(1)}, f32[128,1024]{1,0:T(8,128)}, u32[]{:S(2)}) copy-start(f32[128,1024]{1,0:T(8,128)} %copy-done.16) | copy-start | bytes 1572868
  300.4 7.8 %slice-start.3 = ((s8[8388608]{0:T(1024)(128)(4,1)}), s8[4194304]{0:T(1024)(128)(4,1)S(1)}, s32[]{:S(2)}) async-start(s8[8388608]{0:T(1024)(128)(4,1)} %bitcast.133), calls=%async_computation.3 | async-start | bytes 8388608
  308.2 3.1 copy-start.26
  317.3 3.2 copy-start.31
  322.7 6.1 %copy-start.55 = (f32[128]{0:T(128)S(1)}, f32[128]{0:T(128)}, u32[]{:S(2)}) copy-start(f32[128]{0:T(128)} %copy-done.54) | copy-start | bytes 1540
  536.0 3.4 copy-start.49
  536.0 5.2 copy-start.44
  539.4 2.8 copy-start.41
  542.3 2.1 copy-start.47
  542.3 2.7 copy-start.43
  542.3 3.5 copy-start.42
  543.6 3.0 copy-start.46
  (29 other events, 42.0 us)
